TPU v7x, 32 devices: a whole 2x2x4 slice. The times are simulated.
32 devices in a mesh: pts: 8 (over z, y), tile: 4 (over x, core).
Axes of the slice: x: 2, y: 2, z: 4, core: 2. Of those that a mesh axis runs over, the one named last changes fastest.
Arguments:
- values: float32 [32, 64, 1024], P(('pts', 'tile')), may hold values from -6 to 6
- cycle_taps: float32 [32, 64, 8, 1024], P(('pts', 'tile')), may hold values from 0 to 1
- phi_taps: float32 [32, 64, 8, 1024], P(('pts', 'tile')), may hold values from 0 to 1
- cycle_start: int32 [32, 64, 1024], P(('pts', 'tile')), may hold values from 0 to 24
- phi_start: int32 [32, 64, 1024], P(('pts', 'tile')), may hold values from 0 to 1016
- tile_list: int32 [32, 8, 8], replicated, may hold values from 0 to 255, as said below
- response: float32 [4097], replicated, may hold values from 0.05 to 1
Outputs:
- filtered_grid: float32 [256, 32, 8192], P(None, 'tile', 'pts')
- gradient: float32 [32, 64, 1024], P(('pts', 'tile'))
Inputs may be any that keep to these rules, and one draw needn't show every extreme that they name: For each point block b and phi column q the 8 entries tile_list[b, q, :] are distinct cycle blocks; slot q * 8 + k of block b holds exactly 1024 points, all of whose taps lie in the tile of cycle block tile_list[b, q, k] and phi column q.
All inputs are finite; a program needn't handle non-finite values.
Results may differ from a plain program's by a relative error of at most 0.0003.
Values sent between devices are 32-bit elements; how exact they have to be, the bound alone decides.
No kernel may reach another device: no remote copies, remote signals or barrier semaphores. Data moves between devices by JAX's collectives and lax.ppermute only.
A program may use at most 128 MiB of HBM per device.

v0:
```python
import math

import jax
import jax.numpy as jnp
from jax import lax
from jax.sharding import PartitionSpec as P

NPHI = 8192
TR = 32
NJ = 256
SLOTS_DEV = 64
PPS = 1024


precise = lax.Precision.HIGHEST
radix_first = 64


def contract(formula, lhs_array, rhs_array):
    return jnp.einsum(formula, lhs_array, rhs_array, precision=precise)


def spread_matrix(weights, starts, extent):
    offsets = lax.broadcasted_iota(jnp.int32, (1, 1, extent), 2) - starts[:, :, None]
    result = jnp.zeros(starts.shape + (extent,), jnp.float32)
    for tap_index in range(weights.shape[1]):
        result = result + jnp.where(offsets == tap_index, weights[:, tap_index, :, None], 0.0)
    return result


def angle_table(rows_count, cols_count, modulus):
    left_index = lax.broadcasted_iota(jnp.int32, (rows_count, cols_count), 0)
    right_index = lax.broadcasted_iota(jnp.int32, (rows_count, cols_count), 1)
    phase_int = left_index * right_index % modulus
    angles = phase_int.astype(jnp.float32) * (2.0 * math.pi / modulus)
    return (jnp.cos(angles), jnp.sin(angles))


def filter_cycles(cycle_rows, response):
    length = cycle_rows.shape[-1]
    second = length // radix_first
    cos_first, sin_first = angle_table(radix_first, radix_first, radix_first)
    cos_twist, sin_twist = angle_table(radix_first, second, length)
    cos_second, sin_second = angle_table(second, second, second)
    blocks = cycle_rows.reshape(cycle_rows.shape[:2] + (radix_first, second))
    real_one = contract("giab,ak->gikb", blocks, cos_first)
    imag_one = -contract("giab,ak->gikb", blocks, sin_first)
    real_two = real_one * cos_twist + imag_one * sin_twist
    imag_two = imag_one * cos_twist - real_one * sin_twist
    real_freq = contract("gikb,bm->gikm", real_two, cos_second) + contract(
        "gikb,bm->gikm", imag_two, sin_second
    )
    imag_freq = contract("gikb,bm->gikm", imag_two, cos_second) - contract(
        "gikb,bm->gikm", real_two, sin_second
    )
    full_response = jnp.concatenate([response, response[-2:0:-1]])
    gain_table = full_response.reshape(second, radix_first).T
    real_freq = real_freq * gain_table
    imag_freq = imag_freq * gain_table
    real_back = contract("gikm,bm->gikb", real_freq, cos_second) - contract(
        "gikm,bm->gikb", imag_freq, sin_second
    )
    imag_back = contract("gikm,bm->gikb", imag_freq, cos_second) + contract(
        "gikm,bm->gikb", real_freq, sin_second
    )
    real_turn = real_back * cos_twist - imag_back * sin_twist
    imag_turn = imag_back * cos_twist + real_back * sin_twist
    spatial = contract("gikb,ka->giab", real_turn, cos_first) - contract(
        "gikb,ka->giab", imag_turn, sin_first
    )
    return (spatial / length).reshape(cycle_rows.shape)


def accumulate(arrived, wanted, cycle_blocks):
    selector = (
        lax.broadcasted_iota(jnp.int32, (cycle_blocks, wanted.size), 0) == wanted.reshape(1, -1)
    ).astype(jnp.float32)
    flattened = arrived.reshape(wanted.size, -1)
    return jnp.dot(selector, flattened, precision=precise).reshape(
        (cycle_blocks,) + arrived.shape[2:]
    )


def per_device(values, cycle_taps, phi_taps, cycle_start, phi_start, tile_list, response):
    columns = lax.axis_size("pts")
    part_count = lax.axis_size("tile")
    column = lax.axis_index("pts")
    per_column = SLOTS_DEV // columns
    tile_width = NPHI // columns
    cycle_part = TR // part_count
    cycle_weights = spread_matrix(cycle_taps[0], cycle_start[0], TR)
    phi_weights = spread_matrix(phi_taps[0], phi_start[0], tile_width)
    loaded = cycle_weights * values[0][:, :, None]
    cycle_split = cycle_weights.reshape(columns, per_column, PPS, part_count, cycle_part)
    loaded_split = loaded.reshape(columns, per_column, PPS, part_count, cycle_part)
    phi_split = phi_weights.reshape(columns, per_column, PPS, tile_width)
    partial_value = contract("qkitr,qkic->qtkrc", loaded_split, phi_split)
    partial_value = partial_value.reshape(columns * part_count, per_column, cycle_part, tile_width)
    arrived = lax.all_to_all(
        partial_value, ("pts", "tile"), split_axis=0, concat_axis=0, tiled=True
    )
    wanted = lax.dynamic_index_in_dim(tile_list, column, 1, keepdims=False)
    owned_tiles = accumulate(arrived, wanted, NJ)
    whole_cycles = filter_cycles(
        lax.all_to_all(owned_tiles, "pts", split_axis=0, concat_axis=2, tiled=True), response
    )
    filtered = lax.all_to_all(whole_cycles, "pts", split_axis=2, concat_axis=0, tiled=True)
    picked = jnp.take(filtered, wanted.reshape(-1), axis=0)
    picked = picked.reshape(columns * part_count, per_column, cycle_part, tile_width)
    returned = lax.all_to_all(picked, ("pts", "tile"), split_axis=0, concat_axis=0, tiled=True)
    returned = returned.reshape(columns, part_count, per_column, cycle_part, tile_width)
    rows_read = contract("qkitr,qtkrc->qkic", cycle_split, returned)
    gradient = jnp.sum(rows_read * phi_split, axis=-1).reshape(SLOTS_DEV, PPS)
    return (filtered, gradient[None])


def solution(mesh):
    return jax.shard_map(
        per_device,
        mesh=mesh,
        in_specs=(
            P(("pts", "tile"), None, None),
            P(("pts", "tile"), None, None, None),
            P(("pts", "tile"), None, None, None),
            P(("pts", "tile"), None, None),
            P(("pts", "tile"), None, None),
            P(),
            P(),
        ),
        out_specs=(P(None, "tile", "pts"), P(("pts", "tile"), None, None)),
        check_vma=False,
    )
```

profile of v0, /device:TPU:0, one launch (start us, length us, event | category | flops | bytes accessed | tf_op | source)
XLA Modules:
  0.0 2058.5 jit_solution(15028189321480131888)
XLA Ops:
  27.5 467.0 %fusion.42 = f32[8,4,8,8,1024]{4,3,1,2,0:T(8,128)S(1)} fusion(f32[8,8,1024]{2,1,0:T(8,128)S(1)} %get-tuple-element.28, f32[8,8,1024]{2,1,0:T(8,128)S(1)} %get-tuple-element.29, f32[8,8,1024]{2,1,0:T(8,128)S(1)} %get-tuple-element.30, f32[8,8,1024]{2,1,0:T(8,128)S(1)} %get-tuple-element.31, f32[8,8,1024]{2,1,0:T(8,128)S(1)} %get-tuple-element.32, ...), kind=kOutput, calls=%fused_computation.58 | convolution fusion | flops 27380416512 | bytes 19136512
  507.6 184.6 %all-to-all-done = f32[32,8,8,1024]{3,2,1,0:T(8,128)} async-done(((f32[32,8,8,1024]{3,2,1,0:T(8,128)}), f32[32,8,8,1024]{3,2,1,0:T(8,128)}, u32[]{:S(2)}, u32[]{:S(2)}) %all-to-all-start) | async-done | bytes 8388640 | tf_op jit(solution)/shard_map/all_to_all | solution.py:99
  692.2 15.2 copy.75
  716.5 19.2 fusion.48
  749.8 182.5 %all-to-all-done.1 = f32[256,8,1024]{2,1,0:T(8,128)} async-done(((f32[256,8,1024]{2,1,0:T(8,128)}), f32[256,8,1024]{2,1,0:T(8,128)}, u32[]{:S(2)}, u32[]{:S(2)}) %all-to-all-start.1) | async-done | bytes 8388640 | tf_op jit(solution)/shard_map/all_to_all | solution.py:105
  932.3 15.2 copy.96
  956.8 11.5 fusion.76
  976.8 10.2 fusion.12
  987.0 11.8 add_multiply_fusion
  998.8 11.7 fusion.54
  1010.5 9.5 fusion.63
  1020.0 9.7 fusion.10
  1029.8 11.8 subtract_multiply_fusion
  1041.6 13.0 fusion.56
  1063.9 15.8 fusion.20
  1079.7 20.8 %multiply_bitcast_fusion = f32[32,8,64,128]{3,2,1,0:T(8,128)} fusion(f32[64,32,8,128]{3,0,2,1:T(8,128)} %fusion.20, f32[64,128]{1,0:T(8,128)S(1)} %get-tuple-element.36, f32[64,128]{1,0:T(8,128)S(1)} %get-tuple-element.37, f32[32,8,64,128]{3,2,1,0:T(8,128)} %fusion.60, f32[32,8,64,128]{3,2,1,0:T(8,128)} %fusion.54, f32[32,8,64,128]{3,2,1,0:T(8,128)} %fusion.63, ...), kind=kOutput, calls=%fused_computation.33 | convolution fusion | flops 1625350144 | bytes 50397184 | tf_op jit(solution)/shard_map/gikb,ka->giab/dot_general | solution.py:20
  1100.5 16.3 copy.58
  1116.7 20.5 reshape.200
  1142.6 182.1 %all-to-all-done.2 = f32[8,1,262144]{2,1,0:T(1,128)} async-done(((f32[8,1,262144]{2,1,0:T(1,128)}), f32[8,1,262144]{2,1,0:T(1,128)}, u32[]{:S(2)}, u32[]{:S(2)}) %all-to-all-start.2) | async-done | bytes 8388640 | tf_op jit(solution)/shard_map/all_to_all | solution.py:107
  1325.2 26.6 %reduce = f32[8,262144]{1,0:T(8,128)} reduce(f32[8,1,262144]{2,1,0:T(1,128)} %all-to-all-done.2, f32[]{:T(128)} %broadcast.235), dimensions={1}, to_apply=%all_to_all.34.reduce_sub_computation | reduce | bytes 16777220 | tf_op jit(solution)/shard_map/all_to_all | solution.py:107
  1351.8 25.3 %reshape.201 = f32[8192,8,32]{2,1,0:T(8,128)} reshape(f32[8,262144]{1,0:T(8,128)} %reduce) | data formatting | bytes 16777216
  1377.1 22.7 %copy.48 = f32[8,32,8,1024]{3,2,1,0:T(8,128)} copy(f32[8,32,8,1024]{1,2,3,0:T(8,128)} %bitcast.157) | data formatting | bytes 16777216 | tf_op jit(solution)/shard_map/all_to_all | solution.py:107
  1426.1 177.4 %all-to-all-done.3 = f32[32,8,8,1024]{3,2,1,0:T(8,128)} async-done(((f32[32,8,8,1024]{3,2,1,0:T(8,128)}), f32[32,8,8,1024]{3,2,1,0:T(8,128)}, u32[]{:S(2)}, u32[]{:S(2)}) %all-to-all-start.3) | async-done | bytes 8388640 | tf_op jit(solution)/shard_map/all_to_all | solution.py:110
  1603.5 454.6 %fusion = f32[8,8,1024]{2,1,0:T(8,128)} fusion(f32[8,8,1024]{2,1,0:T(8,128)} %copy-done.32, f32[8,8,1024]{2,1,0:T(8,128)} %copy-done.33, f32[8,8,1024]{2,1,0:T(8,128)} %copy-done.30, f32[8,8,1024]{2,1,0:T(8,128)} %copy-done.31, f32[8,8,1024]{2,1,0:T(8,128)S(1)} %copy-done.27, f32[8,8,1024]{2,1,0:T(8,128)S(1)} %copy-done.29, ...), kind=kOutput, calls=%fused_computation.2 | convolution fusion | flops 27514568704 | bytes 19398656 | tf_op jit(solution)/shard_map/qkitr,qtkrc->qkic/dot_general | solution.py:20
  (127 shorter events, 121.9 us)
Async XLA Ops:
  0.6 19.0 copy-start.37
  0.7 19.0 copy-start.19
  0.7 19.0 copy-start.21
  19.2 475.2 %copy-start.22 = (f32[8,8,1024]{2,1,0:T(8,128)}, f32[8,8,1024]{2,1,0:T(8,128)S(1)}, u32[]{:S(2)}) copy-start(f32[8,8,1024]{2,1,0:T(8,128)S(1)} %get-tuple-element.34) | copy-start | bytes 786436
  19.2 475.2 %copy-start.24 = (f32[8,8,1024]{2,1,0:T(8,128)}, f32[8,8,1024]{2,1,0:T(8,128)S(1)}, u32[]{:S(2)}) copy-start(f32[8,8,1024]{2,1,0:T(8,128)S(1)} %get-tuple-element.35) | copy-start | bytes 786436
  19.3 475.1 %copy-start.26 = (f32[8,8,1024]{2,1,0:T(8,128)}, f32[8,8,1024]{2,1,0:T(8,128)S(1)}, u32[]{:S(2)}) copy-start(f32[8,8,1024]{2,1,0:T(8,128)S(1)} %get-tuple-element.32) | copy-start | bytes 786436
  19.3 475.1 %copy-start.28 = (f32[8,8,1024]{2,1,0:T(8,128)}, f32[8,8,1024]{2,1,0:T(8,128)S(1)}, u32[]{:S(2)}) copy-start(f32[8,8,1024]{2,1,0:T(8,128)S(1)} %get-tuple-element.33) | copy-start | bytes 786436
  19.4 475.0 %copy-start.30 = (f32[8,8,1024]{2,1,0:T(8,128)}, f32[8,8,1024]{2,1,0:T(8,128)S(1)}, u32[]{:S(2)}) copy-start(f32[8,8,1024]{2,1,0:T(8,128)S(1)} %get-tuple-element.30) | copy-start | bytes 786436
  19.5 475.0 %copy-start.31 = (f32[8,8,1024]{2,1,0:T(8,128)}, f32[8,8,1024]{2,1,0:T(8,128)S(1)}, u32[]{:S(2)}) copy-start(f32[8,8,1024]{2,1,0:T(8,128)S(1)} %get-tuple-element.31) | copy-start | bytes 786436
  19.6 474.9 %copy-start.32 = (f32[8,8,1024]{2,1,0:T(8,128)}, f32[8,8,1024]{2,1,0:T(8,128)S(1)}, u32[]{:S(2)}) copy-start(f32[8,8,1024]{2,1,0:T(8,128)S(1)} %get-tuple-element.28) | copy-start | bytes 786436
  19.6 474.9 %copy-start.33 = (f32[8,8,1024]{2,1,0:T(8,128)}, f32[8,8,1024]{2,1,0:T(8,128)S(1)}, u32[]{:S(2)}) copy-start(f32[8,8,1024]{2,1,0:T(8,128)S(1)} %get-tuple-element.29) | copy-start | bytes 786436
  498.8 193.5 %all-to-all-start = ((f32[32,8,8,1024]{3,2,1,0:T(8,128)}), f32[32,8,8,1024]{3,2,1,0:T(8,128)}, u32[]{:S(2)}, u32[]{:S(2)}) async-start(f32[32,8,8,1024]{3,2,1,0:T(8,128)} %bitcast.163), calls=%async_computation | async-start | bytes 16777216 | tf_op jit(solution)/shard_map/all_to_all | solution.py:99
  507.5 199.9 %copy-start.34 = (s32[32,1,8]{2,0,1:T(8,128)}, s32[32,1,8]{2,0,1:T(8,128)S(1)}, u32[]{:S(2)}) copy-start(s32[32,1,8]{2,0,1:T(8,128)S(1)} %copy.40) | copy-start | bytes 3076
  744.0 188.3 %all-to-all-start.1 = ((f32[256,8,1024]{2,1,0:T(8,128)}), f32[256,8,1024]{2,1,0:T(8,128)}, u32[]{:S(2)}, u32[]{:S(2)}) async-start(f32[256,8,1024]{2,1,0:T(8,128)} %copy.44), calls=%async_computation.1 | async-start | bytes 16777216 | tf_op jit(solution)/shard_map/all_to_all | solution.py:105
  956.8 11.5 copy-start.2
  998.8 11.7 copy-start.1
  1041.5 13.0 copy-start
  1041.5 22.3 %slice-start = ((s8[8388608]{0:T(1024)(128)(4,1)}), s8[4194304]{0:T(1024)(128)(4,1)S(1)}, s32[]{:S(2)}) async-start(s8[8388608]{0:T(1024)(128)(4,1)} %bitcast.158), calls=%async_computation.4 | async-start | bytes 8388608
  1137.2 187.4 %all-to-all-start.2 = ((f32[8,1,262144]{2,1,0:T(1,128)}), f32[8,1,262144]{2,1,0:T(1,128)}, u32[]{:S(2)}, u32[]{:S(2)}) async-start(f32[8,1,262144]{2,1,0:T(1,128)} %reshape.200), calls=%async_computation.2 | async-start | bytes 16777216 | tf_op jit(solution)/shard_map/all_to_all | solution.py:107
  1413.5 190.0 %all-to-all-start.3 = ((f32[32,8,8,1024]{3,2,1,0:T(8,128)}), f32[32,8,8,1024]{3,2,1,0:T(8,128)}, u32[]{:S(2)}, u32[]{:S(2)}) async-start(f32[32,8,8,1024]{3,2,1,0:T(8,128)} %broadcast_select_fusion), calls=%async_computation.3 | async-start | bytes 16777216 | tf_op jit(solution)/shard_map/all_to_all | solution.py:110
  1417.4 186.1 %copy-start.23 = (f32[8,8,1024]{2,1,0:T(8,128)S(1)}, f32[8,8,1024]{2,1,0:T(8,128)}, u32[]{:S(2)}) copy-start(f32[8,8,1024]{2,1,0:T(8,128)} %copy-done.22) | copy-start | bytes 786436
  1417.4 186.0 %copy-start.25 = (f32[8,8,1024]{2,1,0:T(8,128)S(1)}, f32[8,8,1024]{2,1,0:T(8,128)}, u32[]{:S(2)}) copy-start(f32[8,8,1024]{2,1,0:T(8,128)} %copy-done.24) | copy-start | bytes 786436
  1417.4 186.0 %copy-start.27 = (f32[8,8,1024]{2,1,0:T(8,128)S(1)}, f32[8,8,1024]{2,1,0:T(8,128)}, u32[]{:S(2)}) copy-start(f32[8,8,1024]{2,1,0:T(8,128)} %copy-done.26) | copy-start | bytes 786436
  1417.5 186.0 %copy-start.29 = (f32[8,8,1024]{2,1,0:T(8,128)S(1)}, f32[8,8,1024]{2,1,0:T(8,128)}, u32[]{:S(2)}) copy-start(f32[8,8,1024]{2,1,0:T(8,128)} %copy-done.28) | copy-start | bytes 786436
  (23 other events, 141.1 us)
where the time goes:
time: 2070 us; the launch traced here: 2060 us
  matrix products  1080 us (52%)
  waiting for transfers between devices  727 us (35%)
  local copies, waits for them, and re-layouts  174 us (8%)
  other arithmetic  50.4 us (2%)
  starting transfers between devices  21.5 us (1%)
    dot_general x13, matrix products, contract(): return jnp.einsum(formula, lhs_array, rhs_array, precision=precise)  598 us
    unnamed x1, matrix products  467 us
    all_to_all x1, waiting for transfers between devices, per_device(): lax.all_to_all(partial_value, ('pts', 'tile'), split_axis=0, concat_axis=...  185 us
    all_to_all x1, waiting for transfers between devices, per_device(): lax.all_to_all(owned_tiles, 'pts', split_axis=0, concat_axis=2, tiled=True)  182 us
    all_to_all x1, waiting for transfers between devices, per_device(): lax.all_to_all(whole_cycles, 'pts', split_axis=2, concat_axis=0, tiled=True)  182 us
    all_to_all x1, waiting for transfers between devices, per_device(): lax.all_to_all(picked, ('pts', 'tile'), split_axis=0, concat_axis=0, tile...  177 us
    unnamed x99, local copies, waits for them, and re-layouts  62.1 us
  transfers between devices with their start and end apart: 4, of which 4 were waited for; matrix products, arithmetic and copies ran while one was open for 1% of the time, Pallas kernels for 0%

commit v1 on v0

--- a/solution.py
+++ b/solution.py
@@ -1,19 +1,383 @@
+import functools
 import math
 
 import jax
 import jax.numpy as jnp
+import numpy as np
 from jax import lax
+from jax.experimental import pallas as pl
+from jax.experimental.pallas import tpu as pltpu
 from jax.sharding import PartitionSpec as P
 
 NPHI = 8192
 TR = 32
-NJ = 256
-SLOTS_DEV = 64
-PPS = 1024
+TAPS = 8
+LANES = 128
+GROUPS = 8
+RADIX = 64
+STEP_SLOTS = 8
+VMEM_LIMIT = 50 * 1024 * 1024
+
+f32 = jnp.float32
+bf16 = jnp.bfloat16
+
+
+def split(x):
+    high = x.astype(bf16)
+    low = (x - high.astype(f32)).astype(bf16)
+    return high, low
+
+
+def split_f32(x):
+    high = x.astype(bf16).astype(f32)
+    return high, x - high
+
+
+def shifted_window(taps, shift):
+    n = taps.shape[1]
+    window = jnp.concatenate([taps, jnp.zeros((8, n), f32)], axis=0)
+    both = jnp.concatenate([shift, shift], axis=0)
+    for bit in (1, 2, 4):
+        moved = pltpu.roll(window, bit, 0)
+        window = jnp.where((both & bit) != 0, moved, window)
+    return window[:8], window[8:]
+
+
+def cycle_factor(taps, starts):
+    cycle_start, phi_start = starts
+    first, second = shifted_window(taps, cycle_start & 7)
+    block = cycle_start >> 3
+    rows = []
+    for h in range(TR // 8):
+        rows.append(jnp.where(block == h, first, jnp.where(block == h - 1, second, 0.0)))
+    rows = jnp.concatenate(rows, axis=0)
+    n = rows.shape[1]
+    mine = lax.broadcasted_iota(jnp.int32, (GROUPS, n), 0) == (phi_start >> 7)
+    parts = []
+    for part in split_f32(rows):
+        spread = jnp.where(mine[None], part[:, None, :], 0.0)
+        parts.append(spread.reshape(TR * GROUPS, n).astype(bf16))
+    return parts
+
+
+def spread_kernel(values, cycle_taps, phi_taps, cycle_start, phi_start, out):
+    n = values.shape[1]
+
+    def one(k, carry):
+        cycle_at = jnp.broadcast_to(cycle_start[pl.ds(k, 1), :], (8, n))
+        phi_at = jnp.broadcast_to(phi_start[pl.ds(k, 1), :], (8, n))
+        loaded = cycle_taps[k] * values[pl.ds(k, 1), :]
+        left_high, left_low = cycle_factor(loaded, (cycle_at, phi_at))
+        lane = phi_at & 127
+        first, second = shifted_window(phi_taps[k], lane & 7)
+        block = lane >> 3
+        pieces = []
+        for h in range(17):
+            pieces.append(jnp.where(block == h, first, jnp.where(block == h - 1, second, 0.0)))
+        pieces.append(jnp.zeros((256 - 17 * 8, n), f32))
+        right_high, right_low = split(jnp.concatenate(pieces, axis=0))
+        dims = (((1,), (1,)), ((), ()))
+        product = lax.dot_general(left_high, right_high, dims, preferred_element_type=f32)
+        product += lax.dot_general(left_high, right_low, dims, preferred_element_type=f32)
+        product += lax.dot_general(left_low, right_high, dims, preferred_element_type=f32)
+        tile = product[:, :128] + pltpu.roll(product[:, 128:], 1, 0)
+        parts = out.shape[1]
+        for r in range(TR):
+            out[r % GROUPS, r // GROUPS, k] = tile[r * 8 : r * 8 + 8]
+        return carry
+
+    lax.fori_loop(0, STEP_SLOTS, one, 0)
+
+
+def spread_tiles(values, cycle_taps, phi_taps, cycle_start, phi_start, part_count):
+    slots, n = values.shape
+    flat = pl.BlockSpec((STEP_SLOTS, n), lambda i: (i, 0))
+    taps = pl.BlockSpec((STEP_SLOTS, TAPS, n), lambda i: (i, 0, 0))
+    rows = TR // part_count
+    return pl.pallas_call(
+        spread_kernel,
+        grid=(slots // STEP_SLOTS,),
+        in_specs=[flat, taps, taps, flat, flat],
+        out_specs=pl.BlockSpec((rows, part_count, STEP_SLOTS, 8, LANES), lambda i: (0, 0, i, 0, 0)),
+        out_shape=jax.ShapeDtypeStruct((rows, part_count, slots, 8, LANES), f32),
+        compiler_params=pltpu.CompilerParams(vmem_limit_bytes=VMEM_LIMIT),
+        cost_estimate=pl.CostEstimate(
+            flops=slots * 2 * 3 * 256 * 256 * n, bytes_accessed=slots * (19 + 32) * n * 4, transcendentals=0
+        ),
+        name="spread",
+    )(values, cycle_taps, phi_taps, cycle_start, phi_start)
+
+
+def read_kernel(cycle_taps, phi_taps, cycle_start, phi_start, tiles, out):
+    n = cycle_start.shape[1]
+
+    def one(k, carry):
+        cycle_at = jnp.broadcast_to(cycle_start[pl.ds(k, 1), :], (8, n))
+        phi_at = jnp.broadcast_to(phi_start[pl.ds(k, 1), :], (8, n))
+        right_high, right_low = cycle_factor(cycle_taps[k], (cycle_at, phi_at))
+        tile = jnp.concatenate([tiles[r % GROUPS, r // GROUPS, k] for r in range(TR)], axis=0)
+        following = pltpu.roll(tile, TR * GROUPS - 1, 0)
+        wide = jnp.concatenate([tile.T, following[:, :128].T[:16]], axis=0)
+        left_high, left_low = split(wide)
+        dims = (((1,), (0,)), ((), ()))
+        picked = lax.dot_general(left_high, right_high, dims, preferred_element_type=f32)
+        picked += lax.dot_general(left_low, right_high, dims, preferred_element_type=f32)
+        picked += lax.dot_general(left_high, right_low, dims, preferred_element_type=f32)
+        lane = phi_at & 127
+        first, second = shifted_window(phi_taps[k], lane & 7)
+        block = lane >> 3
+        low = picked[:8]
+        high = picked[8:16]
+        for h in range(1, 16):
+            here = block == h
+            low = jnp.where(here, picked[h * 8 : h * 8 + 8], low)
+            high = jnp.where(here, picked[h * 8 + 8 : h * 8 + 16], high)
+        out[pl.ds(k, 1), :] = jnp.sum(low * first + high * second, axis=0, keepdims=True)
+        return carry
+
+    lax.fori_loop(0, STEP_SLOTS, one, 0)
+
+
+def read_points(cycle_taps, phi_taps, cycle_start, phi_start, tiles):
+    slots, n = cycle_start.shape
+    flat = pl.BlockSpec((STEP_SLOTS, n), lambda i: (i, 0))
+    taps = pl.BlockSpec((STEP_SLOTS, TAPS, n), lambda i: (i, 0, 0))
+    rows, part_count = tiles.shape[:2]
+    return pl.pallas_call(
+        read_kernel,
+        grid=(slots // STEP_SLOTS,),
+        in_specs=[
+            taps,
+            taps,
+            flat,
+            flat,
+            pl.BlockSpec((rows, part_count, STEP_SLOTS, 8, LANES), lambda i: (0, 0, i, 0, 0)),
+        ],
+        out_specs=flat,
+        out_shape=jax.ShapeDtypeStruct((slots, n), f32),
+        compiler_params=pltpu.CompilerParams(vmem_limit_bytes=VMEM_LIMIT),
+        cost_estimate=pl.CostEstimate(
+            flops=slots * 2 * 3 * 256 * 256 * n, bytes_accessed=slots * (19 + 32) * n * 4, transcendentals=0
+        ),
+        name="read_back",
+    )(cycle_taps, phi_taps, cycle_start, phi_start, tiles)
+
+
+def collect_kernel(tile_list, arrived, out):
+    step = pl.program_id(0)
+    sources = arrived.shape[0]
+    columns, per_column = tile_list.shape[1], tile_list.shape[2]
+
+    @pl.when(step == 0)
+    def _():
+        def clear(j, carry):
+            out[j] = jnp.zeros(out.shape[1:], f32)
+            return carry
+
+        lax.fori_loop(0, out.shape[0], clear, 0)
+
+    def one(b, carry):
+        for q in range(columns):
+            owners = [tile_list[step * sources + b, q, k] for k in range(per_column)]
+            sums = [out[owners[k], q] + arrived[b, q * per_column + k] for k in range(per_column)]
+            for k in range(per_column):
+                out[owners[k], q] = sums[k]
+        return carry
+
+    lax.fori_loop(0, sources, one, 0)
+
+
+def collect(arrived, tile_list, cycle_blocks):
+    blocks, slots = arrived.shape[:2]
+    columns = tile_list.shape[1]
+    step = 4
+    return pl.pallas_call(
+        collect_kernel,
+        grid=(blocks // step,),
+        in_specs=[
+            pl.BlockSpec(memory_space=pltpu.SMEM),
+            pl.BlockSpec((step, slots, 8, LANES), lambda i: (i, 0, 0, 0)),
+        ],
+        out_specs=pl.BlockSpec((cycle_blocks, columns, 8, LANES), lambda i: (0, 0, 0, 0)),
+        out_shape=jax.ShapeDtypeStruct((cycle_blocks, columns, 8, LANES), f32),
+        compiler_params=pltpu.CompilerParams(vmem_limit_bytes=VMEM_LIMIT),
+        cost_estimate=pl.CostEstimate(flops=blocks * slots * 1024, bytes_accessed=16 * 2**20, transcendentals=0),
+        name="collect",
+    )(tile_list, arrived)
+
+
+def pick_kernel(tile_list, filtered, out):
+    step = pl.program_id(0)
+    columns, per_column = tile_list.shape[1], tile_list.shape[2]
+
+    def one(b, carry):
+        for q in range(columns):
+            for k in range(per_column):
+                out[b, q * per_column + k] = filtered[q, tile_list[step * out.shape[0] + b, q, k]]
+        return carry
+
+    lax.fori_loop(0, out.shape[0], one, 0)
+
+
+def pick(filtered, tile_list):
+    blocks, columns, per_column = tile_list.shape
+    slots = columns * per_column
+    step = 4
+    return pl.pallas_call(
+        pick_kernel,
+        grid=(blocks // step,),
+        in_specs=[
+            pl.BlockSpec(memory_space=pltpu.SMEM),
+            pl.BlockSpec(filtered.shape, lambda i: (0, 0, 0, 0)),
+        ],
+        out_specs=pl.BlockSpec((step, slots, 8, LANES), lambda i: (i, 0, 0, 0)),
+        out_shape=jax.ShapeDtypeStruct((blocks, slots, 8, LANES), f32),
+        compiler_params=pltpu.CompilerParams(vmem_limit_bytes=VMEM_LIMIT),
+        cost_estimate=pl.CostEstimate(flops=0, bytes_accessed=16 * 2**20, transcendentals=0),
+        name="pick",
+    )(tile_list, filtered)
+
+
+def merge_kernel(arrived, out):
+    rows, blocks = arrived.shape[:2]
+    for c in range(8):
+        for j in range(blocks):
+            out[j, :, c * LANES : (c + 1) * LANES] = arrived[:, j, c, :]
+
+
+def merge_rows(arrived):
+    rows, blocks = arrived.shape[:2]
+    step = 32
+    return pl.pallas_call(
+        merge_kernel,
+        grid=(blocks // step,),
+        in_specs=[pl.BlockSpec((rows, step, 8, LANES), lambda i: (0, i, 0, 0))],
+        out_specs=pl.BlockSpec((step, rows, 8 * LANES), lambda i: (i, 0, 0)),
+        out_shape=jax.ShapeDtypeStruct((blocks, rows, 8 * LANES), f32),
+        compiler_params=pltpu.CompilerParams(vmem_limit_bytes=VMEM_LIMIT),
+        cost_estimate=pl.CostEstimate(flops=0, bytes_accessed=16 * 2**20, transcendentals=0),
+        name="merge_rows",
+    )(arrived)
+
+
+@functools.cache
+def dft_tables():
+    a = np.arange(RADIX)
+    b = np.arange(LANES)
+    first = 2.0 * np.pi / RADIX * (np.outer(a, a) % RADIX)
+    twist = 2.0 * np.pi / NPHI * np.outer(a, b)
+    second = 2.0 * np.pi / LANES * (np.outer(b, b) % LANES)
+    c1, s1, c2, s2 = np.cos(first), np.sin(first), np.cos(second), np.sin(second)
+    ahead_first = np.block([[c1, s1], [-s1, c1]])
+    back_first = np.block([[c1, -s1], [s1, c1]])
+    ahead_second = np.block([[c2, -s2], [s2, c2]])
+    back_second = np.block([[c2, s2], [-s2, c2]])
+
+    def pair(table):
+        high = np.asarray(table, np.float32).astype(bf16)
+        low = (table - high.astype(np.float64)).astype(np.float32).astype(bf16)
+        return high, low
+
+    def wide(table):
+        high, low = pair(table)
+        return np.concatenate([high, high, low], axis=1)
+
+    def stacked(table):
+        return np.stack(pair(table))
+
+    return (
+        wide(ahead_first),
+        wide(back_first),
+        stacked(ahead_second),
+        stacked(back_second),
+        np.cos(twist).astype(np.float32),
+        np.sin(twist).astype(np.float32),
+    )
+
+
+def dot(lhs, rhs):
+    return lax.dot_general(lhs, rhs, (((1,), (0,)), ((), ())), preferred_element_type=f32)
+
+
+def filter_kernel(ahead_first, back_first, ahead_second, back_second, cos_twist, sin_twist, gain, grid, out):
+    blocks = grid.shape[0]
+    pairs = blocks // 2
+    cos_t, sin_t = cos_twist[...], sin_twist[...]
+    middle = []
+    for p in range(pairs):
+        cell = jnp.concatenate([grid[2 * p].reshape(RADIX, LANES), grid[2 * p + 1].reshape(RADIX, LANES)], axis=0)
+        high, low = split(cell)
+        turned = dot(ahead_first[...], jnp.concatenate([high, low, high], axis=0))
+        real, imag = turned[:RADIX], turned[RADIX:]
+        middle.append(jnp.concatenate([real * cos_t + imag * sin_t, imag * cos_t - real * sin_t], axis=1))
+    middle = jnp.concatenate(middle, axis=0)
+
+    def second(x, table):
+        high, low = split(x)
+        return dot(high, table[0]) + dot(low, table[0]) + dot(high, table[1])
+
+    spectrum = second(middle, ahead_second)
+    spectrum = (spectrum.reshape(pairs, RADIX, 2 * LANES) * gain[...][None]).reshape(pairs * RADIX, 2 * LANES)
+    middle = second(spectrum, back_second)
+    for p in range(pairs):
+        real, imag = middle[p * RADIX : (p + 1) * RADIX, :LANES], middle[p * RADIX : (p + 1) * RADIX, LANES:]
+        cell = jnp.concatenate([real * cos_t - imag * sin_t, imag * cos_t + real * sin_t], axis=0)
+        high, low = split(cell)
+        turned = dot(back_first[...], jnp.concatenate([high, low, high], axis=0))
+        for q in range(8):
+            out[q, 2 * p] = turned[q * 8 : q * 8 + 8]
+            out[q, 2 * p + 1] = turned[RADIX + q * 8 : RADIX + q * 8 + 8]
+
+
+def filter_cycles(grid, response):
+    tables = dft_tables()
+    full = jnp.concatenate([response, response[-2:0:-1]])
+    gain = full.reshape(LANES, RADIX).T * (1.0 / NPHI)
+    gain = jnp.concatenate([gain, gain], axis=1)
+    blocks = grid.shape[0]
+    step = 16
+    whole = [
+        pl.BlockSpec(t.shape, functools.partial(lambda nd, i: (0,) * nd, t.ndim)) for t in tables + (gain,)
+    ]
+    return pl.pallas_call(
+        filter_kernel,
+        grid=(blocks // step,),
+        in_specs=whole + [pl.BlockSpec((step, 8, 8, LANES), lambda i: (i, 0, 0, 0))],
+        out_specs=pl.BlockSpec((8, step, 8, LANES), lambda i: (0, i, 0, 0)),
+        out_shape=jax.ShapeDtypeStruct((8, blocks, 8, LANES), f32),
+        compiler_params=pltpu.CompilerParams(vmem_limit_bytes=VMEM_LIMIT),
+        cost_estimate=pl.CostEstimate(
+            flops=blocks // 2 * 3 * 2 * 2 * (128 * 128 * 128 + 64 * 256 * 256),
+            bytes_accessed=16 * 2**20,
+            transcendentals=0,
+        ),
+        name="filter_cycles",
+    )(*[jnp.asarray(t) for t in tables], gain, grid)
+
+
+def row_owner_plan(values, cycle_taps, phi_taps, cycle_start, phi_start, tile_list, response):
+    part_count = lax.axis_size("tile")
+    rows = TR // part_count
+    blocks, columns, per_column = tile_list.shape
+    slots = columns * per_column
+    cycle_blocks = 256
+    values, cycle_taps, phi_taps = values[0], cycle_taps[0], phi_taps[0]
+    cycle_start, phi_start = cycle_start[0], phi_start[0]
+    tiles = spread_tiles(values, cycle_taps, phi_taps, cycle_start, phi_start, part_count)
+    tiles = tiles.reshape(rows * part_count, slots, 8, LANES)
+    arrived = lax.all_to_all(tiles, ("pts", "tile"), 0, 0, tiled=True)
+    grid = collect(arrived, tile_list, cycle_blocks)
+    filtered = filter_cycles(grid, response)
+    picked = pick(filtered, tile_list)
+    returned = lax.all_to_all(picked, ("pts", "tile"), 0, 0, tiled=True)
+    rows_here = lax.all_to_all(filtered, "pts", 0, 0, tiled=True)
+    gradient = read_points(
+        cycle_taps, phi_taps, cycle_start, phi_start, returned.reshape(rows, part_count, slots, 8, LANES)
+    )
+    return merge_rows(rows_here), gradient[None]
 
 
 precise = lax.Precision.HIGHEST
-radix_first = 64
 
 
 def contract(formula, lhs_array, rhs_array):
@@ -36,13 +400,13 @@
     return (jnp.cos(angles), jnp.sin(angles))
 
 
-def filter_cycles(cycle_rows, response):
+def filter_by_einsum(cycle_rows, response):
     length = cycle_rows.shape[-1]
-    second = length // radix_first
-    cos_first, sin_first = angle_table(radix_first, radix_first, radix_first)
-    cos_twist, sin_twist = angle_table(radix_first, second, length)
+    second = length // RADIX
+    cos_first, sin_first = angle_table(RADIX, RADIX, RADIX)
+    cos_twist, sin_twist = angle_table(RADIX, second, length)
     cos_second, sin_second = angle_table(second, second, second)
-    blocks = cycle_rows.reshape(cycle_rows.shape[:2] + (radix_first, second))
+    blocks = cycle_rows.reshape(cycle_rows.shape[:2] + (RADIX, second))
     real_one = contract("giab,ak->gikb", blocks, cos_first)
     imag_one = -contract("giab,ak->gikb", blocks, sin_first)
     real_two = real_one * cos_twist + imag_one * sin_twist
@@ -54,7 +418,7 @@
         "gikb,bm->gikm", real_two, sin_second
     )
     full_response = jnp.concatenate([response, response[-2:0:-1]])
-    gain_table = full_response.reshape(second, radix_first).T
+    gain_table = full_response.reshape(second, RADIX).T
     real_freq = real_freq * gain_table
     imag_freq = imag_freq * gain_table
     real_back = contract("gikm,bm->gikb", real_freq, cos_second) - contract(
@@ -81,27 +445,27 @@
     )
 
 
-def per_device(values, cycle_taps, phi_taps, cycle_start, phi_start, tile_list, response):
+def column_owner_plan(values, cycle_taps, phi_taps, cycle_start, phi_start, tile_list, response):
     columns = lax.axis_size("pts")
     part_count = lax.axis_size("tile")
     column = lax.axis_index("pts")
-    per_column = SLOTS_DEV // columns
+    per_column = values.shape[1] // columns
     tile_width = NPHI // columns
     cycle_part = TR // part_count
     cycle_weights = spread_matrix(cycle_taps[0], cycle_start[0], TR)
     phi_weights = spread_matrix(phi_taps[0], phi_start[0], tile_width)
     loaded = cycle_weights * values[0][:, :, None]
-    cycle_split = cycle_weights.reshape(columns, per_column, PPS, part_count, cycle_part)
-    loaded_split = loaded.reshape(columns, per_column, PPS, part_count, cycle_part)
-    phi_split = phi_weights.reshape(columns, per_column, PPS, tile_width)
+    cycle_split = cycle_weights.reshape(columns, per_column, values.shape[2], part_count, cycle_part)
+    loaded_split = loaded.reshape(columns, per_column, values.shape[2], part_count, cycle_part)
+    phi_split = phi_weights.reshape(columns, per_column, values.shape[2], tile_width)
     partial_value = contract("qkitr,qkic->qtkrc", loaded_split, phi_split)
     partial_value = partial_value.reshape(columns * part_count, per_column, cycle_part, tile_width)
     arrived = lax.all_to_all(
         partial_value, ("pts", "tile"), split_axis=0, concat_axis=0, tiled=True
     )
     wanted = lax.dynamic_index_in_dim(tile_list, column, 1, keepdims=False)
-    owned_tiles = accumulate(arrived, wanted, NJ)
-    whole_cycles = filter_cycles(
+    owned_tiles = accumulate(arrived, wanted, 256)
+    whole_cycles = filter_by_einsum(
         lax.all_to_all(owned_tiles, "pts", split_axis=0, concat_axis=2, tiled=True), response
     )
     filtered = lax.all_to_all(whole_cycles, "pts", split_axis=2, concat_axis=0, tiled=True)
@@ -110,13 +474,15 @@
     returned = lax.all_to_all(picked, ("pts", "tile"), split_axis=0, concat_axis=0, tiled=True)
     returned = returned.reshape(columns, part_count, per_column, cycle_part, tile_width)
     rows_read = contract("qkitr,qtkrc->qkic", cycle_split, returned)
-    gradient = jnp.sum(rows_read * phi_split, axis=-1).reshape(SLOTS_DEV, PPS)
+    gradient = jnp.sum(rows_read * phi_split, axis=-1).reshape(values.shape[1], values.shape[2])
     return (filtered, gradient[None])
 
 
 def solution(mesh):
+    columns, part_count = mesh.shape["pts"], mesh.shape["tile"]
+    rows_fit = columns * part_count == TR and NPHI // columns == GROUPS * LANES
     return jax.shard_map(
-        per_device,
+        row_owner_plan if rows_fit else column_owner_plan,
         mesh=mesh,
         in_specs=(
             P(("pts", "tile"), None, None),

time: 2070 us -> 698 us (0.34)
  matrix products: 1080 us -> 0 us
  waiting for transfers between devices: 727 us -> 535 us
  local copies, waits for them, and re-layouts: 174 us -> 4.98 us
  Pallas kernels: 0 us -> 140 us
  other arithmetic: 50.4 us -> 0.1 us
    dot_general x14 -> x0, matrix products: 617 us -> none  [the longest x13 598 us: contract(): return jnp.einsum(formula, lhs_array, rhs_array, precision=precise)]
    unnamed x1 -> x0, matrix products: 467 us -> none
    all_to_all x4 -> x3, waiting for transfers between devices: 727 us -> 535 us  [the longest x1 185 us: row_owner_plan(): arrived = lax.all_to_all(tiles, ('pts', 'tile'), 0, 0, tiled=True)]
    pallas_call x0 -> x6, Pallas kernels: none -> 140 us  [the longest x1 45.5 us: spread_tiles(): pl.pallas_call(spread_kernel, grid=(slots // STEP_SLOTS,), in_specs=[flat...]
    unnamed x99 -> x33, local copies, waits for them, and re-layouts: 62.1 us -> 4.76 us
    all_to_all x3 -> x0, local copies, waits for them, and re-layouts: 38.5 us -> none  [the longest x2 23.3 us: per_device(): lax.all_to_all(whole_cycles, 'pts', split_axis=2, concat_axis=0, tiled=True)]
    all_to_all x1 -> x0, other arithmetic: 26.6 us -> none  [per_device(): lax.all_to_all(whole_cycles, 'pts', split_axis=2, concat_axis=0, tiled=True)]
    reshape x4 -> x0, local copies, waits for them, and re-layouts: 25.7 us -> none  [the longest x1 16.3 us: filter_cycles(): return (spatial / length).reshape(cycle_rows.shape)]
  transfers between devices with their start and end apart: 4 -> 3, of which waited for: 4 -> 3; matrix products, arithmetic and copies ran while one was open for 1% -> 0% of each run, Pallas kernels for 0% -> 3%
where the time goes in v1:
time: 698 us; the launch traced here: 697 us
  waiting for transfers between devices  535 us (77%)
  Pallas kernels  140 us (20%)
  starting transfers between devices  16.1 us (2%)
    all_to_all x1, waiting for transfers between devices, row_owner_plan(): arrived = lax.all_to_all(tiles, ('pts', 'tile'), 0, 0, tiled=True)  185 us
    all_to_all x1, waiting for transfers between devices, row_owner_plan(): returned = lax.all_to_all(picked, ('pts', 'tile'), 0, 0, tiled=True)  175 us
    all_to_all x1, waiting for transfers between devices, row_owner_plan(): rows_here = lax.all_to_all(filtered, 'pts', 0, 0, tiled=True)  174 us
    pallas_call x1, Pallas kernels, spread_tiles(): pl.pallas_call(spread_kernel, grid=(slots // STEP_SLOTS,), in_specs=[flat...  45.5 us
    pallas_call x1, Pallas kernels, read_points(): pl.pallas_call(read_kernel, grid=(slots // STEP_SLOTS,), in_specs=[taps,...  37 us
    pallas_call x1, Pallas kernels, filter_cycles(): pl.pallas_call(filter_kernel, grid=(blocks // step,), in_specs=whole + [p...  24.3 us
  transfers between devices with their start and end apart: 3, of which 3 were waited for; matrix products, arithmetic and copies ran while one was open for 0% of the time, Pallas kernels for 3%

profile of v1, /device:TPU:0, one launch (start us, length us, event | category | flops | bytes accessed | tf_op | source)
XLA Modules:
  0.0 696.8 jit_solution(7430934431957487075)
XLA Ops:
  0.6 1.6 copy-done
  2.2 0.9 copy-done.2
  3.2 0.9 copy-done.3
  4.1 0.9 copy-done.5
  5.1 45.5 %spread.1 = f32[8,4,64,8,128]{4,3,2,1,0:T(8,128)} custom-call(f32[64,1024]{1,0:T(8,128)S(1)} %bitcast.12, f32[64,8,1024]{2,1,0:T(8,128)S(1)} %bitcast.10, f32[64,8,1024]{2,1,0:T(8,128)} %bitcast.20, s32[64,1024]{1,0:T(8,128)S(1)} %bitcast.13, s32[64,1024]{1,0:T(8,128)S(1)} %bitcast.15), custom_call_target="tpu_custom_call" | custom-call | flops 25769803776 | bytes 13369344 | tf_op jit(solution)/shard_map/spread/pallas_call | solution.py:97
  50.6 7.4 %all-to-all-start = ((f32[32,64,8,128]{3,2,1,0:T(8,128)}), f32[32,64,8,128]{3,2,1,0:T(8,128)}, u32[]{:S(2)}, u32[]{:S(2)}) async-start(f32[32,64,8,128]{3,2,1,0:T(8,128)} %bitcast.17), calls=%async_computation | async-start | bytes 16777216 | tf_op jit(solution)/shard_map/all_to_all | solution.py:368
  58.0 0.1 copy.18.tile_list
  58.2 0.1 slice.3
  58.2 0.1 reverse
  58.3 0.1 slice.4
  58.4 0.1 maximum_multiply_fusion
  58.5 0.1 mul.14
  58.5 0.1 copy.17
  58.6 0.0 copy-start.7
  58.7 185.3 %all-to-all-done.arrived = f32[32,64,8,128]{3,2,1,0:T(8,128)} async-done(((f32[32,64,8,128]{3,2,1,0:T(8,128)}), f32[32,64,8,128]{3,2,1,0:T(8,128)}, u32[]{:S(2)}, u32[]{:S(2)}) %all-to-all-start) | async-done | bytes 8388640 | tf_op jit(solution)/shard_map/all_to_all | solution.py:368
  244.1 13.3 %collect.1.grid = f32[256,8,8,128]{3,2,1,0:T(8,128)} custom-call(s32[32,8,8]{2,1,0:T(8,128)S(1)} %copy.18.tile_list, f32[32,64,8,128]{3,2,1,0:T(8,128)} %all-to-all-done.arrived), custom_call_target="tpu_custom_call" | custom-call | flops 2097152 | bytes 16777216 | tf_op jit(solution)/shard_map/collect/pallas_call | solution.py:194
  257.5 24.3 %filter_cycles.1.filtered = f32[8,256,8,128]{3,2,1,0:T(8,128)} custom-call(bf16[128,384]{1,0:T(8,128)(2,1)S(1)} %copy-done.9, bf16[128,384]{1,0:T(8,128)(2,1)S(1)} %copy-done.10, bf16[2,256,256]{2,1,0:T(8,128)(2,1)S(1)} %copy-done.7, bf16[2,256,256]{2,1,0:T(8,128)(2,1)S(1)} %copy-done.8, f32[64,128]{1,0:T(8,128)S(1)} %copy-done.11, ...), custom_call_target="tpu_custom_call" | custom-call | flops 9663676416 | bytes 16777216 | tf_op jit(solution)/shard_map/filter_cycles/pallas_call | solution.py:342
  281.8 5.0 all-to-all-start.1
  286.8 9.0 %pick.1 = f32[32,64,8,128]{3,2,1,0:T(8,128)} custom-call(s32[32,8,8]{2,1,0:T(8,128)S(1)} %copy.18.tile_list, f32[8,256,8,128]{3,2,1,0:T(8,128)} %filter_cycles.1.filtered), custom_call_target="tpu_custom_call" | custom-call | bytes 16777216 | tf_op jit(solution)/shard_map/pick/pallas_call | solution.py:226
  295.8 174.2 %all-to-all-done.1.arrived = f32[8,256,8,128]{3,2,1,0:T(8,128)} async-done(((f32[8,256,8,128]{3,2,1,0:T(8,128)}), f32[8,256,8,128]{3,2,1,0:T(8,128)}, u32[]{:S(2)}, u32[]{:S(2)}) %all-to-all-start.1) | async-done | bytes 8388640 | tf_op jit(solution)/shard_map/all_to_all | solution.py:373
  470.0 3.7 all-to-all-start.2
  473.7 10.8 %merge_rows.1 = f32[256,8,1024]{2,1,0:T(8,128)} custom-call(f32[8,256,8,128]{3,2,1,0:T(8,128)} %all-to-all-done.1.arrived), custom_call_target="tpu_custom_call" | custom-call | bytes 16777216 | tf_op jit(solution)/shard_map/merge_rows/pallas_call | solution.py:251
  484.5 175.3 %all-to-all-done.2 = f32[32,64,8,128]{3,2,1,0:T(8,128)} async-done(((f32[32,64,8,128]{3,2,1,0:T(8,128)}), f32[32,64,8,128]{3,2,1,0:T(8,128)}, u32[]{:S(2)}, u32[]{:S(2)}) %all-to-all-start.2) | async-done | bytes 8388640 | tf_op jit(solution)/shard_map/all_to_all | solution.py:372
  659.8 37.0 %read_back.1 = f32[64,1024]{1,0:T(8,128)} custom-call(f32[64,8,1024]{2,1,0:T(8,128)S(1)} %bitcast.11, f32[64,8,1024]{2,1,0:T(8,128)} %bitcast.21, s32[64,1024]{1,0:T(8,128)S(1)} %bitcast.14, s32[64,1024]{1,0:T(8,128)S(1)} %bitcast.16, f32[8,4,64,8,128]{4,3,2,1,0:T(8,128)} %bitcast.7.tiles), custom_call_target="tpu_custom_call" | custom-call | flops 25769803776 | bytes 13369344 | tf_op jit(solution)/shard_map/read_back/pallas_call | solution.py:146
  (26 shorter events, 0.1 us)
Async XLA Ops:
  0.6 1.6 copy-start
  2.2 0.9 copy-start.2
  3.2 0.9 copy-start.3
  4.1 0.9 copy-start.5
  50.6 7.4 %copy-start.14 = (s32[32,8,8]{0,2,1:T(8,128)S(1)}, s32[32,8,8]{0,2,1:T(8,128)}, u32[]{:S(2)}) copy-start(s32[32,8,8]{0,2,1:T(8,128)} %param.18) | copy-start | bytes 24580
  50.6 7.6 %copy-start.13 = (f32[4097]{0:T(1024)S(1)}, f32[4097]{0:T(1024)}, u32[]{:S(2)}) copy-start(f32[4097]{0:T(1024)} %param.19) | copy-start | bytes 49168
  50.6 193.5 %all-to-all-start = ((f32[32,64,8,128]{3,2,1,0:T(8,128)}), f32[32,64,8,128]{3,2,1,0:T(8,128)}, u32[]{:S(2)}, u32[]{:S(2)}) async-start(f32[32,64,8,128]{3,2,1,0:T(8,128)} %bitcast.17), calls=%async_computation | async-start | bytes 16777216 | tf_op jit(solution)/shard_map/all_to_all | solution.py:368
  58.6 198.8 %copy-start.7 = (bf16[2,256,256]{2,1,0:T(8,128)(2,1)S(1)}, bf16[2,256,256]{2,1,0:T(8,128)(2,1)}, u32[]{:S(2)}) copy-start(bf16[2,256,256]{2,1,0:T(8,128)(2,1)} %constant.16.clone.ahead_second) | copy-start | bytes 786436
  58.7 198.8 %copy-start.8 = (bf16[2,256,256]{2,1,0:T(8,128)(2,1)S(1)}, bf16[2,256,256]{2,1,0:T(8,128)(2,1)}, u32[]{:S(2)}) copy-start(bf16[2,256,256]{2,1,0:T(8,128)(2,1)} %constant.17.clone.back_second) | copy-start | bytes 786436
  58.7 198.8 %copy-start.9 = (bf16[128,384]{1,0:T(8,128)(2,1)S(1)}, bf16[128,384]{1,0:T(8,128)(2,1)}, u32[]{:S(2)}) copy-start(bf16[128,384]{1,0:T(8,128)(2,1)} %constant.14.clone.ahead_first) | copy-start | bytes 294916
  58.7 198.7 %copy-start.10 = (bf16[128,384]{1,0:T(8,128)(2,1)S(1)}, bf16[128,384]{1,0:T(8,128)(2,1)}, u32[]{:S(2)}) copy-start(bf16[128,384]{1,0:T(8,128)(2,1)} %constant.15.clone.back_first) | copy-start | bytes 294916
  58.7 198.7 %copy-start.11 = (f32[64,128]{1,0:T(8,128)S(1)}, f32[64,128]{1,0:T(8,128)}, u32[]{:S(2)}) copy-start(f32[64,128]{1,0:T(8,128)} %constant.18.clone.cos_twist) | copy-start | bytes 98308
  58.7 198.7 %copy-start.12 = (f32[64,128]{1,0:T(8,128)S(1)}, f32[64,128]{1,0:T(8,128)}, u32[]{:S(2)}) copy-start(f32[64,128]{1,0:T(8,128)} %constant.19.clone.sin_twist) | copy-start | bytes 98308
  281.8 188.2 %all-to-all-start.1 = ((f32[8,256,8,128]{3,2,1,0:T(8,128)}), f32[8,256,8,128]{3,2,1,0:T(8,128)}, u32[]{:S(2)}, u32[]{:S(2)}) async-start(f32[8,256,8,128]{3,2,1,0:T(8,128)} %filter_cycles.1.filtered), calls=%async_computation.1 | async-start | bytes 16777216 | tf_op jit(solution)/shard_map/all_to_all | solution.py:373
  470.0 189.8 %all-to-all-start.2 = ((f32[32,64,8,128]{3,2,1,0:T(8,128)}), f32[32,64,8,128]{3,2,1,0:T(8,128)}, u32[]{:S(2)}, u32[]{:S(2)}) async-start(f32[32,64,8,128]{3,2,1,0:T(8,128)} %pick.1), calls=%async_computation.2 | async-start | bytes 16777216 | tf_op jit(solution)/shard_map/all_to_all | solution.py:372
  473.7 186.2 %copy-start.1 = (f32[1,64,8,1024]{3,2,1,0:T(8,128)S(1)}, f32[1,64,8,1024]{3,2,1,0:T(8,128)}, u32[]{:S(2)}) copy-start(f32[1,64,8,1024]{3,2,1,0:T(8,128)} %param.14) | copy-start | bytes 6291460
  473.7 186.1 %copy-start.4 = (s32[1,64,1024]{2,1,0:T(8,128)S(1)}, s32[1,64,1024]{2,1,0:T(8,128)}, u32[]{:S(2)}) copy-start(s32[1,64,1024]{2,1,0:T(8,128)} %param.16) | copy-start | bytes 786436
  473.7 186.1 %copy-start.6 = (s32[1,64,1024]{2,1,0:T(8,128)S(1)}, s32[1,64,1024]{2,1,0:T(8,128)}, u32[]{:S(2)}) copy-start(s32[1,64,1024]{2,1,0:T(8,128)} %param.17) | copy-start | bytes 786436

commit v2 on v1

--- a/solution.py
+++ b/solution.py
@@ -89,10 +89,11 @@
     lax.fori_loop(0, STEP_SLOTS, one, 0)
 
 
-def spread_tiles(values, cycle_taps, phi_taps, cycle_start, phi_start, part_count):
-    slots, n = values.shape
-    flat = pl.BlockSpec((STEP_SLOTS, n), lambda i: (i, 0))
-    taps = pl.BlockSpec((STEP_SLOTS, TAPS, n), lambda i: (i, 0, 0))
+def spread_tiles(values, cycle_taps, phi_taps, cycle_start, phi_start, part_count, first, slots):
+    n = values.shape[1]
+    begin = first // STEP_SLOTS
+    flat = pl.BlockSpec((STEP_SLOTS, n), lambda i: (begin + i, 0))
+    taps = pl.BlockSpec((STEP_SLOTS, TAPS, n), lambda i: (begin + i, 0, 0))
     rows = TR // part_count
     return pl.pallas_call(
         spread_kernel,
@@ -163,23 +164,25 @@
     )(cycle_taps, phi_taps, cycle_start, phi_start, tiles)
 
 
-def collect_kernel(tile_list, arrived, out):
+def collect_kernel(first_column, tile_list, arrived, *rest):
+    out = rest[-1]
     step = pl.program_id(0)
-    sources = arrived.shape[0]
-    columns, per_column = tile_list.shape[1], tile_list.shape[2]
+    sources, slots = arrived.shape[:2]
+    per_column = tile_list.shape[2]
 
     @pl.when(step == 0)
     def _():
         def clear(j, carry):
-            out[j] = jnp.zeros(out.shape[1:], f32)
+            out[j] = rest[0][j] if len(rest) == 2 else jnp.zeros(out.shape[1:], f32)
             return carry
 
-        lax.fori_loop(0, out.shape[0], clear, 0)
+        lax.fori_loop(0, out.shape[0], clear, 0, unroll=8)
 
     def one(b, carry):
-        for q in range(columns):
+        for c in range(slots // per_column):
+            q = first_column + c
             owners = [tile_list[step * sources + b, q, k] for k in range(per_column)]
-            sums = [out[owners[k], q] + arrived[b, q * per_column + k] for k in range(per_column)]
+            sums = [out[owners[k], q] + arrived[b, c * per_column + k] for k in range(per_column)]
             for k in range(per_column):
                 out[owners[k], q] = sums[k]
         return carry
@@ -187,33 +190,43 @@
     lax.fori_loop(0, sources, one, 0)
 
 
-def collect(arrived, tile_list, cycle_blocks):
+def collect(arrived, tile_list, first_column, so_far, cycle_blocks):
     blocks, slots = arrived.shape[:2]
     columns = tile_list.shape[1]
     step = 4
+    whole = pl.BlockSpec((cycle_blocks, columns, 8, LANES), lambda i: (0, 0, 0, 0))
+    given = [] if so_far is None else [so_far]
     return pl.pallas_call(
-        collect_kernel,
+        functools.partial(collect_kernel, first_column),
         grid=(blocks // step,),
         in_specs=[
             pl.BlockSpec(memory_space=pltpu.SMEM),
             pl.BlockSpec((step, slots, 8, LANES), lambda i: (i, 0, 0, 0)),
-        ],
-        out_specs=pl.BlockSpec((cycle_blocks, columns, 8, LANES), lambda i: (0, 0, 0, 0)),
+        ]
+        + [whole] * len(given),
+        out_specs=whole,
         out_shape=jax.ShapeDtypeStruct((cycle_blocks, columns, 8, LANES), f32),
         compiler_params=pltpu.CompilerParams(vmem_limit_bytes=VMEM_LIMIT),
         cost_estimate=pl.CostEstimate(flops=blocks * slots * 1024, bytes_accessed=16 * 2**20, transcendentals=0),
         name="collect",
-    )(tile_list, arrived)
-
-
-def pick_kernel(tile_list, filtered, out):
+    )(tile_list, arrived, *given)
+
+
+def pick_kernel(tile_list, *refs):
+    filtered, out = refs[:-1], refs[-1]
     step = pl.program_id(0)
     columns, per_column = tile_list.shape[1], tile_list.shape[2]
+    extent = filtered[0].shape[1]
 
     def one(b, carry):
         for q in range(columns):
             for k in range(per_column):
-                out[b, q * per_column + k] = filtered[q, tile_list[step * out.shape[0] + b, q, k]]
+                j = tile_list[step * out.shape[0] + b, q, k]
+                inside = lax.rem(j, extent)
+                tile = filtered[0][q, inside]
+                for part in range(1, len(filtered)):
+                    tile = jnp.where(j >= part * extent, filtered[part][q, inside], tile)
+                out[b, q * per_column + k] = tile
         return carry
 
     lax.fori_loop(0, out.shape[0], one, 0)
@@ -226,38 +239,41 @@
     return pl.pallas_call(
         pick_kernel,
         grid=(blocks // step,),
-        in_specs=[
-            pl.BlockSpec(memory_space=pltpu.SMEM),
-            pl.BlockSpec(filtered.shape, lambda i: (0, 0, 0, 0)),
-        ],
+        in_specs=[pl.BlockSpec(memory_space=pltpu.SMEM)]
+        + [pl.BlockSpec(part.shape, lambda i: (0, 0, 0, 0)) for part in filtered],
         out_specs=pl.BlockSpec((step, slots, 8, LANES), lambda i: (i, 0, 0, 0)),
         out_shape=jax.ShapeDtypeStruct((blocks, slots, 8, LANES), f32),
         compiler_params=pltpu.CompilerParams(vmem_limit_bytes=VMEM_LIMIT),
         cost_estimate=pl.CostEstimate(flops=0, bytes_accessed=16 * 2**20, transcendentals=0),
         name="pick",
-    )(tile_list, filtered)
-
-
-def merge_kernel(arrived, out):
+    )(tile_list, *filtered)
+
+
+def merge_kernel(arrived, *rest):
+    out = rest[-1]
     rows, blocks = arrived.shape[:2]
     for c in range(8):
         for j in range(blocks):
             out[j, :, c * LANES : (c + 1) * LANES] = arrived[:, j, c, :]
 
 
-def merge_rows(arrived):
+def merge_rows(arrived, first, cycle_blocks, so_far):
     rows, blocks = arrived.shape[:2]
     step = 32
+    begin = first // step
+    given = [] if so_far is None else [so_far]
     return pl.pallas_call(
         merge_kernel,
         grid=(blocks // step,),
-        in_specs=[pl.BlockSpec((rows, step, 8, LANES), lambda i: (0, i, 0, 0))],
-        out_specs=pl.BlockSpec((step, rows, 8 * LANES), lambda i: (i, 0, 0)),
-        out_shape=jax.ShapeDtypeStruct((blocks, rows, 8 * LANES), f32),
+        in_specs=[pl.BlockSpec((rows, step, 8, LANES), lambda i: (0, i, 0, 0))]
+        + [pl.BlockSpec(memory_space=pl.ANY)] * len(given),
+        out_specs=pl.BlockSpec((step, rows, 8 * LANES), lambda i: (begin + i, 0, 0)),
+        out_shape=jax.ShapeDtypeStruct((cycle_blocks, rows, 8 * LANES), f32),
+        input_output_aliases={1: 0} if given else {},
         compiler_params=pltpu.CompilerParams(vmem_limit_bytes=VMEM_LIMIT),
-        cost_estimate=pl.CostEstimate(flops=0, bytes_accessed=16 * 2**20, transcendentals=0),
+        cost_estimate=pl.CostEstimate(flops=0, bytes_accessed=8 * blocks * rows * 1024, transcendentals=0),
         name="merge_rows",
-    )(arrived)
+    )(arrived, *given)
 
 
 @functools.cache
@@ -329,30 +345,37 @@
             out[q, 2 * p + 1] = turned[RADIX + q * 8 : RADIX + q * 8 + 8]
 
 
-def filter_cycles(grid, response):
+def filter_cycles(grid, gain, first, blocks):
     tables = dft_tables()
-    full = jnp.concatenate([response, response[-2:0:-1]])
-    gain = full.reshape(LANES, RADIX).T * (1.0 / NPHI)
-    gain = jnp.concatenate([gain, gain], axis=1)
-    blocks = grid.shape[0]
     step = 16
+    begin = first // step
     whole = [
         pl.BlockSpec(t.shape, functools.partial(lambda nd, i: (0,) * nd, t.ndim)) for t in tables + (gain,)
     ]
     return pl.pallas_call(
         filter_kernel,
         grid=(blocks // step,),
-        in_specs=whole + [pl.BlockSpec((step, 8, 8, LANES), lambda i: (i, 0, 0, 0))],
+        in_specs=whole + [pl.BlockSpec((step, 8, 8, LANES), lambda i: (begin + i, 0, 0, 0))],
         out_specs=pl.BlockSpec((8, step, 8, LANES), lambda i: (0, i, 0, 0)),
         out_shape=jax.ShapeDtypeStruct((8, blocks, 8, LANES), f32),
         compiler_params=pltpu.CompilerParams(vmem_limit_bytes=VMEM_LIMIT),
         cost_estimate=pl.CostEstimate(
             flops=blocks // 2 * 3 * 2 * 2 * (128 * 128 * 128 + 64 * 256 * 256),
-            bytes_accessed=16 * 2**20,
+            bytes_accessed=blocks * 2**16,
             transcendentals=0,
         ),
         name="filter_cycles",
     )(*[jnp.asarray(t) for t in tables], gain, grid)
+
+
+def gain_table(response):
+    full = jnp.concatenate([response, response[-2:0:-1]])
+    gain = full.reshape(LANES, RADIX).T * (1.0 / NPHI)
+    return jnp.concatenate([gain, gain], axis=1)
+
+
+SLOT_CHUNKS = (16, 48)
+FILTER_PARTS = 2
 
 
 def row_owner_plan(values, cycle_taps, phi_taps, cycle_start, phi_start, tile_list, response):
@@ -361,20 +384,31 @@
     blocks, columns, per_column = tile_list.shape
     slots = columns * per_column
     cycle_blocks = 256
-    values, cycle_taps, phi_taps = values[0], cycle_taps[0], phi_taps[0]
-    cycle_start, phi_start = cycle_start[0], phi_start[0]
-    tiles = spread_tiles(values, cycle_taps, phi_taps, cycle_start, phi_start, part_count)
-    tiles = tiles.reshape(rows * part_count, slots, 8, LANES)
-    arrived = lax.all_to_all(tiles, ("pts", "tile"), 0, 0, tiled=True)
-    grid = collect(arrived, tile_list, cycle_blocks)
-    filtered = filter_cycles(grid, response)
+    points = [x[0] for x in (values, cycle_taps, phi_taps, cycle_start, phi_start)]
+    gain = gain_table(response)
+
+    grid, at = None, 0
+    for extent in SLOT_CHUNKS:
+        tiles = spread_tiles(*points, part_count, at, extent)
+        tiles = tiles.reshape(rows * part_count, extent, 8, LANES)
+        arrived = lax.all_to_all(tiles, ("pts", "tile"), 0, 0, tiled=True)
+        grid = collect(arrived, tile_list, at // per_column, grid, cycle_blocks)
+        at += extent
+
+    part_size = cycle_blocks // FILTER_PARTS
+    filtered = [filter_cycles(grid, gain, p * part_size, part_size) for p in range(FILTER_PARTS)]
     picked = pick(filtered, tile_list)
+    shares = [lax.all_to_all(filtered[0], "pts", 0, 0, tiled=True)]
+    picked, shares[0] = lax.optimization_barrier((picked, shares[0]))
     returned = lax.all_to_all(picked, ("pts", "tile"), 0, 0, tiled=True)
-    rows_here = lax.all_to_all(filtered, "pts", 0, 0, tiled=True)
-    gradient = read_points(
-        cycle_taps, phi_taps, cycle_start, phi_start, returned.reshape(rows, part_count, slots, 8, LANES)
-    )
-    return merge_rows(rows_here), gradient[None]
+    for part in filtered[1:]:
+        part, returned = lax.optimization_barrier((part, returned))
+        shares.append(lax.all_to_all(part, "pts", 0, 0, tiled=True))
+    gradient = read_points(*points[1:], returned.reshape(rows, part_count, slots, 8, LANES))
+    whole = None
+    for p, share in enumerate(shares):
+        whole = merge_rows(share, p * part_size, cycle_blocks, whole)
+    return whole, gradient[None]
 
 
 precise = lax.Precision.HIGHEST

time: 698 us -> 632 us (0.905)
  waiting for transfers between devices: 535 us -> 262 us
  blocking collectives: 0 us -> 187 us
  Pallas kernels: 140 us -> 155 us
    all_to_all x2, waiting for transfers between devices: 349 us -> 118 us  [the longest x1 67.6 us: row_owner_plan(): shares = [lax.all_to_all(filtered[0], 'pts', 0, 0, tiled=True)]]
    all_to_all x0 -> x1, blocking collectives: none -> 187 us  [row_owner_plan(): returned = lax.all_to_all(picked, ('pts', 'tile'), 0, 0, tiled=True)]
    all_to_all x1 -> x2, waiting for transfers between devices: 185 us -> 144 us  [row_owner_plan(): arrived = lax.all_to_all(tiles, ('pts', 'tile'), 0, 0, tiled=True)]
    pallas_call x1 -> x2, Pallas kernels: 13.3 us -> 20.3 us  [collect(): pl.pallas_call(functools.partial(collect_kernel, first_column), grid=(blo...]
    pallas_call x1 -> x2, Pallas kernels: 24.3 us -> 26.2 us  [filter_cycles(): pl.pallas_call(filter_kernel, grid=(blocks // step,), in_specs=whole + [p...]
    pallas_call x1 -> x2, Pallas kernels: 45.5 us -> 46.8 us  [spread_tiles(): pl.pallas_call(spread_kernel, grid=(slots // STEP_SLOTS,), in_specs=[flat...]
  transfers between devices with their start and end apart: 3 -> 4, of which waited for: 3 -> 4; matrix products, arithmetic and copies ran while one was open for 0% -> 0% of each run, Pallas kernels for 3% -> 18%
where the time goes in v2:
time: 632 us; the launch traced here: 631 us
  waiting for transfers between devices  262 us (41%)
  blocking collectives  187 us (30%)
  Pallas kernels  155 us (25%)
  starting transfers between devices  20.6 us (3%)
    all_to_all x1, blocking collectives, row_owner_plan(): returned = lax.all_to_all(picked, ('pts', 'tile'), 0, 0, tiled=True)  187 us
    all_to_all x2, waiting for transfers between devices, row_owner_plan(): arrived = lax.all_to_all(tiles, ('pts', 'tile'), 0, 0, tiled=True)  144 us
    all_to_all x1, waiting for transfers between devices, row_owner_plan(): shares = [lax.all_to_all(filtered[0], 'pts', 0, 0, tiled=True)]  67.6 us
    all_to_all x1, waiting for transfers between devices, row_owner_plan(): shares.append(lax.all_to_all(part, 'pts', 0, 0, tiled=True))  50 us
    pallas_call x2, Pallas kernels, spread_tiles(): pl.pallas_call(spread_kernel, grid=(slots // STEP_SLOTS,), in_specs=[flat...  46.8 us
    pallas_call x1, Pallas kernels, read_points(): pl.pallas_call(read_kernel, grid=(slots // STEP_SLOTS,), in_specs=[taps,...  37 us
    pallas_call x2, Pallas kernels, filter_cycles(): pl.pallas_call(filter_kernel, grid=(blocks // step,), in_specs=whole + [p...  26.2 us
    pallas_call x2, Pallas kernels, collect(): pl.pallas_call(functools.partial(collect_kernel, first_column), grid=(blo...  20.3 us
  transfers between devices with their start and end apart: 4, of which 4 were waited for; matrix products, arithmetic and copies ran while one was open for 0% of the time, Pallas kernels for 18%

profile of v2, /device:TPU:0, one launch (start us, length us, event | category | flops | bytes accessed | tf_op | source)
XLA Modules:
  0.0 631.5 jit_solution(16394250965695252980)
XLA Ops:
  0.6 0.9 copy-done.3
  1.6 0.9 copy-done.5
  2.5 0.9 copy-done.7
  3.5 12.1 %spread.3 = f32[8,4,16,8,128]{4,3,2,1,0:T(8,128)S(1)} custom-call(f32[64,1024]{1,0:T(8,128)S(1)} %bitcast.15, f32[64,8,1024]{2,1,0:T(8,128)} %bitcast.12, f32[64,8,1024]{2,1,0:T(8,128)} %bitcast.27, s32[64,1024]{1,0:T(8,128)S(1)} %bitcast.17, s32[64,1024]{1,0:T(8,128)S(1)} %bitcast.20), custom_call_target="tpu_custom_call" | custom-call | flops 6442450944 | bytes 3342336 | tf_op jit(solution)/shard_map/spread/pallas_call | solution.py:98
  15.6 1.3 copy-done
  17.0 7.3 %all-to-all-start.1 = ((f32[32,16,8,128]{3,2,1,0:T(8,128)}), f32[32,16,8,128]{3,2,1,0:T(8,128)S(1)}, u32[]{:S(2)}, u32[]{:S(2)}) async-start(f32[32,16,8,128]{3,2,1,0:T(8,128)} %bitcast.11), calls=%async_computation.1 | async-start | bytes 4194304 | tf_op jit(solution)/shard_map/all_to_all | solution.py:394
  24.3 1.6 copy-done.1
  25.9 34.7 %spread.2 = f32[8,4,48,8,128]{4,3,2,1,0:T(8,128)} custom-call(f32[64,1024]{1,0:T(8,128)S(1)} %bitcast.16, f32[64,8,1024]{2,1,0:T(8,128)S(1)} %bitcast.13, f32[64,8,1024]{2,1,0:T(8,128)} %bitcast.28, s32[64,1024]{1,0:T(8,128)S(1)} %bitcast.18, s32[64,1024]{1,0:T(8,128)S(1)} %bitcast.21), custom_call_target="tpu_custom_call" | custom-call | flops 19327352832 | bytes 10027008 | tf_op jit(solution)/shard_map/spread/pallas_call | solution.py:98
  60.6 12.6 %all-to-all-done.1.arrived = f32[32,16,8,128]{3,2,1,0:T(8,128)S(1)} async-done(((f32[32,16,8,128]{3,2,1,0:T(8,128)}), f32[32,16,8,128]{3,2,1,0:T(8,128)S(1)}, u32[]{:S(2)}, u32[]{:S(2)}) %all-to-all-start.1) | async-done | bytes 2097184 | tf_op jit(solution)/shard_map/all_to_all | solution.py:394
  73.2 4.1 all-to-all-start
  77.9 7.7 %collect.2.rest_0_ = f32[256,8,8,128]{3,2,1,0:T(8,128)} custom-call(s32[32,8,8]{2,1,0:T(8,128)S(1)} %copy.21.tile_list, f32[32,16,8,128]{3,2,1,0:T(8,128)S(1)} %all-to-all-done.1.arrived), custom_call_target="tpu_custom_call" | custom-call | flops 524288 | bytes 16777216 | tf_op jit(solution)/shard_map/collect/pallas_call | solution.py:199
  85.7 131.7 %all-to-all-done.arrived = f32[32,48,8,128]{3,2,1,0:T(8,128)} async-done(((f32[32,48,8,128]{3,2,1,0:T(8,128)}), f32[32,48,8,128]{3,2,1,0:T(8,128)}, u32[]{:S(2)}, u32[]{:S(2)}) %all-to-all-start) | async-done | bytes 6291488 | tf_op jit(solution)/shard_map/all_to_all | solution.py:394
  217.3 12.6 %collect.3.grid = f32[256,8,8,128]{3,2,1,0:T(8,128)} custom-call(s32[32,8,8]{2,1,0:T(8,128)S(1)} %copy.21.tile_list, f32[32,48,8,128]{3,2,1,0:T(8,128)} %all-to-all-done.arrived, f32[256,8,8,128]{3,2,1,0:T(8,128)} %collect.2.rest_0_), custom_call_target="tpu_custom_call" | custom-call | flops 1572864 | bytes 16777216 | tf_op jit(solution)/shard_map/collect/pallas_call | solution.py:199
  230.0 13.1 %filter_cycles.3.refs_0_ = f32[8,128,8,128]{3,2,1,0:T(8,128)} custom-call(bf16[128,384]{1,0:T(8,128)(2,1)S(1)} %copy-done.12, bf16[128,384]{1,0:T(8,128)(2,1)S(1)} %copy-done.11, bf16[2,256,256]{2,1,0:T(8,128)(2,1)S(1)} %copy-done.10, bf16[2,256,256]{2,1,0:T(8,128)(2,1)S(1)} %copy-done.9, f32[64,128]{1,0:T(8,128)S(1)} %copy-done.14, ...), custom_call_target="tpu_custom_call" | custom-call | flops 4831838208 | bytes 8388608 | tf_op jit(solution)/shard_map/filter_cycles/pallas_call | solution.py:355
  243.1 4.6 all-to-all-start.2
  247.7 13.2 %filter_cycles.2.refs_1_ = f32[8,128,8,128]{3,2,1,0:T(8,128)} custom-call(bf16[128,384]{1,0:T(8,128)(2,1)S(1)} %copy-done.12, bf16[128,384]{1,0:T(8,128)(2,1)S(1)} %copy-done.11, bf16[2,256,256]{2,1,0:T(8,128)(2,1)S(1)} %copy-done.10, bf16[2,256,256]{2,1,0:T(8,128)(2,1)S(1)} %copy-done.9, f32[64,128]{1,0:T(8,128)S(1)} %copy-done.14, ...), custom_call_target="tpu_custom_call" | custom-call | flops 4831838208 | bytes 8388608 | tf_op jit(solution)/shard_map/filter_cycles/pallas_call | solution.py:355
  260.8 12.5 %pick.1 = f32[32,64,8,128]{3,2,1,0:T(8,128)} custom-call(s32[32,8,8]{2,1,0:T(8,128)S(1)} %copy.21.tile_list, f32[8,128,8,128]{3,2,1,0:T(8,128)} %filter_cycles.3.refs_0_, f32[8,128,8,128]{3,2,1,0:T(8,128)} %filter_cycles.2.refs_1_), custom_call_target="tpu_custom_call" | custom-call | bytes 16777216 | tf_op jit(solution)/shard_map/pick/pallas_call | solution.py:239
  273.3 67.6 %all-to-all-done.2.arrived = f32[8,128,8,128]{3,2,1,0:T(8,128)} async-done(((f32[8,128,8,128]{3,2,1,0:T(8,128)}), f32[8,128,8,128]{3,2,1,0:T(8,128)}, u32[]{:S(2)}, u32[]{:S(2)}) %all-to-all-start.2) | async-done | bytes 4194336 | tf_op jit(solution)/shard_map/all_to_all | solution.py:401
  341.0 187.2 %all_to_all.25 = f32[32,64,8,128]{3,2,1,0:T(8,128)} all-to-all(f32[32,64,8,128]{3,2,1,0:T(8,128)} %pick.1), channel_id=1, replica_groups=mesh['pts'=8,'tile'=4] {'pts','tile'}, dimensions={0} | all-to-all | bytes 16777216 | tf_op jit(solution)/shard_map/all_to_all | solution.py:403
  528.1 4.6 all-to-all-start.4
  532.7 5.9 merge_rows.2.rest_0_
  538.7 37.0 %read_back.1 = f32[64,1024]{1,0:T(8,128)} custom-call(f32[64,8,1024]{2,1,0:T(8,128)S(1)} %bitcast.14, f32[64,8,1024]{2,1,0:T(8,128)} %bitcast.29, s32[64,1024]{1,0:T(8,128)S(1)} %bitcast.19, s32[64,1024]{1,0:T(8,128)S(1)} %bitcast.22, f32[8,4,64,8,128]{4,3,2,1,0:T(8,128)} %bitcast.23), custom_call_target="tpu_custom_call" | custom-call | flops 25769803776 | bytes 13369344 | tf_op jit(solution)/shard_map/read_back/pallas_call | solution.py:147
  575.7 50.0 %all-to-all-done.4.arrived = f32[8,128,8,128]{3,2,1,0:T(8,128)} async-done(((f32[8,128,8,128]{3,2,1,0:T(8,128)}), f32[8,128,8,128]{3,2,1,0:T(8,128)}, u32[]{:S(2)}, u32[]{:S(2)}) %all-to-all-start.4) | async-done | bytes 4194336 | tf_op jit(solution)/shard_map/all_to_all | solution.py:406
  625.7 5.8 merge_rows.3
  (37 shorter events, 0.6 us)
Async XLA Ops:
  0.6 1.0 copy-start.3
  1.6 0.9 copy-start.5
  2.5 0.9 copy-start.7
  3.5 20.8 %copy-start.4 = (f32[1,64,1024]{2,1,0:T(8,128)S(1)}, f32[1,64,1024]{2,1,0:T(8,128)}, u32[]{:S(2)}) copy-start(f32[1,64,1024]{2,1,0:T(8,128)} %param.13) | copy-start | bytes 786436
  3.5 20.8 %copy-start.6 = (s32[1,64,1024]{2,1,0:T(8,128)S(1)}, s32[1,64,1024]{2,1,0:T(8,128)}, u32[]{:S(2)}) copy-start(s32[1,64,1024]{2,1,0:T(8,128)} %param.16) | copy-start | bytes 786436
  3.5 20.8 %copy-start.8 = (s32[1,64,1024]{2,1,0:T(8,128)S(1)}, s32[1,64,1024]{2,1,0:T(8,128)}, u32[]{:S(2)}) copy-start(s32[1,64,1024]{2,1,0:T(8,128)} %param.17) | copy-start | bytes 786436
  15.6 1.3 copy-start
  17.0 56.2 %all-to-all-start.1 = ((f32[32,16,8,128]{3,2,1,0:T(8,128)}), f32[32,16,8,128]{3,2,1,0:T(8,128)S(1)}, u32[]{:S(2)}, u32[]{:S(2)}) async-start(f32[32,16,8,128]{3,2,1,0:T(8,128)} %bitcast.11), calls=%async_computation.1 | async-start | bytes 4194304 | tf_op jit(solution)/shard_map/all_to_all | solution.py:394
  24.3 1.6 copy-start.1
  73.2 4.1 copy-start.15
  73.2 4.6 copy-start.16
  73.2 144.2 %all-to-all-start = ((f32[32,48,8,128]{3,2,1,0:T(8,128)}), f32[32,48,8,128]{3,2,1,0:T(8,128)}, u32[]{:S(2)}, u32[]{:S(2)}) async-start(f32[32,48,8,128]{3,2,1,0:T(8,128)} %bitcast.24), calls=%async_computation | async-start | bytes 12582912 | tf_op jit(solution)/shard_map/all_to_all | solution.py:394
  85.6 144.3 %copy-start.9 = (bf16[2,256,256]{2,1,0:T(8,128)(2,1)S(1)}, bf16[2,256,256]{2,1,0:T(8,128)(2,1)}, u32[]{:S(2)}) copy-start(bf16[2,256,256]{2,1,0:T(8,128)(2,1)} %constant.17.clone.back_second) | copy-start | bytes 786436
  85.6 144.3 %copy-start.10 = (bf16[2,256,256]{2,1,0:T(8,128)(2,1)S(1)}, bf16[2,256,256]{2,1,0:T(8,128)(2,1)}, u32[]{:S(2)}) copy-start(bf16[2,256,256]{2,1,0:T(8,128)(2,1)} %constant.16.clone.ahead_second) | copy-start | bytes 786436
  85.6 144.3 %copy-start.11 = (bf16[128,384]{1,0:T(8,128)(2,1)S(1)}, bf16[128,384]{1,0:T(8,128)(2,1)}, u32[]{:S(2)}) copy-start(bf16[128,384]{1,0:T(8,128)(2,1)} %constant.15.clone.back_first) | copy-start | bytes 294916
  85.6 144.3 %copy-start.12 = (bf16[128,384]{1,0:T(8,128)(2,1)S(1)}, bf16[128,384]{1,0:T(8,128)(2,1)}, u32[]{:S(2)}) copy-start(bf16[128,384]{1,0:T(8,128)(2,1)} %constant.14.clone.ahead_first) | copy-start | bytes 294916
  85.6 144.3 %copy-start.13 = (f32[64,128]{1,0:T(8,128)S(1)}, f32[64,128]{1,0:T(8,128)}, u32[]{:S(2)}) copy-start(f32[64,128]{1,0:T(8,128)} %constant.19.clone.sin_twist) | copy-start | bytes 98308
  85.6 144.3 %copy-start.14 = (f32[64,128]{1,0:T(8,128)S(1)}, f32[64,128]{1,0:T(8,128)}, u32[]{:S(2)}) copy-start(f32[64,128]{1,0:T(8,128)} %constant.18.clone.cos_twist) | copy-start | bytes 98308
  243.1 97.9 %all-to-all-start.2 = ((f32[8,128,8,128]{3,2,1,0:T(8,128)}), f32[8,128,8,128]{3,2,1,0:T(8,128)}, u32[]{:S(2)}, u32[]{:S(2)}) async-start(f32[8,128,8,128]{3,2,1,0:T(8,128)} %filter_cycles.3.refs_0_), calls=%async_computation.2 | async-start | bytes 8388608 | tf_op jit(solution)/shard_map/all_to_all | solution.py:401
  528.1 97.5 %all-to-all-start.4 = ((f32[8,128,8,128]{3,2,1,0:T(8,128)}), f32[8,128,8,128]{3,2,1,0:T(8,128)}, u32[]{:S(2)}, u32[]{:S(2)}) async-start(f32[8,128,8,128]{3,2,1,0:T(8,128)} %filter_cycles.2.refs_1_), calls=%async_computation.4 | async-start | bytes 8388608 | tf_op jit(solution)/shard_map/all_to_all | solution.py:406
  532.7 6.0 copy-start.2

commit v3 on v0

v3 whole, which is shorter than its diff:
```python
import functools
import math

import jax
import jax.numpy as jnp
import numpy as np
from jax import lax
from jax.experimental import pallas as pl
from jax.experimental.pallas import tpu as pltpu
from jax.sharding import Mesh
from jax.sharding import PartitionSpec as P

NPHI = 8192
TR = 32
TAPS = 8
LANES = 128
GROUPS = 8
RADIX = 64
STEP_SLOTS = 8
VMEM_LIMIT = 50 * 1024 * 1024

f32 = jnp.float32
bf16 = jnp.bfloat16


def split(x):
    high = x.astype(bf16)
    low = (x - high.astype(f32)).astype(bf16)
    return high, low


def split_f32(x):
    high = x.astype(bf16).astype(f32)
    return high, x - high


def shifted_window(taps, shift):
    n = taps.shape[1]
    window = jnp.concatenate([taps, jnp.zeros((8, n), f32)], axis=0)
    both = jnp.concatenate([shift, shift], axis=0)
    for bit in (1, 2, 4):
        moved = pltpu.roll(window, bit, 0)
        window = jnp.where((both & bit) != 0, moved, window)
    return window[:8], window[8:]


def twice(x):
    return jnp.concatenate([x, x], axis=0)


def cycle_factor(taps, cycle_start, phi_start):
    first, second = shifted_window(taps, cycle_start & 7)
    block = cycle_start >> 3
    rows = []
    for h in range(TR // 8):
        rows.append(jnp.where(block == h, first, jnp.where(block == h - 1, second, 0.0)))
    group = twice((phi_start >> 7).astype(f32)).astype(bf16)
    masks = [group == g for g in range(GROUPS)]
    zero = jnp.zeros(group.shape, bf16)
    parts = []
    for part in split(jnp.concatenate(rows, axis=0)):
        pieces = []
        for mask in masks:
            pieces += [jnp.where(mask, part[at : at + 16], zero) for at in range(0, TR, 16)]
        parts.append(jnp.concatenate(pieces, axis=0))
    return parts


def phi_factor(taps, phi_start):
    first, second = shifted_window(taps, phi_start & 7)
    odd = (phi_start & 8) != 0
    zero = jnp.zeros(first.shape, f32)
    near = jnp.concatenate([jnp.where(odd, zero, first), jnp.where(odd, first, second)], axis=0)
    far = jnp.concatenate([jnp.where(odd, second, zero), zero], axis=0)
    block = twice(((phi_start & 127) >> 4).astype(f32)).astype(bf16)
    masks = [block == h for h in range(8)]
    zero = jnp.zeros(block.shape, bf16)
    parts = []
    for low, high in zip(split(near), split(far)):
        pieces = [jnp.where(masks[0], low, zero)]
        for h in range(1, 8):
            pieces.append(jnp.where(masks[h], low, jnp.where(masks[h - 1], high, zero)))
        pieces.append(jnp.where(masks[7], high, zero))
        parts.append(jnp.concatenate(pieces, axis=0))
    return parts


def spread_kernel(values, cycle_taps, phi_taps, cycle_start, phi_start, out, turn):
    n = values.shape[1]
    shares, parts, rows = out.shape[:3]
    for k in range(STEP_SLOTS):
        cycle_at = jnp.broadcast_to(cycle_start[k : k + 1, :], (8, n))
        phi_at = jnp.broadcast_to(phi_start[k : k + 1, :], (8, n))
        loaded = cycle_taps[k] * values[k : k + 1, :]
        left_high, left_low = cycle_factor(loaded, cycle_at, phi_at)
        empty = jnp.zeros((256 - 144, n), bf16)
        right_high, right_low = [jnp.concatenate([x, empty], axis=0) for x in phi_factor(phi_taps[k], phi_at)]
        left = jnp.concatenate([left_high, left_high, left_low], axis=1)
        right = jnp.concatenate([right_high, right_low, right_high], axis=1)
        product = lax.dot_general(left, right, (((1,), (1,)), ((), ())), preferred_element_type=f32)
        for g in range(GROUPS):
            tile = product[g * TR : (g + 1) * TR, :LANES]
            if g:
                tile = tile + product[(g - 1) * TR : g * TR, LANES:]
            for at in range(0, TR, 8):
                turn[k, pl.ds(at * GROUPS + g, 8, stride=GROUPS), :] = tile[at : at + 8]
        for r in range(TR):
            t, p, row = r // (shares * rows), r // rows % shares, r % rows
            out[p, t, row, k] = turn[k, r * GROUPS : (r + 1) * GROUPS, :]


def point_specs(place, n):
    flat = pl.BlockSpec((STEP_SLOTS, n), lambda *at: (place(*at), 0))
    taps = pl.BlockSpec((STEP_SLOTS, TAPS, n), lambda *at: (place(*at), 0, 0))
    return [flat, taps, taps, flat, flat]


def spread_tiles(points, shares, part_count, first, slots):
    n = points[0].shape[1]
    begin = first // STEP_SLOTS
    heads = (shares, part_count, TR // (shares * part_count))
    return pl.pallas_call(
        spread_kernel,
        grid=(slots // STEP_SLOTS,),
        in_specs=point_specs(lambda i: begin + i, n),
        out_specs=pl.BlockSpec(heads + (STEP_SLOTS, 8, LANES), lambda i: (0, 0, 0, i, 0, 0)),
        out_shape=jax.ShapeDtypeStruct(heads + (slots, 8, LANES), f32),
        scratch_shapes=[pltpu.VMEM((STEP_SLOTS, TR * GROUPS, LANES), f32)],
        compiler_params=pltpu.CompilerParams(vmem_limit_bytes=VMEM_LIMIT),
        cost_estimate=pl.CostEstimate(
            flops=slots * 2 * 3 * 256 * 256 * n, bytes_accessed=slots * (19 + 32) * n * 4, transcendentals=0
        ),
        name="spread",
    )(*points)


def read_kernel(row_of, begin, cycle_taps, phi_taps, cycle_start, phi_start, tiles, *rest):
    out, turn = rest[-2:]
    n = cycle_start.shape[1]
    for k in range(STEP_SLOTS):
        cycle_at = jnp.broadcast_to(cycle_start[k : k + 1, :], (8, n))
        phi_at = jnp.broadcast_to(phi_start[k : k + 1, :], (8, n))
        right_high, right_low = cycle_factor(cycle_taps[k], cycle_at, phi_at)
        for r in range(TR):
            turn[k, r * GROUPS : (r + 1) * GROUPS, :] = tiles[row_of(r, k)]
        pieces = [
            turn[k, pl.ds(at * GROUPS + g, 8, stride=GROUPS), :] for g in range(GROUPS) for at in range(0, TR, 8)
        ]
        tile = jnp.concatenate(pieces, axis=0).T
        following = pltpu.roll(tile[:16], TR * (GROUPS - 1), 1)
        left_high, left_low = split(jnp.concatenate([tile, following], axis=0))
        left = jnp.concatenate([left_high, left_low, left_high], axis=1)
        right = jnp.concatenate([right_high, right_high, right_low], axis=0)
        picked = dot(left, right)
        lane = phi_at & 127
        first, second = shifted_window(phi_taps[k], lane & 7)
        block = lane >> 3
        low = picked[:8]
        high = picked[8:16]
        for h in range(1, 16):
            here = block == h
            low = jnp.where(here, picked[h * 8 : h * 8 + 8], low)
            high = jnp.where(here, picked[h * 8 + 8 : h * 8 + 16], high)
        out[k : k + 1, :] = jnp.sum(low * first + high * second, axis=0, keepdims=True)


def read_points(points, begin, slots, tiles, tile_spec, row_of, so_far):
    total, n = points[0].shape
    given = [] if so_far is None else [so_far]
    return pl.pallas_call(
        functools.partial(read_kernel, row_of),
        grid_spec=pltpu.PrefetchScalarGridSpec(
            num_scalar_prefetch=1,
            grid=(slots // STEP_SLOTS,),
            in_specs=point_specs(lambda i, at: at[0] + i, n)[1:]
            + [tile_spec]
            + [pl.BlockSpec(memory_space=pl.ANY)] * len(given),
            out_specs=pl.BlockSpec((STEP_SLOTS, n), lambda i, at: (at[0] + i, 0)),
            scratch_shapes=[pltpu.VMEM((STEP_SLOTS, TR * GROUPS, LANES), f32)],
        ),
        out_shape=jax.ShapeDtypeStruct((total, n), f32),
        input_output_aliases={6: 0} if given else {},
        compiler_params=pltpu.CompilerParams(vmem_limit_bytes=VMEM_LIMIT),
        cost_estimate=pl.CostEstimate(
            flops=slots * 2 * 3 * 256 * 256 * n, bytes_accessed=slots * (19 + 32) * n * 4, transcendentals=0
        ),
        name="read_back",
    )(begin // STEP_SLOTS, *points[1:], tiles, *given)


def pick_far_kernel(tile_list, *refs):
    filtered, out = refs[:-1], refs[-1]
    step = pl.program_id(0)
    blocks, columns, per_column = tile_list.shape
    first = filtered[0].shape[1]

    def one(d, carry):
        block = step * out.shape[0] + d
        other = (1 - block // (blocks // 2)) * (columns // 2)
        for c in range(columns // 2):
            for k in range(per_column):
                j = tile_list[block, other + c, k]
                early = filtered[0][other + c, jnp.minimum(j, first - 1)]
                late = filtered[1][other + c, jnp.maximum(j - first, 0)]
                out[d, c * per_column + k] = jnp.where(j < first, early, late)
        return carry

    lax.fori_loop(0, out.shape[0], one, 0)


def pick_far(filtered, tile_list):
    blocks, columns, per_column = tile_list.shape
    shape = (blocks, columns // 2 * per_column, 8, LANES)
    step = 4
    return pl.pallas_call(
        pick_far_kernel,
        grid=(blocks // step,),
        in_specs=[pl.BlockSpec(memory_space=pltpu.SMEM)]
        + [pl.BlockSpec(part.shape, lambda i: (0, 0, 0, 0)) for part in filtered],
        out_specs=pl.BlockSpec((step,) + shape[1:], lambda i: (i, 0, 0, 0)),
        out_shape=jax.ShapeDtypeStruct(shape, f32),
        compiler_params=pltpu.CompilerParams(vmem_limit_bytes=VMEM_LIMIT),
        cost_estimate=pl.CostEstimate(flops=0, bytes_accessed=12 * 2**20, transcendentals=0),
        name="pick_far",
    )(tile_list, *filtered)


def pick_near_kernel(place, tile_list, *refs):
    shares, out = refs[:-1], refs[-1]
    step = pl.program_id(0)
    per_column = tile_list.shape[2]
    rows, first = shares[0].shape[:2]

    def one(d, carry):
        block = place[0] + step * out.shape[0] + d
        for k in range(per_column):
            j = tile_list[block, place[1], k]
            for row in range(rows):
                early = shares[0][row, jnp.minimum(j, first - 1)]
                late = shares[1][row, jnp.maximum(j - first, 0)]
                out[d, k, row] = jnp.where(j < first, early, late)
        return carry

    lax.fori_loop(0, out.shape[0], one, 0)


def pick_near(shares, place, tile_list):
    blocks, columns, per_column = tile_list.shape
    shape = (blocks // 2, per_column, shares[0].shape[0], 8, LANES)
    step = 4
    return pl.pallas_call(
        pick_near_kernel,
        grid=(shape[0] // step,),
        in_specs=[pl.BlockSpec(memory_space=pltpu.SMEM)] * 2
        + [pl.BlockSpec(part.shape, lambda i: (0, 0, 0, 0)) for part in shares],
        out_specs=pl.BlockSpec((step,) + shape[1:], lambda i: (i, 0, 0, 0, 0)),
        out_shape=jax.ShapeDtypeStruct(shape, f32),
        compiler_params=pltpu.CompilerParams(vmem_limit_bytes=VMEM_LIMIT),
        cost_estimate=pl.CostEstimate(flops=0, bytes_accessed=12 * 2**20, transcendentals=0),
        name="pick_near",
    )(place, tile_list, *shares)


def merge_kernel(arrived, *rest):
    out = rest[-1]
    rows, blocks = arrived.shape[:2]
    for c in range(8):
        for j in range(blocks):
            out[j, :, c * LANES : (c + 1) * LANES] = arrived[:, j, c, :]


def merge_rows(arrived, first, cycle_blocks, so_far):
    rows, blocks = arrived.shape[:2]
    step = 32
    begin = first // step
    given = [] if so_far is None else [so_far]
    return pl.pallas_call(
        merge_kernel,
        grid=(blocks // step,),
        in_specs=[pl.BlockSpec((rows, step, 8, LANES), lambda i: (0, i, 0, 0))]
        + [pl.BlockSpec(memory_space=pl.ANY)] * len(given),
        out_specs=pl.BlockSpec((step, rows, 8 * LANES), lambda i: (begin + i, 0, 0)),
        out_shape=jax.ShapeDtypeStruct((cycle_blocks, rows, 8 * LANES), f32),
        input_output_aliases={1: 0} if given else {},
        compiler_params=pltpu.CompilerParams(vmem_limit_bytes=VMEM_LIMIT),
        cost_estimate=pl.CostEstimate(flops=0, bytes_accessed=8 * blocks * rows * 1024, transcendentals=0),
        name="merge_rows",
    )(arrived, *given)


@functools.cache
def dft_tables():
    a = np.arange(RADIX)
    b = np.arange(LANES)
    first = 2.0 * np.pi / RADIX * (np.outer(a, a) % RADIX)
    twist = 2.0 * np.pi / NPHI * np.outer(a, b)
    second = 2.0 * np.pi / LANES * (np.outer(b, b) % LANES)
    c1, s1, c2, s2 = np.cos(first), np.sin(first), np.cos(second), np.sin(second)
    ahead_first = np.block([[c1, s1], [-s1, c1]])
    back_first = np.block([[c1, -s1], [s1, c1]])
    ahead_second = np.block([[c2, -s2], [s2, c2]])
    back_second = np.block([[c2, s2], [-s2, c2]])

    def pair(table):
        high = np.asarray(table, np.float32).astype(bf16)
        low = (table - high.astype(np.float64)).astype(np.float32).astype(bf16)
        return high, low

    def wide(table):
        high, low = pair(table)
        return np.concatenate([high, high, low], axis=1)

    def stacked(table):
        high, low = pair(table)
        return np.concatenate([high, high, low], axis=0)

    return (
        wide(ahead_first),
        wide(back_first),
        stacked(ahead_second),
        stacked(back_second),
        np.cos(twist).astype(np.float32),
        np.sin(twist).astype(np.float32),
    )


def dot(lhs, rhs):
    return lax.dot_general(lhs, rhs, (((1,), (0,)), ((), ())), preferred_element_type=f32)


def first_dots(table, cells):
    turned = []
    for at in range(0, len(cells), 2):
        high, low = split(jnp.concatenate(cells[at : at + 2], axis=1))
        both = dot(table, jnp.concatenate([high, low, high], axis=0))
        turned += [both[:, :LANES], both[:, LANES:]]
    return turned


def filter_block(tables, cells):
    ahead_first, back_first, ahead_second, back_second, cos_twist, sin_twist, gain = tables
    count = len(cells)
    cos_t, sin_t = cos_twist[...], sin_twist[...]
    middle = []
    for turned in first_dots(ahead_first[...], cells):
        real, imag = turned[:RADIX], turned[RADIX:]
        middle.append(jnp.concatenate([real * cos_t + imag * sin_t, imag * cos_t - real * sin_t], axis=1))
    middle = jnp.concatenate(middle, axis=0)

    def second(x, table):
        high, low = split(x)
        return dot(jnp.concatenate([high, low, high], axis=1), table[...])

    spectrum = second(middle, ahead_second)
    spectrum = (spectrum.reshape(count, RADIX, 2 * LANES) * gain[...][None]).reshape(count * RADIX, 2 * LANES)
    middle = second(spectrum, back_second)
    cells = []
    for c in range(count):
        real, imag = middle[c * RADIX : (c + 1) * RADIX, :LANES], middle[c * RADIX : (c + 1) * RADIX, LANES:]
        cells.append(jnp.concatenate([real * cos_t - imag * sin_t, imag * cos_t + real * sin_t], axis=0))
    return first_dots(back_first[...], cells)


FILTER_STEP = 32


def filter_into(tables, grid, first, out):
    cells = [grid[first + j].reshape(RADIX, LANES) for j in range(FILTER_STEP)]
    cells = [jnp.concatenate(cells[j : j + 2], axis=0) for j in range(0, FILTER_STEP, 2)]
    for p, turned in enumerate(filter_block(tables, cells)):
        for part in range(2):
            for c in range(8):
                at = part * RADIX + c * 8
                out[c, 2 * p + part] = turned[at : at + 8]


def filter_kernel(*refs):
    filter_into(refs[:7], refs[7], 0, refs[8])


def whole_specs(arrays):
    return [pl.BlockSpec(x.shape, functools.partial(lambda nd, i: (0,) * nd, x.ndim)) for x in arrays]


def filter_cost(blocks):
    return pl.CostEstimate(
        flops=blocks * 3 * 2 * (128 * 128 * 128 + 64 * 256 * 256), bytes_accessed=blocks * 2**16, transcendentals=0
    )


def filter_cycles(grid, tables):
    blocks, columns = grid.shape[:2]
    return pl.pallas_call(
        filter_kernel,
        grid=(blocks // FILTER_STEP,),
        in_specs=whole_specs(tables) + [pl.BlockSpec((FILTER_STEP, columns, 8, LANES), lambda i: (i, 0, 0, 0))],
        out_specs=pl.BlockSpec((columns, FILTER_STEP, 8, LANES), lambda i: (0, i, 0, 0)),
        out_shape=jax.ShapeDtypeStruct((columns, blocks, 8, LANES), f32),
        compiler_params=pltpu.CompilerParams(vmem_limit_bytes=VMEM_LIMIT),
        cost_estimate=filter_cost(blocks),
        name="filter_cycles",
    )(*tables, grid)


COLLECT_STEP = 4


def collect_kernel(chunks, tile_list, *refs):
    arrived, rest = refs[: len(chunks)], refs[len(chunks) :]
    tables, (out, others, total, sem) = rest[:7], rest[7:]
    step = pl.program_id(0)
    per_column = tile_list.shape[2]
    cycle_blocks = total.shape[0]
    collecting = tile_list.shape[0] // COLLECT_STEP
    first = cycle_blocks - others.shape[0]

    @pl.when(step == 0)
    def _():
        def clear(j, carry):
            total[j] = jnp.zeros(total.shape[1:], f32)
            return carry

        lax.fori_loop(0, cycle_blocks, clear, 0, unroll=8)

    @pl.when(step < collecting)
    def _():
        for d in range(COLLECT_STEP):
            for ref, begin in zip(arrived, chunks):
                for c in range(ref.shape[1] // per_column):
                    q = begin // per_column + c
                    owners = [tile_list[step * COLLECT_STEP + d, q, k] for k in range(per_column)]
                    sums = [total[owners[k], q] + ref[d, c * per_column + k] for k in range(per_column)]
                    for k in range(per_column):
                        total[owners[k], q] = sums[k]

    hand_over = pltpu.make_async_copy(total.at[pl.ds(first, others.shape[0])], others, sem)

    @pl.when(step >= collecting)
    def _():
        @pl.when(step == collecting)
        def _():
            hand_over.start()

        filter_into(tables, total, (step - collecting) * FILTER_STEP, out)

        @pl.when(step == pl.num_programs(0) - 1)
        def _():
            hand_over.wait()


def collect_and_filter(arrived, chunks, tile_list, tables, cycle_blocks, part):
    blocks, columns, per_column = tile_list.shape
    collecting = blocks // COLLECT_STEP
    steps = part // FILTER_STEP
    return pl.pallas_call(
        functools.partial(collect_kernel, chunks),
        grid=(collecting + steps,),
        in_specs=[pl.BlockSpec(memory_space=pltpu.SMEM)]
        + [
            pl.BlockSpec((COLLECT_STEP,) + x.shape[1:], lambda i: (jnp.minimum(i, collecting - 1), 0, 0, 0))
            for x in arrived
        ]
        + whole_specs(tables),
        out_specs=[
            pl.BlockSpec((columns, FILTER_STEP, 8, LANES), lambda i: (0, jnp.maximum(i - collecting, 0), 0, 0)),
            pl.BlockSpec(memory_space=pl.ANY),
        ],
        out_shape=[
            jax.ShapeDtypeStruct((columns, part, 8, LANES), f32),
            jax.ShapeDtypeStruct((cycle_blocks - part, columns, 8, LANES), f32),
        ],
        scratch_shapes=[pltpu.VMEM((cycle_blocks, columns, 8, LANES), f32), pltpu.SemaphoreType.DMA],
        compiler_params=pltpu.CompilerParams(vmem_limit_bytes=VMEM_LIMIT),
        cost_estimate=filter_cost(part + 64),
        name="collect_filter",
    )(tile_list, *arrived, *tables)


def gain_table(response):
    full = jnp.concatenate([response, response[-2:0:-1]])
    gain = full.reshape(LANES, RADIX).T * (1.0 / NPHI)
    return jnp.concatenate([gain, gain], axis=1)


SLOT_CHUNKS = (8, 56)
FILTER_FIRST = 64
AXES = ("half", "share", "tile")


def after(x, *others):
    return lax.optimization_barrier((x, *others))[0]


def row_owner_plan(values, cycle_taps, phi_taps, cycle_start, phi_start, tile_list, response):
    half, share = lax.axis_index("half"), lax.axis_index("share")
    shares, part_count = lax.axis_size("share"), lax.axis_size("tile")
    blocks, columns, per_column = tile_list.shape
    near_slots = shares * per_column
    cycle_blocks = 256
    points = [x[0] for x in (values, cycle_taps, phi_taps, cycle_start, phi_start)]
    tables = [jnp.asarray(t) for t in dft_tables()] + [gain_table(response)]
    place = jnp.stack([half * (blocks // 2), half * shares + share]).astype(jnp.int32)

    def exchange(x, axes):
        return lax.all_to_all(x, axes, 0, 0, tiled=True)

    arrived, begins, at = [], [], 0
    for extent in SLOT_CHUNKS:
        tiles = spread_tiles(points, columns, part_count, at, extent)
        arrived.append(exchange(tiles.reshape(blocks, extent, 8, LANES), AXES))
        begins.append(at)
        at += extent
    early, others = collect_and_filter(arrived, begins, tile_list, tables, cycle_blocks, FILTER_FIRST)
    late = filter_cycles(others, tables)

    early_share = exchange(early, AXES[:2])
    far = pick_far([early, late], tile_list)
    late_share = exchange(after(late, early_share), AXES[:2])
    far_tiles = exchange(after(far, late_share), AXES)
    near = pick_near([early_share, late_share], place, tile_list)
    near_tiles = exchange(after(near, far_tiles), AXES[1:])

    far_tiles = far_tiles.reshape(columns, part_count, near_slots, 8, LANES)
    far_spec = pl.BlockSpec((columns, part_count, STEP_SLOTS, 8, LANES), lambda i, at: (0, 0, i, 0, 0))
    far_begin = ((1 - half) * near_slots).astype(jnp.int32).reshape(1)
    gradient = read_points(
        points, far_begin, near_slots, far_tiles, far_spec, lambda r, k: (r % columns, r // columns, k), None
    )
    near_tiles = near_tiles.reshape(shares, part_count, per_column, columns, 8, LANES)
    near_spec = pl.BlockSpec((None,) + near_tiles.shape[1:], lambda i, at: (i, 0, 0, 0, 0, 0))
    near_begin = (half * near_slots).astype(jnp.int32).reshape(1)
    gradient = read_points(
        points, near_begin, near_slots, near_tiles, near_spec, lambda r, k: (r // columns, k, r % columns), gradient
    )
    whole = merge_rows(early_share, 0, cycle_blocks, None)
    whole = merge_rows(late_share, FILTER_FIRST, cycle_blocks, whole)
    return whole, gradient[None]


precise = lax.Precision.HIGHEST


def contract(formula, lhs_array, rhs_array):
    return jnp.einsum(formula, lhs_array, rhs_array, precision=precise)


def spread_matrix(weights, starts, extent):
    offsets = lax.broadcasted_iota(jnp.int32, (1, 1, extent), 2) - starts[:, :, None]
    result = jnp.zeros(starts.shape + (extent,), jnp.float32)
    for tap_index in range(weights.shape[1]):
        result = result + jnp.where(offsets == tap_index, weights[:, tap_index, :, None], 0.0)
    return result


def angle_table(rows_count, cols_count, modulus):
    left_index = lax.broadcasted_iota(jnp.int32, (rows_count, cols_count), 0)
    right_index = lax.broadcasted_iota(jnp.int32, (rows_count, cols_count), 1)
    phase_int = left_index * right_index % modulus
    angles = phase_int.astype(jnp.float32) * (2.0 * math.pi / modulus)
    return (jnp.cos(angles), jnp.sin(angles))


def filter_by_einsum(cycle_rows, response):
    length = cycle_rows.shape[-1]
    second = length // RADIX
    cos_first, sin_first = angle_table(RADIX, RADIX, RADIX)
    cos_twist, sin_twist = angle_table(RADIX, second, length)
    cos_second, sin_second = angle_table(second, second, second)
    blocks = cycle_rows.reshape(cycle_rows.shape[:2] + (RADIX, second))
    real_one = contract("giab,ak->gikb", blocks, cos_first)
    imag_one = -contract("giab,ak->gikb", blocks, sin_first)
    real_two = real_one * cos_twist + imag_one * sin_twist
    imag_two = imag_one * cos_twist - real_one * sin_twist
    real_freq = contract("gikb,bm->gikm", real_two, cos_second) + contract(
        "gikb,bm->gikm", imag_two, sin_second
    )
    imag_freq = contract("gikb,bm->gikm", imag_two, cos_second) - contract(
        "gikb,bm->gikm", real_two, sin_second
    )
    full_response = jnp.concatenate([response, response[-2:0:-1]])
    gain_table = full_response.reshape(second, RADIX).T
    real_freq = real_freq * gain_table
    imag_freq = imag_freq * gain_table
    real_back = contract("gikm,bm->gikb", real_freq, cos_second) - contract(
        "gikm,bm->gikb", imag_freq, sin_second
    )
    imag_back = contract("gikm,bm->gikb", imag_freq, cos_second) + contract(
        "gikm,bm->gikb", real_freq, sin_second
    )
    real_turn = real_back * cos_twist - imag_back * sin_twist
    imag_turn = imag_back * cos_twist + real_back * sin_twist
    spatial = contract("gikb,ka->giab", real_turn, cos_first) - contract(
        "gikb,ka->giab", imag_turn, sin_first
    )
    return (spatial / length).reshape(cycle_rows.shape)


def accumulate(arrived, wanted, cycle_blocks):
    selector = (
        lax.broadcasted_iota(jnp.int32, (cycle_blocks, wanted.size), 0) == wanted.reshape(1, -1)
    ).astype(jnp.float32)
    flattened = arrived.reshape(wanted.size, -1)
    return jnp.dot(selector, flattened, precision=precise).reshape(
        (cycle_blocks,) + arrived.shape[2:]
    )


def column_owner_plan(values, cycle_taps, phi_taps, cycle_start, phi_start, tile_list, response):
    columns = lax.axis_size("pts")
    part_count = lax.axis_size("tile")
    column = lax.axis_index("pts")
    per_column = values.shape[1] // columns
    tile_width = NPHI // columns
    cycle_part = TR // part_count
    cycle_weights = spread_matrix(cycle_taps[0], cycle_start[0], TR)
    phi_weights = spread_matrix(phi_taps[0], phi_start[0], tile_width)
    loaded = cycle_weights * values[0][:, :, None]
    cycle_split = cycle_weights.reshape(columns, per_column, values.shape[2], part_count, cycle_part)
    loaded_split = loaded.reshape(columns, per_column, values.shape[2], part_count, cycle_part)
    phi_split = phi_weights.reshape(columns, per_column, values.shape[2], tile_width)
    partial_value = contract("qkitr,qkic->qtkrc", loaded_split, phi_split)
    partial_value = partial_value.reshape(columns * part_count, per_column, cycle_part, tile_width)
    arrived = lax.all_to_all(
        partial_value, ("pts", "tile"), split_axis=0, concat_axis=0, tiled=True
    )
    wanted = lax.dynamic_index_in_dim(tile_list, column, 1, keepdims=False)
    owned_tiles = accumulate(arrived, wanted, 256)
    whole_cycles = filter_by_einsum(
        lax.all_to_all(owned_tiles, "pts", split_axis=0, concat_axis=2, tiled=True), response
    )
    filtered = lax.all_to_all(whole_cycles, "pts", split_axis=2, concat_axis=0, tiled=True)
    picked = jnp.take(filtered, wanted.reshape(-1), axis=0)
    picked = picked.reshape(columns * part_count, per_column, cycle_part, tile_width)
    returned = lax.all_to_all(picked, ("pts", "tile"), split_axis=0, concat_axis=0, tiled=True)
    returned = returned.reshape(columns, part_count, per_column, cycle_part, tile_width)
    rows_read = contract("qkitr,qtkrc->qkic", cycle_split, returned)
    gradient = jnp.sum(rows_read * phi_split, axis=-1).reshape(values.shape[1], values.shape[2])
    return (filtered, gradient[None])


def solution(mesh):
    columns, part_count = mesh.shape["pts"], mesh.shape["tile"]
    step, pts, tile = column_owner_plan, "pts", "tile"
    if columns * part_count == TR and columns % 2 == 0 and NPHI // columns == GROUPS * LANES:
        mesh = Mesh(mesh.devices.reshape(2, columns // 2, part_count), AXES)
        step, pts = row_owner_plan, ("half", "share")
    block = (pts, tile) if pts == "pts" else AXES
    return jax.shard_map(
        step,
        mesh=mesh,
        in_specs=(
            P(block, None, None),
            P(block, None, None, None),
            P(block, None, None, None),
            P(block, None, None),
            P(block, None, None),
            P(),
            P(),
        ),
        out_specs=(P(None, tile, pts), P(block, None, None)),
        check_vma=False,
    )
```

time: 2070 us -> 605 us (0.29)
  matrix products: 1080 us -> 0 us
  waiting for transfers between devices: 727 us -> 448 us
  local copies, waits for them, and re-layouts: 174 us -> 9.14 us
  Pallas kernels: 0 us -> 114 us
  other arithmetic: 50.4 us -> 0.18 us
    dot_general x14 -> x0, matrix products: 617 us -> none  [the longest x13 598 us: contract(): return jnp.einsum(formula, lhs_array, rhs_array, precision=precise)]
    unnamed x1 -> x0, matrix products: 467 us -> none
    all_to_all x4 -> x6, waiting for transfers between devices: 727 us -> 448 us  [exchange(): return lax.all_to_all(x, axes, 0, 0, tiled=True)]
    pallas_call x0 -> x10, Pallas kernels: none -> 114 us  [the longest x2 34.3 us: spread_tiles(): pl.pallas_call(spread_kernel, grid=(slots // STEP_SLOTS,), in_specs=point...]
    unnamed x99 -> x41, local copies, waits for them, and re-layouts: 62.1 us -> 8.92 us
    all_to_all x3 -> x0, local copies, waits for them, and re-layouts: 38.5 us -> none  [the longest x2 23.3 us: per_device(): lax.all_to_all(whole_cycles, 'pts', split_axis=2, concat_axis=0, tiled=True)]
    all_to_all x1 -> x0, other arithmetic: 26.6 us -> none  [per_device(): lax.all_to_all(whole_cycles, 'pts', split_axis=2, concat_axis=0, tiled=True)]
    reshape x4 -> x0, local copies, waits for them, and re-layouts: 25.7 us -> none  [the longest x1 16.3 us: filter_cycles(): return (spatial / length).reshape(cycle_rows.shape)]
  transfers between devices with their start and end apart: 4 -> 6, of which waited for: 4 -> 5; matrix products, arithmetic and copies ran while one was open for 1% -> 0% of each run, Pallas kernels for 0% -> 14%
where the time goes in v3:
time: 605 us; the launch traced here: 602 us
  waiting for transfers between devices  448 us (74%)
  Pallas kernels  114 us (19%)
  starting transfers between devices  29.9 us (5%)
  local copies, waits for them, and re-layouts  9.14 us (2%)
    all_to_all x6, waiting for transfers between devices, exchange(): return lax.all_to_all(x, axes, 0, 0, tiled=True)  448 us
    pallas_call x2, Pallas kernels, spread_tiles(): pl.pallas_call(spread_kernel, grid=(slots // STEP_SLOTS,), in_specs=point...  34.3 us
    all_to_all x6, starting transfers between devices, exchange(): return lax.all_to_all(x, axes, 0, 0, tiled=True)  29.9 us
    pallas_call x2, Pallas kernels, read_points(): pl.pallas_call(functools.partial(read_kernel, row_of), grid_spec=pltpu.Pr...  23.4 us
    pallas_call x1, Pallas kernels, filter_cycles(): pl.pallas_call(filter_kernel, grid=(blocks // FILTER_STEP,), in_specs=who...  15.5 us
    pallas_call x1, Pallas kernels, collect_and_filter(): pl.pallas_call(functools.partial(collect_kernel, chunks), grid=(collectin...  14.7 us
  transfers between devices with their start and end apart: 6, of which 5 were waited for; matrix products, arithmetic and copies ran while one was open for 0% of the time, Pallas kernels for 14%

profile of v3, /device:TPU:0, one launch (start us, length us, event | category | flops | bytes accessed | tf_op | source)
XLA Modules:
  0.0 601.8 jit_solution(17599695955097879056)
XLA Ops:
  0.6 1.6 copy-done.1
  5.1 5.8 spread.2
  10.9 7.3 %all-to-all-start = ((f32[32,8,8,128]{3,2,1,0:T(8,128)}), f32[32,8,8,128]{3,2,1,0:T(8,128)S(1)}, u32[]{:S(2)}, u32[]{:S(2)}) async-start(f32[32,8,8,128]{3,2,1,0:T(8,128)} %bitcast.6), calls=%async_computation | async-start | bytes 2097152 | tf_op jit(solution)/shard_map/all_to_all | solution.py:505
  18.2 1.6 copy-done.2
  19.8 28.5 %spread.3 = f32[8,4,1,56,8,128]{5,4,3,2,1,0:T(8,128)} custom-call(f32[64,1024]{1,0:T(8,128)S(1)} %bitcast.21, f32[64,8,1024]{2,1,0:T(8,128)S(1)} %bitcast.17, f32[64,8,1024]{2,1,0:T(8,128)} %bitcast.34, s32[64,1024]{1,0:T(8,128)S(1)} %bitcast.23, s32[64,1024]{1,0:T(8,128)S(1)} %bitcast.27), custom_call_target="tpu_custom_call" | custom-call | flops 22548578304 | bytes 11698176 | tf_op jit(solution)/shard_map/spread/pallas_call | solution.py:122
  48.4 6.0 all-to-all-start.1
  54.9 162.5 %all-to-all-done.1.refs_1_ = f32[32,56,8,128]{3,2,1,0:T(8,128)} async-done(((f32[32,56,8,128]{3,2,1,0:T(8,128)}), f32[32,56,8,128]{3,2,1,0:T(8,128)}, u32[]{:S(2)}, u32[]{:S(2)}) %all-to-all-start.1) | async-done | bytes 7340064 | tf_op jit(solution)/shard_map/all_to_all | solution.py:505
  217.5 14.7 %collect_filter.1 = (f32[8,64,8,128]{3,2,1,0:T(8,128)}, f32[192,8,8,128]{3,2,1,0:T(8,128)}) custom-call(s32[32,8,8]{2,1,0:T(8,128)S(1)} %copy.21.tile_list, f32[32,8,8,128]{3,2,1,0:T(8,128)S(1)} %all-to-all-done.refs_0_, f32[32,56,8,128]{3,2,1,0:T(8,128)} %all-to-all-done.1.refs_1_, bf16[128,384]{1,0:T(8,128)(2,1)S(1)} %copy-done.13, ...), custom_call_target="tpu_custom_call" | custom-call | flops 4831838208 | bytes 8388608 | tf_op jit(solution)/shard_map/collect_filter/pallas_call | solution.py:455
  232.2 3.6 all-to-all-start.2
  236.8 15.5 %filter_cycles.1.refs_1_ = f32[8,192,8,128]{3,2,1,0:T(8,128)} custom-call(bf16[128,384]{1,0:T(8,128)(2,1)S(1)} %copy-done.13, bf16[128,384]{1,0:T(8,128)(2,1)S(1)} %copy-done.14, bf16[768,256]{1,0:T(8,128)(2,1)S(1)} %copy-done.10, bf16[768,256]{1,0:T(8,128)(2,1)S(1)} %copy-done.12, f32[64,128]{1,0:T(8,128)S(1)} %copy-done.15, f32[64,128]{1,0:T(8,128)S(1)} %copy-done.16, ...), custom_call_target="tpu_custom_call" | custom-call | flops 7247757312 | bytes 12582912 | tf_op jit(solution)/shard_map/filter_cycles/pallas_call | solution.py:393
  252.3 31.7 %all-to-all-done.2.arrived.refs_0_ = f32[8,64,8,128]{3,2,1,0:T(8,128)S(1)} async-done(((f32[8,64,8,128]{3,2,1,0:T(8,128)}), f32[8,64,8,128]{3,2,1,0:T(8,128)S(1)}, u32[]{:S(2)}, u32[]{:S(2)}) %all-to-all-start.2) | async-done | bytes 2097184 | tf_op jit(solution)/shard_map/all_to_all | solution.py:505
  284.0 4.8 all-to-all-start.3
  288.8 1.6 copy-done
  290.4 9.2 %pick_far.1 = f32[32,32,8,128]{3,2,1,0:T(8,128)} custom-call(s32[32,8,8]{2,1,0:T(8,128)S(1)} %copy.21.tile_list, f32[8,64,8,128]{3,2,1,0:T(8,128)S(1)} %copy-done, f32[8,192,8,128]{3,2,1,0:T(8,128)} %filter_cycles.1.refs_1_), custom_call_target="tpu_custom_call" | custom-call | bytes 12582912 | tf_op jit(solution)/shard_map/pick_far/pallas_call | solution.py:215
  299.6 126.6 %all-to-all-done.3.arrived.refs_1_ = f32[8,192,8,128]{3,2,1,0:T(8,128)} async-done(((f32[8,192,8,128]{3,2,1,0:T(8,128)}), f32[8,192,8,128]{3,2,1,0:T(8,128)}, u32[]{:S(2)}, u32[]{:S(2)}) %all-to-all-start.3) | async-done | bytes 6291488 | tf_op jit(solution)/shard_map/all_to_all | solution.py:505
  426.2 3.6 all-to-all-start.4
  429.8 5.8 pick_near.1
  435.6 88.1 %all-to-all-done.4 = f32[32,32,8,128]{3,2,1,0:T(8,128)} async-done(((f32[32,32,8,128]{3,2,1,0:T(8,128)}), f32[32,32,8,128]{3,2,1,0:T(8,128)}, u32[]{:S(2)}, u32[]{:S(2)}) %all-to-all-start.4) | async-done | bytes 4194336 | tf_op jit(solution)/shard_map/all_to_all | solution.py:505
  523.7 4.7 all-to-all-start.5
  528.5 2.4 merge_rows.2.rest_0_
  530.9 8.4 %merge_rows.3 = f32[256,8,1024]{2,1,0:T(8,128)} custom-call(f32[8,192,8,128]{3,2,1,0:T(8,128)} %all-to-all-done.3.arrived.refs_1_, f32[256,8,1024]{2,1,0:T(8,128)} %merge_rows.2.rest_0_), custom_call_target="tpu_custom_call", output_to_operand_aliasing={{}: (1, {})} | custom-call | bytes 12582912 | tf_op jit(solution)/shard_map/merge_rows/pallas_call | solution.py:277
  539.3 11.7 %read_back.2.rest_0_ = f32[64,1024]{1,0:T(8,128)} custom-call(s32[1]{0:T(128)S(6)} %select_n.9.begin, f32[64,8,1024]{2,1,0:T(8,128)S(1)} %bitcast.18, f32[64,8,1024]{2,1,0:T(8,128)} %bitcast.35, s32[64,1024]{1,0:T(8,128)S(1)} %bitcast.24, s32[64,1024]{1,0:T(8,128)S(1)} %bitcast.28, f32[8,4,32,8,128]{4,3,2,1,0:T(8,128)} %bitcast.13.tiles), custom_call_target="tpu_custom_call" | custom-call | flops 12884901888 | bytes 6684672 | tf_op jit(solution)/shard_map/read_back/pallas_call | solution.py:170
  551.0 39.1 %all-to-all-done.5 = f32[16,8,8,8,128]{4,3,2,1,0:T(8,128)} async-done(((f32[16,8,8,8,128]{4,3,2,1,0:T(8,128)}), f32[16,8,8,8,128]{4,3,2,1,0:T(8,128)}, u32[]{:S(2)}, u32[]{:S(2)}) %all-to-all-start.5) | async-done | bytes 4194336 | tf_op jit(solution)/shard_map/all_to_all | solution.py:505
  590.1 11.7 %read_back.3 = f32[64,1024]{1,0:T(8,128)} custom-call(s32[1]{0:T(128)S(6)} %select_n.8.begin, f32[64,8,1024]{2,1,0:T(8,128)S(1)} %bitcast.19, f32[64,8,1024]{2,1,0:T(8,128)} %bitcast.36, s32[64,1024]{1,0:T(8,128)S(1)} %bitcast.25, s32[64,1024]{1,0:T(8,128)S(1)} %bitcast.29, f32[4,4,8,8,8,128]{5,4,3,2,1,0:T(8,128)} %bitcast.11.tiles, ...), custom_call_target="tpu_custom_call", output_to_operand_aliasing={{}: (6, {})} | custom-call | flops 12884901888 | bytes 6684672 | tf_op jit(solution)/shard_map/read_back/pallas_call | solution.py:170
  (45 shorter events, 4.6 us)
Async XLA Ops:
  0.6 1.6 copy-start.1
  2.2 0.9 copy-start.4
  3.2 0.9 copy-start.6
  5.1 13.1 %copy-start.5 = (f32[1,64,1024]{2,1,0:T(8,128)S(1)}, f32[1,64,1024]{2,1,0:T(8,128)}, u32[]{:S(2)}) copy-start(f32[1,64,1024]{2,1,0:T(8,128)} %param.13) | copy-start | bytes 786436
  5.1 13.1 %copy-start.7 = (s32[1,64,1024]{2,1,0:T(8,128)S(1)}, s32[1,64,1024]{2,1,0:T(8,128)}, u32[]{:S(2)}) copy-start(s32[1,64,1024]{2,1,0:T(8,128)} %param.16) | copy-start | bytes 786436
  5.1 13.1 %copy-start.9 = (s32[1,64,1024]{2,1,0:T(8,128)S(1)}, s32[1,64,1024]{2,1,0:T(8,128)}, u32[]{:S(2)}) copy-start(s32[1,64,1024]{2,1,0:T(8,128)} %param.17) | copy-start | bytes 786436
  10.9 37.4 %all-to-all-start = ((f32[32,8,8,128]{3,2,1,0:T(8,128)}), f32[32,8,8,128]{3,2,1,0:T(8,128)S(1)}, u32[]{:S(2)}, u32[]{:S(2)}) async-start(f32[32,8,8,128]{3,2,1,0:T(8,128)} %bitcast.6), calls=%async_computation | async-start | bytes 2097152 | tf_op jit(solution)/shard_map/all_to_all | solution.py:505
  18.2 1.6 copy-start.2
  48.3 6.0 %copy-start.18 = (s32[32,8,8]{0,2,1:T(8,128)S(1)}, s32[32,8,8]{0,2,1:T(8,128)}, u32[]{:S(2)}) copy-start(s32[32,8,8]{0,2,1:T(8,128)} %param.18) | copy-start | bytes 24580
  48.3 6.2 %copy-start.17 = (f32[4097]{0:T(1024)S(1)}, f32[4097]{0:T(1024)}, u32[]{:S(2)}) copy-start(f32[4097]{0:T(1024)} %param.19) | copy-start | bytes 49168
  48.3 169.1 %copy-start.10 = (bf16[768,256]{1,0:T(8,128)(2,1)S(1)}, bf16[768,256]{1,0:T(8,128)(2,1)}, u32[]{:S(2)}) copy-start(bf16[768,256]{1,0:T(8,128)(2,1)} %constant.68.clone.refs_4_.refs_2_) | copy-start | bytes 1179652
  48.3 169.1 %copy-start.11 = (bf16[768,256]{1,0:T(8,128)(2,1)S(1)}, bf16[768,256]{1,0:T(8,128)(2,1)}, u32[]{:S(2)}) copy-start(bf16[768,256]{1,0:T(8,128)(2,1)} %constant.69.clone.refs_5_.refs_3_) | copy-start | bytes 1179652
  48.3 169.1 %copy-start.13 = (bf16[128,384]{1,0:T(8,128)(2,1)S(1)}, bf16[128,384]{1,0:T(8,128)(2,1)}, u32[]{:S(2)}) copy-start(bf16[128,384]{1,0:T(8,128)(2,1)} %constant.66.clone.refs_2_.refs_0_) | copy-start | bytes 294916
  48.3 169.1 %copy-start.14 = (bf16[128,384]{1,0:T(8,128)(2,1)S(1)}, bf16[128,384]{1,0:T(8,128)(2,1)}, u32[]{:S(2)}) copy-start(bf16[128,384]{1,0:T(8,128)(2,1)} %constant.67.clone.refs_3_.refs_1_) | copy-start | bytes 294916
  48.3 169.1 %copy-start.15 = (f32[64,128]{1,0:T(8,128)S(1)}, f32[64,128]{1,0:T(8,128)}, u32[]{:S(2)}) copy-start(f32[64,128]{1,0:T(8,128)} %constant.70.clone.refs_6_.refs_4_) | copy-start | bytes 98308
  48.4 169.1 %copy-start.16 = (f32[64,128]{1,0:T(8,128)S(1)}, f32[64,128]{1,0:T(8,128)}, u32[]{:S(2)}) copy-start(f32[64,128]{1,0:T(8,128)} %constant.71.clone.refs_7_.refs_5_) | copy-start | bytes 98308
  48.4 169.1 %all-to-all-start.1 = ((f32[32,56,8,128]{3,2,1,0:T(8,128)}), f32[32,56,8,128]{3,2,1,0:T(8,128)}, u32[]{:S(2)}, u32[]{:S(2)}) async-start(f32[32,56,8,128]{3,2,1,0:T(8,128)} %bitcast.30), calls=%async_computation.1 | async-start | bytes 14680064 | tf_op jit(solution)/shard_map/all_to_all | solution.py:505
  232.2 51.9 %all-to-all-start.2 = ((f32[8,64,8,128]{3,2,1,0:T(8,128)}), f32[8,64,8,128]{3,2,1,0:T(8,128)S(1)}, u32[]{:S(2)}, u32[]{:S(2)}) async-start(f32[8,64,8,128]{3,2,1,0:T(8,128)} %get-tuple-element.8.refs_0_), calls=%async_computation.2 | async-start | bytes 4194304 | tf_op jit(solution)/shard_map/all_to_all | solution.py:505
  235.8 1.0 copy-start.12
  284.0 142.1 %all-to-all-start.3 = ((f32[8,192,8,128]{3,2,1,0:T(8,128)}), f32[8,192,8,128]{3,2,1,0:T(8,128)}, u32[]{:S(2)}, u32[]{:S(2)}) async-start(f32[8,192,8,128]{3,2,1,0:T(8,128)} %filter_cycles.1.refs_1_), calls=%async_computation.3 | async-start | bytes 12582912 | tf_op jit(solution)/shard_map/all_to_all | solution.py:505
  288.8 1.6 copy-start
  426.2 97.6 %all-to-all-start.4 = ((f32[32,32,8,128]{3,2,1,0:T(8,128)}), f32[32,32,8,128]{3,2,1,0:T(8,128)}, u32[]{:S(2)}, u32[]{:S(2)}) async-start(f32[32,32,8,128]{3,2,1,0:T(8,128)} %pick_far.1), calls=%async_computation.4 | async-start | bytes 8388608 | tf_op jit(solution)/shard_map/all_to_all | solution.py:505
  523.7 66.4 %all-to-all-start.5 = ((f32[16,8,8,8,128]{4,3,2,1,0:T(8,128)}), f32[16,8,8,8,128]{4,3,2,1,0:T(8,128)}, u32[]{:S(2)}, u32[]{:S(2)}) async-start(f32[16,8,8,8,128]{4,3,2,1,0:T(8,128)} %pick_near.1), calls=%async_computation.5 | async-start | bytes 8388608 | tf_op jit(solution)/shard_map/all_to_all | solution.py:505
  530.9 8.4 %copy-start.3 = (f32[1,64,8,1024]{3,2,1,0:T(8,128)S(1)}, f32[1,64,8,1024]{3,2,1,0:T(8,128)}, u32[]{:S(2)}) copy-start(f32[1,64,8,1024]{3,2,1,0:T(8,128)} %param.14) | copy-start | bytes 6291460
  (1 other events, 0.9 us)

commit v4 on v3

--- a/solution.py
+++ b/solution.py
@@ -17,7 +17,7 @@
 GROUPS = 8
 RADIX = 64
 STEP_SLOTS = 8
-VMEM_LIMIT = 50 * 1024 * 1024
+VMEM_LIMIT = 60 * 1024 * 1024
 
 f32 = jnp.float32
 bf16 = jnp.bfloat16
@@ -134,15 +134,15 @@
     )(*points)
 
 
-def read_kernel(row_of, begin, cycle_taps, phi_taps, cycle_start, phi_start, tiles, *rest):
-    out, turn = rest[-2:]
+def read_kernel(count, place_rows, begin, cycle_taps, phi_taps, cycle_start, phi_start, *rest):
+    tiles, (out, turn) = rest[:count], rest[-2:]
     n = cycle_start.shape[1]
     for k in range(STEP_SLOTS):
         cycle_at = jnp.broadcast_to(cycle_start[k : k + 1, :], (8, n))
         phi_at = jnp.broadcast_to(phi_start[k : k + 1, :], (8, n))
         right_high, right_low = cycle_factor(cycle_taps[k], cycle_at, phi_at)
-        for r in range(TR):
-            turn[k, r * GROUPS : (r + 1) * GROUPS, :] = tiles[row_of(r, k)]
+        for r, row in place_rows(begin, tiles, k):
+            turn[k, pl.ds(r * GROUPS, GROUPS), :] = row
         pieces = [
             turn[k, pl.ds(at * GROUPS + g, 8, stride=GROUPS), :] for g in range(GROUPS) for at in range(0, TR, 8)
         ]
@@ -164,28 +164,28 @@
         out[k : k + 1, :] = jnp.sum(low * first + high * second, axis=0, keepdims=True)
 
 
-def read_points(points, begin, slots, tiles, tile_spec, row_of, so_far):
+def read_points(points, begin, slots, tiles, tile_specs, place_rows, so_far):
     total, n = points[0].shape
     given = [] if so_far is None else [so_far]
     return pl.pallas_call(
-        functools.partial(read_kernel, row_of),
+        functools.partial(read_kernel, len(tile_specs), place_rows),
         grid_spec=pltpu.PrefetchScalarGridSpec(
             num_scalar_prefetch=1,
             grid=(slots // STEP_SLOTS,),
             in_specs=point_specs(lambda i, at: at[0] + i, n)[1:]
-            + [tile_spec]
+            + tile_specs
             + [pl.BlockSpec(memory_space=pl.ANY)] * len(given),
             out_specs=pl.BlockSpec((STEP_SLOTS, n), lambda i, at: (at[0] + i, 0)),
             scratch_shapes=[pltpu.VMEM((STEP_SLOTS, TR * GROUPS, LANES), f32)],
         ),
         out_shape=jax.ShapeDtypeStruct((total, n), f32),
-        input_output_aliases={6: 0} if given else {},
+        input_output_aliases={5 + len(tile_specs): 0} if given else {},
         compiler_params=pltpu.CompilerParams(vmem_limit_bytes=VMEM_LIMIT),
         cost_estimate=pl.CostEstimate(
             flops=slots * 2 * 3 * 256 * 256 * n, bytes_accessed=slots * (19 + 32) * n * 4, transcendentals=0
         ),
         name="read_back",
-    )(begin // STEP_SLOTS, *points[1:], tiles, *given)
+    )(begin, *points[1:], *tiles, *given)
 
 
 def pick_far_kernel(tile_list, *refs):
@@ -225,36 +225,71 @@
     )(tile_list, *filtered)
 
 
+def pick_own_kernel(place, tile_list, *refs):
+    filtered, outs = refs[:2], refs[2:]
+    columns, per_column = tile_list.shape[1:]
+    first = filtered[0].shape[1]
+
+    for d, out in enumerate(outs):
+        block = place[0] + (place[2] ^ d)
+
+        def one(c, carry):
+            column = place[4] + c
+            for k in range(per_column):
+                j = tile_list[block, column, k]
+                inside, beyond = jnp.minimum(j, first - 1), jnp.maximum(j - first, 0)
+                out[c * per_column + k] = jnp.where(j < first, filtered[0][column, inside], filtered[1][column, beyond])
+            return carry
+
+        lax.fori_loop(0, columns // 2, one, 0)
+
+
+def pick_own(filtered, place, tile_list):
+    blocks, columns, per_column = tile_list.shape
+    shape = (columns // 2 * per_column, 8, LANES)
+    return pl.pallas_call(
+        pick_own_kernel,
+        grid=(1,),
+        in_specs=[pl.BlockSpec(memory_space=pltpu.SMEM)] * 2
+        + [pl.BlockSpec(part.shape, lambda i: (0, 0, 0, 0)) for part in filtered],
+        out_specs=[pl.BlockSpec(shape, lambda i: (0, 0, 0))] * (blocks // 2),
+        out_shape=[jax.ShapeDtypeStruct(shape, f32)] * (blocks // 2),
+        compiler_params=pltpu.CompilerParams(vmem_limit_bytes=VMEM_LIMIT),
+        cost_estimate=pl.CostEstimate(flops=0, bytes_accessed=10 * 2**20, transcendentals=0),
+        name="pick_own",
+    )(place, tile_list, *filtered)
+
+
 def pick_near_kernel(place, tile_list, *refs):
-    shares, out = refs[:-1], refs[-1]
-    step = pl.program_id(0)
+    shares, outs = refs[:2], refs[2:]
     per_column = tile_list.shape[2]
-    rows, first = shares[0].shape[:2]
-
-    def one(d, carry):
-        block = place[0] + step * out.shape[0] + d
-        for k in range(per_column):
+    first = shares[0].shape[1]
+    rows = outs[0].shape[1]
+
+    for d, out in enumerate(outs):
+        block = place[0] + (place[2] ^ d)
+
+        def one(k, carry):
             j = tile_list[block, place[1], k]
+            inside, beyond = jnp.minimum(j, first - 1), jnp.maximum(j - first, 0)
             for row in range(rows):
-                early = shares[0][row, jnp.minimum(j, first - 1)]
-                late = shares[1][row, jnp.maximum(j - first, 0)]
-                out[d, k, row] = jnp.where(j < first, early, late)
-        return carry
-
-    lax.fori_loop(0, out.shape[0], one, 0)
+                at = place[3] + row
+                out[k, row] = jnp.where(j < first, shares[0][at, inside], shares[1][at, beyond])
+            return carry
+
+        lax.fori_loop(0, per_column, one, 0)
 
 
 def pick_near(shares, place, tile_list):
     blocks, columns, per_column = tile_list.shape
-    shape = (blocks // 2, per_column, shares[0].shape[0], 8, LANES)
-    step = 4
+    shape = (per_column, shares[0].shape[0] // 2, 8, LANES)
     return pl.pallas_call(
         pick_near_kernel,
-        grid=(shape[0] // step,),
+        grid=(1,),
         in_specs=[pl.BlockSpec(memory_space=pltpu.SMEM)] * 2
         + [pl.BlockSpec(part.shape, lambda i: (0, 0, 0, 0)) for part in shares],
-        out_specs=pl.BlockSpec((step,) + shape[1:], lambda i: (i, 0, 0, 0, 0)),
-        out_shape=jax.ShapeDtypeStruct(shape, f32),
+        out_specs=[pl.BlockSpec(shape, lambda i: (0, 0, 0, 0))] * (blocks // 2),
+        out_shape=[jax.ShapeDtypeStruct(shape, f32)] * (blocks // 2),
         compiler_params=pltpu.CompilerParams(vmem_limit_bytes=VMEM_LIMIT),
         cost_estimate=pl.CostEstimate(flops=0, bytes_accessed=12 * 2**20, transcendentals=0),
         name="pick_near",
@@ -483,7 +518,7 @@
 
 
 SLOT_CHUNKS = (8, 56)
-FILTER_FIRST = 64
+FILTER_FIRST = 32
 AXES = ("half", "share", "tile")
 
 
@@ -499,7 +534,10 @@
     cycle_blocks = 256
     points = [x[0] for x in (values, cycle_taps, phi_taps, cycle_start, phi_start)]
     tables = [jnp.asarray(t) for t in dft_tables()] + [gain_table(response)]
-    place = jnp.stack([half * (blocks // 2), half * shares + share]).astype(jnp.int32)
+    index = share * part_count + lax.axis_index("tile")
+    place = jnp.stack(
+        [half * (blocks // 2), half * shares + share, index, (1 - half) * shares, half * shares]
+    ).astype(jnp.int32)
 
     def exchange(x, axes):
         return lax.all_to_all(x, axes, 0, 0, tiled=True)
@@ -513,25 +551,42 @@
     early, others = collect_and_filter(arrived, begins, tile_list, tables, cycle_blocks, FILTER_FIRST)
     late = filter_cycles(others, tables)
 
+    def pass_on(parts):
+        moved = [parts[0]]
+        for d in range(1, blocks // 2):
+            moved.append(lax.ppermute(parts[d], AXES[1:], [(i, i ^ d) for i in range(blocks // 2)]))
+        return moved
+
     early_share = exchange(early, AXES[:2])
     far = pick_far([early, late], tile_list)
     late_share = exchange(after(late, early_share), AXES[:2])
-    far_tiles = exchange(after(far, late_share), AXES)
-    near = pick_near([early_share, late_share], place, tile_list)
-    near_tiles = exchange(after(near, far_tiles), AXES[1:])
+    own = pass_on(pick_own([after(early, far), late], place, tile_list))
+    far_tiles = exchange(after(far, late_share, *own[1:]), AXES)
+    near = pass_on(pick_near([early_share, late_share], place, tile_list))
 
     far_tiles = far_tiles.reshape(columns, part_count, near_slots, 8, LANES)
     far_spec = pl.BlockSpec((columns, part_count, STEP_SLOTS, 8, LANES), lambda i, at: (0, 0, i, 0, 0))
-    far_begin = ((1 - half) * near_slots).astype(jnp.int32).reshape(1)
-    gradient = read_points(
-        points, far_begin, near_slots, far_tiles, far_spec, lambda r, k: (r % columns, r // columns, k), None
-    )
-    near_tiles = near_tiles.reshape(shares, part_count, per_column, columns, 8, LANES)
-    near_spec = pl.BlockSpec((None,) + near_tiles.shape[1:], lambda i, at: (i, 0, 0, 0, 0, 0))
-    near_begin = (half * near_slots).astype(jnp.int32).reshape(1)
-    gradient = read_points(
-        points, near_begin, near_slots, near_tiles, near_spec, lambda r, k: (r // columns, k, r % columns), gradient
-    )
+
+    def far_rows(begin, tiles, k):
+        return [(r, tiles[0][r % columns, r // columns, k]) for r in range(TR)]
+
+    def near_rows(begin, tiles, k):
+        step = pl.program_id(0)
+        for t in range(part_count):
+            for p in range(shares):
+                source = begin[1] ^ (p * part_count + t)
+                yield t * columns + begin[0] + p, tiles[0][source, step * STEP_SLOTS + k]
+                source = begin[1] ^ (step * part_count + t)
+                yield t * columns + (shares - begin[0]) + p, tiles[1][source, k, p]
+
+    begin = jnp.stack([(1 - half) * shares, index]).astype(jnp.int32)
+    gradient = read_points(points, begin, near_slots, [far_tiles], [far_spec], far_rows, None)
+    near_tiles = [jnp.stack(own), jnp.stack(near)]
+    near_specs = [
+        pl.BlockSpec(x.shape, functools.partial(lambda nd, i, at: (0,) * nd, x.ndim)) for x in near_tiles
+    ]
+    begin = jnp.stack([half * shares, index]).astype(jnp.int32)
+    gradient = read_points(points, begin, near_slots, near_tiles, near_specs, near_rows, gradient)
     whole = merge_rows(early_share, 0, cycle_blocks, None)
     whole = merge_rows(late_share, FILTER_FIRST, cycle_blocks, whole)
     return whole, gradient[None]

time: 605 us -> 571 us (0.944)
  waiting for transfers between devices: 448 us -> 322 us
  starting transfers between devices: 29.9 us -> 97.8 us
  Pallas kernels: 114 us -> 131 us
    all_to_all x6 -> x5, waiting for transfers between devices: 448 us -> 169 us  [exchange(): return lax.all_to_all(x, axes, 0, 0, tiled=True)]
    ppermute x0 -> x30, waiting for transfers between devices: none -> 153 us  [pass_on(): lax.ppermute(parts[d], AXES[1:], [(i, i ^ d) for i in range(blocks // 2)])]
    ppermute x0 -> x30, starting transfers between devices: none -> 59.8 us  [pass_on(): lax.ppermute(parts[d], AXES[1:], [(i, i ^ d) for i in range(blocks // 2)])]
    pallas_call x3 -> x4, Pallas kernels: 29.2 us -> 41.2 us  [the longest x2 26.6 us: read_points(): pl.pallas_call(functools.partial(read_kernel, len(tile_specs), place_rows...]
    all_to_all x6 -> x5, starting transfers between devices: 29.9 us -> 38 us  [exchange(): return lax.all_to_all(x, axes, 0, 0, tiled=True)]
    unnamed x41 -> x67, local copies, waits for them, and re-layouts: 8.92 us -> 13 us
  transfers between devices with their start and end apart: 6 -> 35, of which waited for: 5 -> 18; matrix products, arithmetic and copies ran while one was open for 0% -> 3% of each run, Pallas kernels for 14% -> 15%
where the time goes in v4:
time: 571 us; the launch traced here: 568 us
  waiting for transfers between devices  322 us (56%)
  Pallas kernels  131 us (23%)
  starting transfers between devices  97.8 us (17%)
  local copies, waits for them, and re-layouts  14.6 us (3%)
    all_to_all x5, waiting for transfers between devices, exchange(): return lax.all_to_all(x, axes, 0, 0, tiled=True)  169 us
    ppermute x30, waiting for transfers between devices, pass_on(): lax.ppermute(parts[d], AXES[1:], [(i, i ^ d) for i in range(blocks // 2)])  153 us
    ppermute x30, starting transfers between devices, pass_on(): lax.ppermute(parts[d], AXES[1:], [(i, i ^ d) for i in range(blocks // 2)])  59.8 us
    all_to_all x5, starting transfers between devices, exchange(): return lax.all_to_all(x, axes, 0, 0, tiled=True)  38 us
    pallas_call x2, Pallas kernels, spread_tiles(): pl.pallas_call(spread_kernel, grid=(slots // STEP_SLOTS,), in_specs=point...  34.6 us
    pallas_call x2, Pallas kernels, read_points(): pl.pallas_call(functools.partial(read_kernel, len(tile_specs), place_rows...  26.6 us
    pallas_call x1, Pallas kernels, filter_cycles(): pl.pallas_call(filter_kernel, grid=(blocks // FILTER_STEP,), in_specs=who...  18.1 us
    pallas_call x1, Pallas kernels, collect_and_filter(): pl.pallas_call(functools.partial(collect_kernel, chunks), grid=(collectin...  13.7 us
  transfers between devices with their start and end apart: 35, of which 18 were waited for; matrix products, arithmetic and copies ran while one was open for 3% of the time, Pallas kernels for 15%

profile of v4, /device:TPU:0, one launch (start us, length us, event | category | flops | bytes accessed | tf_op | source)
XLA Modules:
  0.0 567.7 jit_solution(5316463501654165979)
XLA Ops:
  0.6 5.9 %spread.2 = f32[8,4,1,8,8,128]{5,4,3,2,1,0:T(8,128)} custom-call(f32[64,1024]{1,0:T(8,128)} %bitcast.92, f32[64,8,1024]{2,1,0:T(8,128)} %bitcast.84, f32[64,8,1024]{2,1,0:T(8,128)} %bitcast.88, s32[64,1024]{1,0:T(8,128)} %bitcast.94, s32[64,1024]{1,0:T(8,128)} %bitcast.98), custom_call_target="tpu_custom_call" | custom-call | flops 3221225472 | bytes 1671168 | tf_op jit(solution)/shard_map/spread/pallas_call | solution.py:122
  6.5 7.3 %all-to-all-start = ((f32[32,8,8,128]{3,2,1,0:T(8,128)}), f32[32,8,8,128]{3,2,1,0:T(8,128)S(1)}, u32[]{:S(2)}, u32[]{:S(2)}) async-start(f32[32,8,8,128]{3,2,1,0:T(8,128)} %bitcast.81), calls=%async_computation | async-start | bytes 2097152 | tf_op jit(solution)/shard_map/all_to_all | solution.py:543
  13.8 28.8 %spread.3 = f32[8,4,1,56,8,128]{5,4,3,2,1,0:T(8,128)} custom-call(f32[64,1024]{1,0:T(8,128)} %bitcast.93, f32[64,8,1024]{2,1,0:T(8,128)} %bitcast.85, f32[64,8,1024]{2,1,0:T(8,128)} %bitcast.89, s32[64,1024]{1,0:T(8,128)} %bitcast.95, s32[64,1024]{1,0:T(8,128)} %bitcast.99), custom_call_target="tpu_custom_call" | custom-call | flops 22548578304 | bytes 11698176 | tf_op jit(solution)/shard_map/spread/pallas_call | solution.py:122
  43.6 5.9 %all-to-all-start.1 = ((f32[32,56,8,128]{3,2,1,0:T(8,128)}), f32[32,56,8,128]{3,2,1,0:T(8,128)}, u32[]{:S(2)}, u32[]{:S(2)}) async-start(f32[32,56,8,128]{3,2,1,0:T(8,128)} %bitcast.80), calls=%async_computation.1 | async-start | bytes 14680064 | tf_op jit(solution)/shard_map/all_to_all | solution.py:543
  51.5 161.2 %all-to-all-done.1.refs_1_ = f32[32,56,8,128]{3,2,1,0:T(8,128)} async-done(((f32[32,56,8,128]{3,2,1,0:T(8,128)}), f32[32,56,8,128]{3,2,1,0:T(8,128)}, u32[]{:S(2)}, u32[]{:S(2)}) %all-to-all-start.1) | async-done | bytes 7340064 | tf_op jit(solution)/shard_map/all_to_all | solution.py:543
  212.7 13.7 %collect_filter.1 = (f32[8,32,8,128]{3,2,1,0:T(8,128)}, f32[224,8,8,128]{3,2,1,0:T(8,128)}) custom-call(s32[32,8,8]{2,1,0:T(8,128)} %copy.22.tile_list, f32[32,8,8,128]{3,2,1,0:T(8,128)} %copy-done.1, f32[32,56,8,128]{3,2,1,0:T(8,128)} %all-to-all-done.1.refs_1_, bf16[128,384]{1,0:T(8,128)(2,1)} %constant.33.clone.refs_2_.refs_0_, ...), custom_call_target="tpu_custom_call" | custom-call | flops 3623878656 | bytes 6291456 | tf_op jit(solution)/shard_map/collect_filter/pallas_call | solution.py:490
  230.0 18.1 %filter_cycles.1.refs_1_ = f32[8,224,8,128]{3,2,1,0:T(8,128)} custom-call(bf16[128,384]{1,0:T(8,128)(2,1)} %constant.33.clone.refs_2_.refs_0_, bf16[128,384]{1,0:T(8,128)(2,1)} %constant.34.clone.refs_3_.refs_1_, bf16[768,256]{1,0:T(8,128)(2,1)} %constant.35.clone.refs_4_.refs_2_, bf16[768,256]{1,0:T(8,128)(2,1)} %constant.36.clone.refs_5_.refs_3_, ...), custom_call_target="tpu_custom_call" | custom-call | flops 8455716864 | bytes 14680064 | tf_op jit(solution)/shard_map/filter_cycles/pallas_call | solution.py:428
  248.1 7.6 %all-to-all-done.2.arrived.refs_0_ = f32[8,32,8,128]{3,2,1,0:T(8,128)S(1)} async-done(((f32[8,32,8,128]{3,2,1,0:T(8,128)}), f32[8,32,8,128]{3,2,1,0:T(8,128)S(1)}, u32[]{:S(2)}, u32[]{:S(2)}) %all-to-all-start.2) | async-done | bytes 1048608 | tf_op jit(solution)/shard_map/all_to_all | solution.py:543
  256.7 5.0 all-to-all-start.3
  262.5 9.9 %pick_far.1 = f32[32,32,8,128]{3,2,1,0:T(8,128)} custom-call(s32[32,8,8]{2,1,0:T(8,128)} %copy.22.tile_list, f32[8,32,8,128]{3,2,1,0:T(8,128)} %get-tuple-element.42.refs_0_, f32[8,224,8,128]{3,2,1,0:T(8,128)} %filter_cycles.1.refs_1_), custom_call_target="tpu_custom_call" | custom-call | bytes 12582912 | tf_op jit(solution)/shard_map/pick_far/pallas_call | solution.py:215
  272.3 7.6 %pick_own.1 = (f32[32,8,128]{2,1,0:T(8,128)}, f32[32,8,128]{2,1,0:T(8,128)}, f32[32,8,128]{2,1,0:T(8,128)}, f32[32,8,128]{2,1,0:T(8,128)}, f32[32,8,128]{2,1,0:T...) custom-call(s32[5]{0:T(128)} %stack.136.place, ...), custom_call_target="tpu_custom_call" | custom-call | bytes 10485760 | tf_op jit(solution)/shard_map/pick_own/pallas_call | solution.py:250
  289.2 95.4 %collective-permute-done.10 = f32[32,8,128]{2,1,0:T(8,128)S(1)} collective-permute-done((f32[32,8,128]{2,1,0:T(8,128)}, f32[32,8,128]{2,1,0:T(8,128)S(1)}, u32[]{:S(2)}, u32[]{:S(2)}) %collective-permute-start.10) | collective-permute-done | bytes 131104 | tf_op jit(solution)/shard_map/ppermute | solution.py:557
  392.5 5.4 collective-permute-start.5
  401.5 7.8 %collective-permute-done.3 = f32[32,8,128]{2,1,0:T(8,128)S(1)} collective-permute-done((f32[32,8,128]{2,1,0:T(8,128)}, f32[32,8,128]{2,1,0:T(8,128)S(1)}, u32[]{:S(2)}, u32[]{:S(2)}) %collective-permute-start.3) | collective-permute-done | bytes 131104 | tf_op jit(solution)/shard_map/ppermute | solution.py:557
  409.3 11.8 %collective-permute-start.8 = (f32[32,8,128]{2,1,0:T(8,128)}, f32[32,8,128]{2,1,0:T(8,128)S(1)}, u32[]{:S(2)}, u32[]{:S(2)}) collective-permute-start(f32[32,8,128]{2,1,0:T(8,128)} %get-tuple-element.52), channel_id=1, source_target_pairs={{0,9},{1,8},{2,11},{3,10},{4,13},{5,12},{6,15},{7,14},{8,1},{9,0},... | collective-permute-start | bytes 393224 | tf_op jit(solution)/shard_map/ppermute | solution.py:557
  430.9 16.1 %all-to-all-start.4 = ((f32[32,32,8,128]{3,2,1,0:T(8,128)}), f32[32,32,8,128]{3,2,1,0:T(8,128)}, u32[]{:S(2)}, u32[]{:S(2)}) async-start(f32[32,32,8,128]{3,2,1,0:T(8,128)} %pick_far.1), calls=%async_computation.4 | async-start | bytes 8388608 | tf_op jit(solution)/shard_map/all_to_all | solution.py:543
  461.6 7.0 %pick_near.1 = (f32[8,4,8,128]{3,2,1,0:T(8,128)}, f32[8,4,8,128]{3,2,1,0:T(8,128)}, f32[8,4,8,128]{3,2,1,0:T(8,128)}, f32[8,4,8,128]{3,2,1,0:T(8,128)}, f32[8,4,...) custom-call(s32[5]{0:T(128)} %stack.136.place, ...), custom_call_target="tpu_custom_call" | custom-call | bytes 12582912 | tf_op jit(solution)/shard_map/pick_near/pallas_call | solution.py:286
  472.4 10.3 %merge_rows.3 = f32[256,8,1024]{2,1,0:T(8,128)} custom-call(f32[8,224,8,128]{3,2,1,0:T(8,128)} %all-to-all-done.3.arrived.refs_1_, f32[256,8,1024]{2,1,0:T(8,128)} %merge_rows.2.rest_0_), custom_call_target="tpu_custom_call", output_to_operand_aliasing={{}: (1, {})} | custom-call | bytes 14680064 | tf_op jit(solution)/shard_map/merge_rows/pallas_call | solution.py:312
  490.0 9.2 %collective-permute-done.20 = f32[8,4,8,128]{3,2,1,0:T(8,128)S(1)} collective-permute-done((f32[8,4,8,128]{3,2,1,0:T(8,128)S(1)}, f32[8,4,8,128]{3,2,1,0:T(8,128)S(1)}, u32[]{:S(2)}, u32[]{:S(2)}) %collective-permute-start.20) | collective-permute-done | bytes 131104 | tf_op jit(solution)/shard_map/ppermute | solution.py:557
  503.4 5.8 %collective-permute-start.26 = (f32[8,4,8,128]{3,2,1,0:T(8,128)S(1)}, f32[8,4,8,128]{3,2,1,0:T(8,128)S(1)}, u32[]{:S(2)}, u32[]{:S(2)}) collective-permute-start(f32[8,4,8,128]{3,2,1,0:T(8,128)S(1)} %copy-done.10), channel_id=1, source_target_pairs={{0,12},{1,13},{2,14},{3,15},{4,8},{5,9},{6,10},{7,11},{8,4},{9,5},... | collective-permute-start | bytes 393224 | tf_op jit(solution)/shard_map/ppermute | solution.py:557
  509.2 10.1 %collective-permute-done.22 = f32[8,4,8,128]{3,2,1,0:T(8,128)S(1)} collective-permute-done((f32[8,4,8,128]{3,2,1,0:T(8,128)S(1)}, f32[8,4,8,128]{3,2,1,0:T(8,128)S(1)}, u32[]{:S(2)}, u32[]{:S(2)}) %collective-permute-start.22) | collective-permute-done | bytes 131104 | tf_op jit(solution)/shard_map/ppermute | solution.py:557
  534.1 4.8 collective-permute-done.28
  541.1 12.7 %read_back.2.rest_2_ = f32[64,1024]{1,0:T(8,128)} custom-call(s32[2]{0:T(128)} %pad_add_fusion.1.begin, f32[64,8,1024]{2,1,0:T(8,128)} %bitcast.86, f32[64,8,1024]{2,1,0:T(8,128)} %bitcast.90, s32[64,1024]{1,0:T(8,128)} %bitcast.96, s32[64,1024]{1,0:T(8,128)} %bitcast.100, f32[8,4,32,8,128]{4,3,2,1,0:T(8,128)} %bitcast.45.rest_0_), custom_call_target="tpu_custom_call" | custom-call | flops 12884901888 | bytes 6684672 | tf_op jit(solution)/shard_map/read_back/pallas_call | solution.py:170
  553.8 13.9 %read_back.3 = f32[64,1024]{1,0:T(8,128)} custom-call(s32[2]{0:T(128)} %pad_add_fusion.begin, f32[64,8,1024]{2,1,0:T(8,128)} %bitcast.87, f32[64,8,1024]{2,1,0:T(8,128)} %bitcast.91, s32[64,1024]{1,0:T(8,128)} %bitcast.97, s32[64,1024]{1,0:T(8,128)} %bitcast.101, ...), custom_call_target="tpu_custom_call", output_to_operand_aliasing={{}: (7, {})} | custom-call | flops 12884901888 | bytes 6684672 | tf_op jit(solution)/shard_map/read_back/pallas_call | solution.py:170
  (134 shorter events, 85.4 us)
Async XLA Ops:
  6.5 36.1 %all-to-all-start = ((f32[32,8,8,128]{3,2,1,0:T(8,128)}), f32[32,8,8,128]{3,2,1,0:T(8,128)S(1)}, u32[]{:S(2)}, u32[]{:S(2)}) async-start(f32[32,8,8,128]{3,2,1,0:T(8,128)} %bitcast.81), calls=%async_computation | async-start | bytes 2097152 | tf_op jit(solution)/shard_map/all_to_all | solution.py:543
  43.6 169.1 %all-to-all-start.1 = ((f32[32,56,8,128]{3,2,1,0:T(8,128)}), f32[32,56,8,128]{3,2,1,0:T(8,128)}, u32[]{:S(2)}, u32[]{:S(2)}) async-start(f32[32,56,8,128]{3,2,1,0:T(8,128)} %bitcast.80), calls=%async_computation.1 | async-start | bytes 14680064 | tf_op jit(solution)/shard_map/all_to_all | solution.py:543
  226.4 29.3 %all-to-all-start.2 = ((f32[8,32,8,128]{3,2,1,0:T(8,128)}), f32[8,32,8,128]{3,2,1,0:T(8,128)S(1)}, u32[]{:S(2)}, u32[]{:S(2)}) async-start(f32[8,32,8,128]{3,2,1,0:T(8,128)} %get-tuple-element.42.refs_0_), calls=%async_computation.2 | async-start | bytes 2097152 | tf_op jit(solution)/shard_map/all_to_all | solution.py:543
  256.7 174.1 %all-to-all-start.3 = ((f32[8,224,8,128]{3,2,1,0:T(8,128)}), f32[8,224,8,128]{3,2,1,0:T(8,128)}, u32[]{:S(2)}, u32[]{:S(2)}) async-start(f32[8,224,8,128]{3,2,1,0:T(8,128)} %filter_cycles.1.refs_1_), calls=%async_computation.3 | async-start | bytes 14680064 | tf_op jit(solution)/shard_map/all_to_all | solution.py:543
  280.2 104.4 %collective-permute-start.10 = (f32[32,8,128]{2,1,0:T(8,128)}, f32[32,8,128]{2,1,0:T(8,128)S(1)}, u32[]{:S(2)}, u32[]{:S(2)}) collective-permute-start(f32[32,8,128]{2,1,0:T(8,128)} %get-tuple-element.54), channel_id=1, source_target_pairs={{0,11},{1,10},{2,9},{3,8},{4,15},{5,14},{6,13},{7,12},{8,3},{9,2},... | collective-permute-start | bytes 393224 | tf_op jit(solution)/shard_map/ppermute | solution.py:557
  283.0 104.4 %collective-permute-start.11 = (f32[32,8,128]{2,1,0:T(8,128)}, f32[32,8,128]{2,1,0:T(8,128)S(1)}, u32[]{:S(2)}, u32[]{:S(2)}) collective-permute-start(f32[32,8,128]{2,1,0:T(8,128)} %get-tuple-element.55), channel_id=1, source_target_pairs={{0,12},{1,13},{2,14},{3,15},{4,8},{5,9},{6,10},{7,11},{8,4},{9,5},... | collective-permute-start | bytes 393224 | tf_op jit(solution)/shard_map/ppermute | solution.py:557
  284.4 105.9 %collective-permute-start.12 = (f32[32,8,128]{2,1,0:T(8,128)}, f32[32,8,128]{2,1,0:T(8,128)S(1)}, u32[]{:S(2)}, u32[]{:S(2)}) collective-permute-start(f32[32,8,128]{2,1,0:T(8,128)} %get-tuple-element.56), channel_id=1, source_target_pairs={{0,13},{1,12},{2,15},{3,14},{4,9},{5,8},{6,11},{7,10},{8,5},{9,4},... | collective-permute-start | bytes 393224 | tf_op jit(solution)/shard_map/ppermute | solution.py:557
  285.6 107.0 %collective-permute-start.13 = (f32[32,8,128]{2,1,0:T(8,128)}, f32[32,8,128]{2,1,0:T(8,128)S(1)}, u32[]{:S(2)}, u32[]{:S(2)}) collective-permute-start(f32[32,8,128]{2,1,0:T(8,128)} %get-tuple-element.57), channel_id=1, source_target_pairs={{0,14},{1,15},{2,12},{3,13},{4,10},{5,11},{6,8},{7,9},{8,6},{9,7},... | collective-permute-start | bytes 393224 | tf_op jit(solution)/shard_map/ppermute | solution.py:557
  286.6 111.3 %collective-permute-start.14 = (f32[32,8,128]{2,1,0:T(8,128)}, f32[32,8,128]{2,1,0:T(8,128)S(1)}, u32[]{:S(2)}, u32[]{:S(2)}) collective-permute-start(f32[32,8,128]{2,1,0:T(8,128)} %get-tuple-element.58), channel_id=1, source_target_pairs={{0,15},{1,14},{2,13},{3,12},{4,11},{5,10},{6,9},{7,8},{8,7},{9,6},... | collective-permute-start | bytes 393224 | tf_op jit(solution)/shard_map/ppermute | solution.py:557
  387.4 21.9 %collective-permute-start.3 = (f32[32,8,128]{2,1,0:T(8,128)}, f32[32,8,128]{2,1,0:T(8,128)S(1)}, u32[]{:S(2)}, u32[]{:S(2)}) collective-permute-start(f32[32,8,128]{2,1,0:T(8,128)} %get-tuple-element.47), channel_id=1, source_target_pairs={{0,4},{1,5},{2,6},{3,7},{4,0},{5,1},{6,2},{7,3},{8,12},{9,13},{10,... | collective-permute-start | bytes 393224 | tf_op jit(solution)/shard_map/ppermute | solution.py:557
  390.3 30.8 %collective-permute-start.4 = (f32[32,8,128]{2,1,0:T(8,128)}, f32[32,8,128]{2,1,0:T(8,128)S(1)}, u32[]{:S(2)}, u32[]{:S(2)}) collective-permute-start(f32[32,8,128]{2,1,0:T(8,128)} %get-tuple-element.48), channel_id=1, source_target_pairs={{0,5},{1,4},{2,7},{3,6},{4,1},{5,0},{6,3},{7,2},{8,13},{9,12},{10,... | collective-permute-start | bytes 393224 | tf_op jit(solution)/shard_map/ppermute | solution.py:557
  392.5 31.4 %collective-permute-start.5 = (f32[32,8,128]{2,1,0:T(8,128)}, f32[32,8,128]{2,1,0:T(8,128)S(1)}, u32[]{:S(2)}, u32[]{:S(2)}) collective-permute-start(f32[32,8,128]{2,1,0:T(8,128)} %get-tuple-element.49), channel_id=1, source_target_pairs={{0,6},{1,7},{2,4},{3,5},{4,2},{5,3},{6,0},{7,1},{8,14},{9,15},{10,... | collective-permute-start | bytes 393224 | tf_op jit(solution)/shard_map/ppermute | solution.py:557
  397.9 26.1 %collective-permute-start.6 = (f32[32,8,128]{2,1,0:T(8,128)}, f32[32,8,128]{2,1,0:T(8,128)S(1)}, u32[]{:S(2)}, u32[]{:S(2)}) collective-permute-start(f32[32,8,128]{2,1,0:T(8,128)} %get-tuple-element.50), channel_id=1, source_target_pairs={{0,7},{1,6},{2,5},{3,4},{4,3},{5,2},{6,1},{7,0},{8,15},{9,14},{10,... | collective-permute-start | bytes 393224 | tf_op jit(solution)/shard_map/ppermute | solution.py:557
  397.9 27.6 %collective-permute-start.7 = (f32[32,8,128]{2,1,0:T(8,128)}, f32[32,8,128]{2,1,0:T(8,128)S(1)}, u32[]{:S(2)}, u32[]{:S(2)}) collective-permute-start(f32[32,8,128]{2,1,0:T(8,128)} %get-tuple-element.51), channel_id=1, source_target_pairs={{0,8},{1,9},{2,10},{3,11},{4,12},{5,13},{6,14},{7,15},{8,0},{9,1},... | collective-permute-start | bytes 393224 | tf_op jit(solution)/shard_map/ppermute | solution.py:557
  409.3 19.2 %collective-permute-start.8 = (f32[32,8,128]{2,1,0:T(8,128)}, f32[32,8,128]{2,1,0:T(8,128)S(1)}, u32[]{:S(2)}, u32[]{:S(2)}) collective-permute-start(f32[32,8,128]{2,1,0:T(8,128)} %get-tuple-element.52), channel_id=1, source_target_pairs={{0,9},{1,8},{2,11},{3,10},{4,13},{5,12},{6,15},{7,14},{8,1},{9,0},... | collective-permute-start | bytes 393224 | tf_op jit(solution)/shard_map/ppermute | solution.py:557
  430.9 110.2 %all-to-all-start.4 = ((f32[32,32,8,128]{3,2,1,0:T(8,128)}), f32[32,32,8,128]{3,2,1,0:T(8,128)}, u32[]{:S(2)}, u32[]{:S(2)}) async-start(f32[32,32,8,128]{3,2,1,0:T(8,128)} %pick_far.1), calls=%async_computation.4 | async-start | bytes 8388608 | tf_op jit(solution)/shard_map/all_to_all | solution.py:543
  470.5 16.6 %collective-permute-start.18 = (f32[8,4,8,128]{3,2,1,0:T(8,128)}, f32[8,4,8,128]{3,2,1,0:T(8,128)S(1)}, u32[]{:S(2)}, u32[]{:S(2)}) collective-permute-start(f32[8,4,8,128]{3,2,1,0:T(8,128)} %get-tuple-element.63), channel_id=1, source_target_pairs={{0,4},{1,5},{2,6},{3,7},{4,0},{5,1},{6,2},{7,3},{8,12},{9,13},{10,... | collective-permute-start | bytes 393224 | tf_op jit(solution)/shard_map/ppermute | solution.py:557
  485.3 18.1 %collective-permute-start.21 = (f32[8,4,8,128]{3,2,1,0:T(8,128)S(1)}, f32[8,4,8,128]{3,2,1,0:T(8,128)S(1)}, u32[]{:S(2)}, u32[]{:S(2)}) collective-permute-start(f32[8,4,8,128]{3,2,1,0:T(8,128)S(1)} %copy-done.15), channel_id=1, source_target_pairs={{0,7},{1,6},{2,5},{3,4},{4,3},{5,2},{6,1},{7,0},{8,15},{9,14},{10,... | collective-permute-start | bytes 393224 | tf_op jit(solution)/shard_map/ppermute | solution.py:557
  485.4 33.9 %collective-permute-start.22 = (f32[8,4,8,128]{3,2,1,0:T(8,128)S(1)}, f32[8,4,8,128]{3,2,1,0:T(8,128)S(1)}, u32[]{:S(2)}, u32[]{:S(2)}) collective-permute-start(f32[8,4,8,128]{3,2,1,0:T(8,128)S(1)} %copy-done.14), channel_id=1, source_target_pairs={{0,8},{1,9},{2,10},{3,11},{4,12},{5,13},{6,14},{7,15},{8,0},{9,1},... | collective-permute-start | bytes 393224 | tf_op jit(solution)/shard_map/ppermute | solution.py:557
  487.2 35.0 %collective-permute-start.23 = (f32[8,4,8,128]{3,2,1,0:T(8,128)S(1)}, f32[8,4,8,128]{3,2,1,0:T(8,128)S(1)}, u32[]{:S(2)}, u32[]{:S(2)}) collective-permute-start(f32[8,4,8,128]{3,2,1,0:T(8,128)S(1)} %copy-done.13), channel_id=1, source_target_pairs={{0,9},{1,8},{2,11},{3,10},{4,13},{5,12},{6,15},{7,14},{8,1},{9,0},... | collective-permute-start | bytes 393224 | tf_op jit(solution)/shard_map/ppermute | solution.py:557
  487.6 38.4 %collective-permute-start.24 = (f32[8,4,8,128]{3,2,1,0:T(8,128)S(1)}, f32[8,4,8,128]{3,2,1,0:T(8,128)S(1)}, u32[]{:S(2)}, u32[]{:S(2)}) collective-permute-start(f32[8,4,8,128]{3,2,1,0:T(8,128)S(1)} %copy-done.12), channel_id=1, source_target_pairs={{0,10},{1,11},{2,8},{3,9},{4,14},{5,15},{6,12},{7,13},{8,2},{9,3},... | collective-permute-start | bytes 393224 | tf_op jit(solution)/shard_map/ppermute | solution.py:557
  499.2 28.6 %collective-permute-start.25 = (f32[8,4,8,128]{3,2,1,0:T(8,128)S(1)}, f32[8,4,8,128]{3,2,1,0:T(8,128)S(1)}, u32[]{:S(2)}, u32[]{:S(2)}) collective-permute-start(f32[8,4,8,128]{3,2,1,0:T(8,128)S(1)} %copy-done.11), channel_id=1, source_target_pairs={{0,11},{1,10},{2,9},{3,8},{4,15},{5,14},{6,13},{7,12},{8,3},{9,2},... | collective-permute-start | bytes 393224 | tf_op jit(solution)/shard_map/ppermute | solution.py:557
  503.4 27.1 %collective-permute-start.26 = (f32[8,4,8,128]{3,2,1,0:T(8,128)S(1)}, f32[8,4,8,128]{3,2,1,0:T(8,128)S(1)}, u32[]{:S(2)}, u32[]{:S(2)}) collective-permute-start(f32[8,4,8,128]{3,2,1,0:T(8,128)S(1)} %copy-done.10), channel_id=1, source_target_pairs={{0,12},{1,13},{2,14},{3,15},{4,8},{5,9},{6,10},{7,11},{8,4},{9,5},... | collective-permute-start | bytes 393224 | tf_op jit(solution)/shard_map/ppermute | solution.py:557
  522.1 16.7 %collective-permute-start.28 = (f32[8,4,8,128]{3,2,1,0:T(8,128)S(1)}, f32[8,4,8,128]{3,2,1,0:T(8,128)S(1)}, u32[]{:S(2)}, u32[]{:S(2)}) collective-permute-start(f32[8,4,8,128]{3,2,1,0:T(8,128)S(1)} %copy-done.8), channel_id=1, source_target_pairs={{0,14},{1,15},{2,12},{3,13},{4,10},{5,11},{6,8},{7,9},{8,6},{9,7},... | collective-permute-start | bytes 393224 | tf_op jit(solution)/shard_map/ppermute | solution.py:557
  (28 other events, 454.1 us)

commit v5 on v4

--- a/solution.py
+++ b/solution.py
@@ -48,12 +48,24 @@
     return jnp.concatenate([x, x], axis=0)
 
 
-def cycle_factor(taps, cycle_start, phi_start):
+def half_rows(groups, upper):
+    first = lax.broadcasted_iota(jnp.int32, groups[0].shape, 0) < 4
+    merged = []
+    for at in range(0, len(groups), 2):
+        left, right = groups[at : at + 2]
+        lower = jnp.where(first, left, pltpu.roll(right, 4, 0))
+        merged.append(jnp.where(upper, jnp.where(first, pltpu.roll(left, 4, 0), right), lower))
+    return merged
+
+
+def cycle_factor(taps, cycle_start, phi_start, upper=None):
     first, second = shifted_window(taps, cycle_start & 7)
     block = cycle_start >> 3
     rows = []
     for h in range(TR // 8):
         rows.append(jnp.where(block == h, first, jnp.where(block == h - 1, second, 0.0)))
+    if upper is not None:
+        rows = half_rows(rows, upper)
     group = twice((phi_start >> 7).astype(f32)).astype(bf16)
     masks = [group == g for g in range(GROUPS)]
     zero = jnp.zeros(group.shape, bf16)
@@ -61,7 +73,7 @@
     for part in split(jnp.concatenate(rows, axis=0)):
         pieces = []
         for mask in masks:
-            pieces += [jnp.where(mask, part[at : at + 16], zero) for at in range(0, TR, 16)]
+            pieces += [jnp.where(mask, part[at : at + 16], zero) for at in range(0, part.shape[0], 16)]
         parts.append(jnp.concatenate(pieces, axis=0))
     return parts
 
@@ -134,20 +146,21 @@
     )(*points)
 
 
-def read_kernel(count, place_rows, begin, cycle_taps, phi_taps, cycle_start, phi_start, *rest):
-    tiles, (out, turn) = rest[:count], rest[-2:]
+def read_kernel(count, cycles, place_rows, begin, cycle_taps, phi_taps, cycle_start, phi_start, *rest):
+    tiles, so_far, (out, turn) = rest[:count], rest[count:-2], rest[-2:]
     n = cycle_start.shape[1]
+    upper = None if cycles == TR else begin[2] != 0
     for k in range(STEP_SLOTS):
         cycle_at = jnp.broadcast_to(cycle_start[k : k + 1, :], (8, n))
         phi_at = jnp.broadcast_to(phi_start[k : k + 1, :], (8, n))
-        right_high, right_low = cycle_factor(cycle_taps[k], cycle_at, phi_at)
+        right_high, right_low = cycle_factor(cycle_taps[k], cycle_at, phi_at, upper)
         for r, row in place_rows(begin, tiles, k):
-            turn[k, pl.ds(r * GROUPS, GROUPS), :] = row
+            turn[k, r * GROUPS : (r + 1) * GROUPS, :] = row
         pieces = [
-            turn[k, pl.ds(at * GROUPS + g, 8, stride=GROUPS), :] for g in range(GROUPS) for at in range(0, TR, 8)
+            turn[k, pl.ds(at * GROUPS + g, 8, stride=GROUPS), :] for g in range(GROUPS) for at in range(0, cycles, 8)
         ]
         tile = jnp.concatenate(pieces, axis=0).T
-        following = pltpu.roll(tile[:16], TR * (GROUPS - 1), 1)
+        following = pltpu.roll(tile[:16], cycles * (GROUPS - 1), 1)
         left_high, left_low = split(jnp.concatenate([tile, following], axis=0))
         left = jnp.concatenate([left_high, left_low, left_high], axis=1)
         right = jnp.concatenate([right_high, right_high, right_low], axis=0)
@@ -161,28 +174,31 @@
             here = block == h
             low = jnp.where(here, picked[h * 8 : h * 8 + 8], low)
             high = jnp.where(here, picked[h * 8 + 8 : h * 8 + 16], high)
-        out[k : k + 1, :] = jnp.sum(low * first + high * second, axis=0, keepdims=True)
-
-
-def read_points(points, begin, slots, tiles, tile_specs, place_rows, so_far):
+        result = jnp.sum(low * first + high * second, axis=0, keepdims=True)
+        if so_far and cycles < TR:
+            result = result + so_far[0][k : k + 1, :]
+        out[k : k + 1, :] = result
+
+
+def read_points(points, begin, slots, tiles, tile_specs, cycles, place_rows, so_far):
     total, n = points[0].shape
     given = [] if so_far is None else [so_far]
+    specs = point_specs(lambda i, at: at[0] + i, n)
+    given_spec = pl.BlockSpec(memory_space=pl.ANY) if cycles == TR else specs[0]
     return pl.pallas_call(
-        functools.partial(read_kernel, len(tile_specs), place_rows),
+        functools.partial(read_kernel, len(tile_specs), cycles, place_rows),
         grid_spec=pltpu.PrefetchScalarGridSpec(
             num_scalar_prefetch=1,
             grid=(slots // STEP_SLOTS,),
-            in_specs=point_specs(lambda i, at: at[0] + i, n)[1:]
-            + tile_specs
-            + [pl.BlockSpec(memory_space=pl.ANY)] * len(given),
-            out_specs=pl.BlockSpec((STEP_SLOTS, n), lambda i, at: (at[0] + i, 0)),
-            scratch_shapes=[pltpu.VMEM((STEP_SLOTS, TR * GROUPS, LANES), f32)],
+            in_specs=specs[1:] + tile_specs + [given_spec] * len(given),
+            out_specs=specs[0],
+            scratch_shapes=[pltpu.VMEM((STEP_SLOTS, cycles * GROUPS, LANES), f32)],
         ),
         out_shape=jax.ShapeDtypeStruct((total, n), f32),
         input_output_aliases={5 + len(tile_specs): 0} if given else {},
         compiler_params=pltpu.CompilerParams(vmem_limit_bytes=VMEM_LIMIT),
         cost_estimate=pl.CostEstimate(
-            flops=slots * 2 * 3 * 256 * 256 * n, bytes_accessed=slots * (19 + 32) * n * 4, transcendentals=0
+            flops=slots * 2 * 3 * 256 * 8 * cycles * n, bytes_accessed=slots * (19 + cycles) * n * 4, transcendentals=0
         ),
         name="read_back",
     )(begin, *points[1:], *tiles, *given)
@@ -225,12 +241,16 @@
     )(tile_list, *filtered)
 
 
+def outs_by_device(outs):
+    return [(out, share) for share in range(outs[0].shape[0]) for out in outs]
+
+
 def pick_own_kernel(place, tile_list, *refs):
     filtered, outs = refs[:2], refs[2:]
     columns, per_column = tile_list.shape[1:]
     first = filtered[0].shape[1]
 
-    for d, out in enumerate(outs):
+    for d, (out, share) in enumerate(outs_by_device(outs)):
         block = place[0] + (place[2] ^ d)
 
         def one(c, carry):
@@ -238,22 +258,23 @@
             for k in range(per_column):
                 j = tile_list[block, column, k]
                 inside, beyond = jnp.minimum(j, first - 1), jnp.maximum(j - first, 0)
-                out[c * per_column + k] = jnp.where(j < first, filtered[0][column, inside], filtered[1][column, beyond])
+                tile = jnp.where(j < first, filtered[0][column, inside], filtered[1][column, beyond])
+                out[share, c * per_column + k] = tile
             return carry
 
         lax.fori_loop(0, columns // 2, one, 0)
 
 
-def pick_own(filtered, place, tile_list):
+def pick_own(filtered, place, tile_list, part_count):
     blocks, columns, per_column = tile_list.shape
-    shape = (columns // 2 * per_column, 8, LANES)
+    shape = (blocks // 2 // part_count, columns // 2 * per_column, 8, LANES)
     return pl.pallas_call(
         pick_own_kernel,
         grid=(1,),
         in_specs=[pl.BlockSpec(memory_space=pltpu.SMEM)] * 2
         + [pl.BlockSpec(part.shape, lambda i: (0, 0, 0, 0)) for part in filtered],
-        out_specs=[pl.BlockSpec(shape, lambda i: (0, 0, 0))] * (blocks // 2),
-        out_shape=[jax.ShapeDtypeStruct(shape, f32)] * (blocks // 2),
+        out_specs=[pl.BlockSpec(shape, lambda i: (0, 0, 0, 0))] * part_count,
+        out_shape=[jax.ShapeDtypeStruct(shape, f32)] * part_count,
         compiler_params=pltpu.CompilerParams(vmem_limit_bytes=VMEM_LIMIT),
         cost_estimate=pl.CostEstimate(flops=0, bytes_accessed=10 * 2**20, transcendentals=0),
         name="pick_own",
@@ -264,9 +285,9 @@
     shares, outs = refs[:2], refs[2:]
     per_column = tile_list.shape[2]
     first = shares[0].shape[1]
-    rows = outs[0].shape[1]
-
-    for d, out in enumerate(outs):
+    rows = outs[0].shape[2]
+
+    for d, (out, share) in enumerate(outs_by_device(outs)):
         block = place[0] + (place[2] ^ d)
 
         def one(k, carry):
@@ -274,22 +295,22 @@
             inside, beyond = jnp.minimum(j, first - 1), jnp.maximum(j - first, 0)
             for row in range(rows):
                 at = place[3] + row
-                out[k, row] = jnp.where(j < first, shares[0][at, inside], shares[1][at, beyond])
+                out[share, k, row] = jnp.where(j < first, shares[0][at, inside], shares[1][at, beyond])
             return carry
 
         lax.fori_loop(0, per_column, one, 0)
 
 
-def pick_near(shares, place, tile_list):
+def pick_near(shares, place, tile_list, part_count):
     blocks, columns, per_column = tile_list.shape
-    shape = (per_column, shares[0].shape[0] // 2, 8, LANES)
+    shape = (blocks // 2 // part_count, per_column, shares[0].shape[0] // 2, 8, LANES)
     return pl.pallas_call(
         pick_near_kernel,
         grid=(1,),
         in_specs=[pl.BlockSpec(memory_space=pltpu.SMEM)] * 2
         + [pl.BlockSpec(part.shape, lambda i: (0, 0, 0, 0)) for part in shares],
-        out_specs=[pl.BlockSpec(shape, lambda i: (0, 0, 0, 0))] * (blocks // 2),
-        out_shape=[jax.ShapeDtypeStruct(shape, f32)] * (blocks // 2),
+        out_specs=[pl.BlockSpec(shape, lambda i: (0, 0, 0, 0, 0))] * part_count,
+        out_shape=[jax.ShapeDtypeStruct(shape, f32)] * part_count,
         compiler_params=pltpu.CompilerParams(vmem_limit_bytes=VMEM_LIMIT),
         cost_estimate=pl.CostEstimate(flops=0, bytes_accessed=12 * 2**20, transcendentals=0),
         name="pick_near",
@@ -438,6 +459,7 @@
 
 
 COLLECT_STEP = 4
+COLLECT_BATCH = 32
 
 
 def collect_kernel(chunks, tile_list, *refs):
@@ -461,12 +483,14 @@
     def _():
         for d in range(COLLECT_STEP):
             for ref, begin in zip(arrived, chunks):
-                for c in range(ref.shape[1] // per_column):
-                    q = begin // per_column + c
-                    owners = [tile_list[step * COLLECT_STEP + d, q, k] for k in range(per_column)]
-                    sums = [total[owners[k], q] + ref[d, c * per_column + k] for k in range(per_column)]
-                    for k in range(per_column):
-                        total[owners[k], q] = sums[k]
+                for c in range(0, ref.shape[1], COLLECT_BATCH):
+                    where = []
+                    for slot in range(begin + c, min(begin + c + COLLECT_BATCH, begin + ref.shape[1])):
+                        q, k = slot // per_column, slot % per_column
+                        where.append((tile_list[step * COLLECT_STEP + d, q, k], q))
+                    sums = [total[j, q] + ref[d, c + at] for at, (j, q) in enumerate(where)]
+                    for (j, q), x in zip(where, sums):
+                        total[j, q] = x
 
     hand_over = pltpu.make_async_copy(total.at[pl.ds(first, others.shape[0])], others, sem)
 
@@ -552,17 +576,20 @@
     late = filter_cycles(others, tables)
 
     def pass_on(parts):
-        moved = [parts[0]]
-        for d in range(1, blocks // 2):
-            moved.append(lax.ppermute(parts[d], AXES[1:], [(i, i ^ d) for i in range(blocks // 2)]))
-        return moved
+        def step(x, axis, size, d):
+            return lax.ppermute(x, axis, [(i, i ^ d) for i in range(size)]) if d else x
+
+        here = [step(x, AXES[2], part_count, d) for d, x in enumerate(parts)]
+        return [
+            step(jnp.stack([x[d] for x in here]), AXES[1], shares, d) for d in range(shares)
+        ]
 
     early_share = exchange(early, AXES[:2])
     far = pick_far([early, late], tile_list)
     late_share = exchange(after(late, early_share), AXES[:2])
-    own = pass_on(pick_own([after(early, far), late], place, tile_list))
+    own = pass_on(pick_own([after(early, far), late], place, tile_list, part_count))
     far_tiles = exchange(after(far, late_share, *own[1:]), AXES)
-    near = pass_on(pick_near([early_share, late_share], place, tile_list))
+    near = pass_on(pick_near([early_share, late_share], place, tile_list, part_count))
 
     far_tiles = far_tiles.reshape(columns, part_count, near_slots, 8, LANES)
     far_spec = pl.BlockSpec((columns, part_count, STEP_SLOTS, 8, LANES), lambda i, at: (0, 0, i, 0, 0))
@@ -570,23 +597,36 @@
     def far_rows(begin, tiles, k):
         return [(r, tiles[0][r % columns, r // columns, k]) for r in range(TR)]
 
-    def near_rows(begin, tiles, k):
+    def own_rows(begin, tiles, k):
         step = pl.program_id(0)
         for t in range(part_count):
             for p in range(shares):
                 source = begin[1] ^ (p * part_count + t)
-                yield t * columns + begin[0] + p, tiles[0][source, step * STEP_SLOTS + k]
-                source = begin[1] ^ (step * part_count + t)
-                yield t * columns + (shares - begin[0]) + p, tiles[1][source, k, p]
-
-    begin = jnp.stack([(1 - half) * shares, index]).astype(jnp.int32)
-    gradient = read_points(points, begin, near_slots, [far_tiles], [far_spec], far_rows, None)
-    near_tiles = [jnp.stack(own), jnp.stack(near)]
-    near_specs = [
-        pl.BlockSpec(x.shape, functools.partial(lambda nd, i, at: (0,) * nd, x.ndim)) for x in near_tiles
-    ]
-    begin = jnp.stack([half * shares, index]).astype(jnp.int32)
-    gradient = read_points(points, begin, near_slots, near_tiles, near_specs, near_rows, gradient)
+                yield t * shares + p, tiles[0][source, step * STEP_SLOTS + k]
+
+    def near_rows(begin, tiles, k):
+        apart = begin[1] // part_count ^ pl.program_id(0)
+        for t in range(part_count):
+            source = begin[1] % part_count ^ t
+            for p in range(shares):
+                row = tiles[0][source, k, p]
+                for d in range(1, shares):
+                    row = jnp.where(apart == d, tiles[d][source, k, p], row)
+                yield t * shares + p, row
+
+    def whole_specs_at(arrays):
+        return [pl.BlockSpec(x.shape, functools.partial(lambda nd, i, at: (0,) * nd, x.ndim)) for x in arrays]
+
+    def begin_at(which, upper):
+        return jnp.stack([which * shares, index, upper]).astype(jnp.int32)
+
+    own = [jnp.concatenate(own)]
+    gradient = read_points(points, begin_at(half, half), near_slots, own, whole_specs_at(own), TR // 2, own_rows, None)
+    gradient = read_points(points, begin_at(1 - half, half), near_slots, [far_tiles], [far_spec], TR, far_rows, gradient)
+    near = [after(x, gradient) for x in near]
+    gradient = read_points(
+        points, begin_at(half, 1 - half), near_slots, near, whole_specs_at(near), TR // 2, near_rows, gradient
+    )
     whole = merge_rows(early_share, 0, cycle_blocks, None)
     whole = merge_rows(late_share, FILTER_FIRST, cycle_blocks, whole)
     return whole, gradient[None]

time: 571 us -> 554 us (0.970)
  starting transfers between devices: 97.8 us -> 43.5 us
  waiting for transfers between devices: 322 us -> 352 us
  Pallas kernels: 131 us -> 141 us
    ppermute x30 -> x12, starting transfers between devices: 59.8 us -> 11.2 us  [step(): return lax.ppermute(x, axis, [(i, i ^ d) for i in range(size)]) if d else x]
    all_to_all x5, waiting for transfers between devices: 169 us -> 213 us  [exchange(): return lax.all_to_all(x, axes, 0, 0, tiled=True)]
    ppermute x30 -> x12, waiting for transfers between devices: 153 us -> 138 us  [step(): return lax.ppermute(x, axis, [(i, i ^ d) for i in range(size)]) if d else x]
    pallas_call x2 -> x3, Pallas kernels: 26.6 us -> 37.1 us  [read_points(): pl.pallas_call(functools.partial(read_kernel, len(tile_specs), cycles, pl...]
    unnamed x67 -> x27, local copies, waits for them, and re-layouts: 13 us -> 10.3 us
  transfers between devices with their start and end apart: 35 -> 17, of which waited for: 18 -> 11; matrix products, arithmetic and copies ran while one was open for 3% -> 2% of each run, Pallas kernels for 15% -> 20%
where the time goes in v5:
time: 554 us; the launch traced here: 553 us
  waiting for transfers between devices  352 us (64%)
  Pallas kernels  141 us (25%)
  starting transfers between devices  43.5 us (8%)
  local copies, waits for them, and re-layouts  12.1 us (2%)
    all_to_all x5, waiting for transfers between devices, exchange(): return lax.all_to_all(x, axes, 0, 0, tiled=True)  213 us
    ppermute x12, waiting for transfers between devices, step(): return lax.ppermute(x, axis, [(i, i ^ d) for i in range(size)]) if d else x  138 us
    pallas_call x3, Pallas kernels, read_points(): pl.pallas_call(functools.partial(read_kernel, len(tile_specs), cycles, pl...  37.1 us
    pallas_call x2, Pallas kernels, spread_tiles(): pl.pallas_call(spread_kernel, grid=(slots // STEP_SLOTS,), in_specs=point...  34.6 us
    all_to_all x5, starting transfers between devices, exchange(): return lax.all_to_all(x, axes, 0, 0, tiled=True)  32.3 us
    pallas_call x1, Pallas kernels, filter_cycles(): pl.pallas_call(filter_kernel, grid=(blocks // FILTER_STEP,), in_specs=who...  18.2 us
    pallas_call x1, Pallas kernels, collect_and_filter(): pl.pallas_call(functools.partial(collect_kernel, chunks), grid=(collectin...  14 us
    pallas_call x2, Pallas kernels, merge_rows(): pl.pallas_call(merge_kernel, grid=(blocks // step,), in_specs=[pl.BlockSp...  13 us
  transfers between devices with their start and end apart: 17, of which 11 were waited for; matrix products, arithmetic and copies ran while one was open for 2% of the time, Pallas kernels for 20%

profile of v5, /device:TPU:0, one launch (start us, length us, event | category | flops | bytes accessed | tf_op | source)
XLA Modules:
  0.0 553.4 jit_solution(4473762355818322077)
XLA Ops:
  6.5 7.3 %all-to-all-start = ((f32[32,8,8,128]{3,2,1,0:T(8,128)}), f32[32,8,8,128]{3,2,1,0:T(8,128)S(1)}, u32[]{:S(2)}, u32[]{:S(2)}) async-start(f32[32,8,8,128]{3,2,1,0:T(8,128)} %bitcast.19), calls=%async_computation | async-start | bytes 2097152 | tf_op jit(solution)/shard_map/all_to_all | solution.py:567
  13.8 28.8 %spread.3 = f32[8,4,1,56,8,128]{5,4,3,2,1,0:T(8,128)} custom-call(f32[64,1024]{1,0:T(8,128)} %bitcast.33, f32[64,8,1024]{2,1,0:T(8,128)} %bitcast.23, f32[64,8,1024]{2,1,0:T(8,128)} %bitcast.28, s32[64,1024]{1,0:T(8,128)} %bitcast.35, s32[64,1024]{1,0:T(8,128)} %bitcast.40), custom_call_target="tpu_custom_call" | custom-call | flops 22548578304 | bytes 11698176 | tf_op jit(solution)/shard_map/spread/pallas_call | solution.py:134
  43.6 5.9 %all-to-all-start.1 = ((f32[32,56,8,128]{3,2,1,0:T(8,128)}), f32[32,56,8,128]{3,2,1,0:T(8,128)}, u32[]{:S(2)}, u32[]{:S(2)}) async-start(f32[32,56,8,128]{3,2,1,0:T(8,128)} %bitcast.18), calls=%async_computation.1 | async-start | bytes 14680064 | tf_op jit(solution)/shard_map/all_to_all | solution.py:567
  51.5 161.2 %all-to-all-done.1.refs_1_ = f32[32,56,8,128]{3,2,1,0:T(8,128)} async-done(((f32[32,56,8,128]{3,2,1,0:T(8,128)}), f32[32,56,8,128]{3,2,1,0:T(8,128)}, u32[]{:S(2)}, u32[]{:S(2)}) %all-to-all-start.1) | async-done | bytes 7340064 | tf_op jit(solution)/shard_map/all_to_all | solution.py:567
  212.7 14.0 %collect_filter.1 = (f32[8,32,8,128]{3,2,1,0:T(8,128)}, f32[224,8,8,128]{3,2,1,0:T(8,128)}) custom-call(s32[32,8,8]{2,1,0:T(8,128)} %copy.23.tile_list, f32[32,8,8,128]{3,2,1,0:T(8,128)} %copy-done.1, f32[32,56,8,128]{3,2,1,0:T(8,128)} %all-to-all-done.1.refs_1_, bf16[128,384]{1,0:T(8,128)(2,1)} %constant.33.clone.refs_2_.refs_0_, ...), custom_call_target="tpu_custom_call" | custom-call | flops 3623878656 | bytes 6291456 | tf_op jit(solution)/shard_map/collect_filter/pallas_call | solution.py:514
  230.2 18.2 %filter_cycles.1.refs_1_ = f32[8,224,8,128]{3,2,1,0:T(8,128)} custom-call(bf16[128,384]{1,0:T(8,128)(2,1)} %constant.33.clone.refs_2_.refs_0_, bf16[128,384]{1,0:T(8,128)(2,1)} %constant.34.clone.refs_3_.refs_1_, bf16[768,256]{1,0:T(8,128)(2,1)} %constant.35.clone.refs_4_.refs_2_, bf16[768,256]{1,0:T(8,128)(2,1)} %constant.36.clone.refs_5_.refs_3_, ...), custom_call_target="tpu_custom_call" | custom-call | flops 8455716864 | bytes 14680064 | tf_op jit(solution)/shard_map/filter_cycles/pallas_call | solution.py:449
  248.4 7.6 %all-to-all-done.2.arrived.refs_0_ = f32[8,32,8,128]{3,2,1,0:T(8,128)S(1)} async-done(((f32[8,32,8,128]{3,2,1,0:T(8,128)}), f32[8,32,8,128]{3,2,1,0:T(8,128)S(1)}, u32[]{:S(2)}, u32[]{:S(2)}) %all-to-all-start.2) | async-done | bytes 1048608 | tf_op jit(solution)/shard_map/all_to_all | solution.py:567
  262.7 9.9 %pick_far.1 = f32[32,32,8,128]{3,2,1,0:T(8,128)} custom-call(s32[32,8,8]{2,1,0:T(8,128)} %copy.23.tile_list, f32[8,32,8,128]{3,2,1,0:T(8,128)} %get-tuple-element.26.refs_0_, f32[8,224,8,128]{3,2,1,0:T(8,128)} %filter_cycles.1.refs_1_), custom_call_target="tpu_custom_call" | custom-call | bytes 12582912 | tf_op jit(solution)/shard_map/pick_far/pallas_call | solution.py:231
  272.5 7.7 %pick_own.1 = (f32[4,32,8,128]{3,2,1,0:T(8,128)}, f32[4,32,8,128]{3,2,1,0:T(8,128)}, f32[4,32,8,128]{3,2,1,0:T(8,128)}, f32[4,32,8,128]{3,2,1,0:T(8,128)}) custom-call(s32[5]{0:T(128)} %stack.68.place, s32[32,8,8]{2,1,0:T(8,128)} %copy.23.tile_list, f32[8,32,8,128]{3,2,1,0:T(8,128)} %get-tuple-element.26.refs_0_, f32[8,224,8,128]{3,2,1,0:T(8,128)} %filter_cycles.1.refs_1_), custom_call_target="tpu_custom_call" | custom-call | bytes 10485760 | tf_op jit(solution)/shard_map/pick_own/pallas_call | solution.py:271
  284.5 10.6 %collective-permute-done.4 = f32[4,32,8,128]{3,2,1,0:T(8,128)S(1)} collective-permute-done((f32[4,32,8,128]{3,2,1,0:T(8,128)}, f32[4,32,8,128]{3,2,1,0:T(8,128)S(1)}, u32[]{:S(2)}, u32[]{:S(2)}) %collective-permute-start.4) | collective-permute-done | bytes 524320 | tf_op jit(solution)/shard_map/ppermute | solution.py:580
  295.8 9.8 %collective-permute-done.5 = f32[4,32,8,128]{3,2,1,0:T(8,128)S(1)} collective-permute-done((f32[4,32,8,128]{3,2,1,0:T(8,128)}, f32[4,32,8,128]{3,2,1,0:T(8,128)S(1)}, u32[]{:S(2)}, u32[]{:S(2)}) %collective-permute-start.5) | collective-permute-done | bytes 524320 | tf_op jit(solution)/shard_map/ppermute | solution.py:580
  310.1 23.2 %collective-permute-done.6 = f32[4,32,8,128]{3,2,1,0:T(8,128)S(1)} collective-permute-done((f32[4,32,8,128]{3,2,1,0:T(8,128)S(1)}, f32[4,32,8,128]{3,2,1,0:T(8,128)S(1)}, u32[]{:S(2)}, u32[]{:S(2)}) %collective-permute-start.6) | collective-permute-done | bytes 524320 | tf_op jit(solution)/shard_map/ppermute | solution.py:580
  333.2 59.9 %collective-permute-done.7 = f32[4,32,8,128]{3,2,1,0:T(8,128)S(1)} collective-permute-done((f32[4,32,8,128]{3,2,1,0:T(8,128)S(1)}, f32[4,32,8,128]{3,2,1,0:T(8,128)S(1)}, u32[]{:S(2)}, u32[]{:S(2)}) %collective-permute-start.7) | collective-permute-done | bytes 524320 | tf_op jit(solution)/shard_map/ppermute | solution.py:580
  393.1 9.3 %collective-permute-done.8 = f32[4,32,8,128]{3,2,1,0:T(8,128)S(1)} collective-permute-done((f32[4,32,8,128]{3,2,1,0:T(8,128)S(1)}, f32[4,32,8,128]{3,2,1,0:T(8,128)S(1)}, u32[]{:S(2)}, u32[]{:S(2)}) %collective-permute-start.8) | collective-permute-done | bytes 524320 | tf_op jit(solution)/shard_map/ppermute | solution.py:580
  402.4 19.2 %all-to-all-done.3.arrived.refs_1_ = f32[8,224,8,128]{3,2,1,0:T(8,128)} async-done(((f32[8,224,8,128]{3,2,1,0:T(8,128)}), f32[8,224,8,128]{3,2,1,0:T(8,128)}, u32[]{:S(2)}, u32[]{:S(2)}) %all-to-all-start.3) | async-done | bytes 7340064 | tf_op jit(solution)/shard_map/all_to_all | solution.py:567
  421.7 10.4 %all-to-all-start.4 = ((f32[32,32,8,128]{3,2,1,0:T(8,128)}), f32[32,32,8,128]{3,2,1,0:T(8,128)}, u32[]{:S(2)}, u32[]{:S(2)}) async-start(f32[32,32,8,128]{3,2,1,0:T(8,128)} %pick_far.1), calls=%async_computation.4 | async-start | bytes 8388608 | tf_op jit(solution)/shard_map/all_to_all | solution.py:567
  436.5 7.0 %pick_near.1 = (f32[4,8,4,8,128]{4,3,2,1,0:T(8,128)}, f32[4,8,4,8,128]{4,3,2,1,0:T(8,128)}, f32[4,8,4,8,128]{4,3,2,1,0:T(8,128)}, f32[4,8,4,8,128]{4,3,2,1,0:T(8,128)}) custom-call(s32[5]{0:T(128)} %stack.68.place, s32[32,8,8]{2,1,0:T(8,128)} %copy.23.tile_list, f32[8,32,8,128]{3,2,1,0:T(8,128)} %copy-done, f32[8,224,8,128]{3,2,1,0:T(8,128)} %all-to-all-done.3.arrived.refs_1_), custom_call_target="tpu_custom_call" | custom-call | bytes 12582912 | tf_op jit(solution)/shard_map/pick_near/pallas_call | solution.py:307
  445.4 12.0 %read_back.3.rest_1_ = f32[64,1024]{1,0:T(8,128)} custom-call(s32[3]{0:T(128)} %pad_add_fusion.2.begin, f32[64,8,1024]{2,1,0:T(8,128)} %bitcast.24, f32[64,8,1024]{2,1,0:T(8,128)} %bitcast.29, s32[64,1024]{1,0:T(8,128)} %bitcast.36, s32[64,1024]{1,0:T(8,128)} %bitcast.41, f32[16,32,8,128]{3,2,1,0:T(8,128)} %constant_dynamic-update-slice_fusion.rest_0_), custom_call_target="tpu_custom_call" | custom-call | flops 6442450944 | bytes 4587520 | tf_op jit(solution)/shard_map/read_back/pallas_call | solution.py:188
  460.3 10.1 %merge_rows.3 = f32[256,8,1024]{2,1,0:T(8,128)} custom-call(f32[8,224,8,128]{3,2,1,0:T(8,128)} %all-to-all-done.3.arrived.refs_1_, f32[256,8,1024]{2,1,0:T(8,128)} %merge_rows.2.rest_0_), custom_call_target="tpu_custom_call", output_to_operand_aliasing={{}: (1, {})} | custom-call | bytes 14680064 | tf_op jit(solution)/shard_map/merge_rows/pallas_call | solution.py:333
  470.4 12.6 %collective-permute-done.1 = f32[4,8,4,8,128]{4,3,2,1,0:T(8,128)S(1)} collective-permute-done((f32[4,8,4,8,128]{4,3,2,1,0:T(8,128)}, f32[4,8,4,8,128]{4,3,2,1,0:T(8,128)S(1)}, u32[]{:S(2)}, u32[]{:S(2)}) %collective-permute-start.1) | collective-permute-done | bytes 524320 | tf_op jit(solution)/shard_map/ppermute | solution.py:580
  483.1 13.0 %collective-permute-done.2 = f32[4,8,4,8,128]{4,3,2,1,0:T(8,128)S(1)} collective-permute-done((f32[4,8,4,8,128]{4,3,2,1,0:T(8,128)S(1)}, f32[4,8,4,8,128]{4,3,2,1,0:T(8,128)S(1)}, u32[]{:S(2)}, u32[]{:S(2)}) %collective-permute-start.2) | collective-permute-done | bytes 524320 | tf_op jit(solution)/shard_map/ppermute | solution.py:580
  501.0 25.4 %all-to-all-done.4 = f32[32,32,8,128]{3,2,1,0:T(8,128)} async-done(((f32[32,32,8,128]{3,2,1,0:T(8,128)}), f32[32,32,8,128]{3,2,1,0:T(8,128)}, u32[]{:S(2)}, u32[]{:S(2)}) %all-to-all-start.4) | async-done | bytes 4194336 | tf_op jit(solution)/shard_map/all_to_all | solution.py:567
  526.4 12.7 %read_back.4.rest_4_ = f32[64,1024]{1,0:T(8,128)} custom-call(s32[3]{0:T(128)} %add_add_fusion.begin, f32[64,8,1024]{2,1,0:T(8,128)} %bitcast.25, f32[64,8,1024]{2,1,0:T(8,128)} %bitcast.30, s32[64,1024]{1,0:T(8,128)} %bitcast.37, s32[64,1024]{1,0:T(8,128)} %bitcast.42, f32[8,4,32,8,128]{4,3,2,1,0:T(8,128)} %bitcast.15.rest_0_, ...), custom_call_target="tpu_custom_call", output_to_operand_aliasing={{}: (6, {})} | custom-call | flops 12884901888 | bytes 6684672 | tf_op jit(solution)/shard_map/read_back/pallas_call | solution.py:188
  540.9 12.5 %read_back.5 = f32[64,1024]{1,0:T(8,128)} custom-call(s32[3]{0:T(128)} %pad_add_fusion.begin, f32[64,8,1024]{2,1,0:T(8,128)} %bitcast.26, f32[64,8,1024]{2,1,0:T(8,128)} %bitcast.31, s32[64,1024]{1,0:T(8,128)} %bitcast.38, s32[64,1024]{1,0:T(8,128)} %bitcast.43, f32[4,8,4,8,128]{4,3,2,1,0:T(8,128)} %pad_maximum_fusion.rest_0_, ...), custom_call_target="tpu_custom_call", output_to_operand_aliasing={{}: (9, {})} | custom-call | flops 6442450944 | bytes 4587520 | tf_op jit(solution)/shard_map/read_back/pallas_call | solution.py:188
  (70 shorter events, 44.3 us)
Async XLA Ops:
  6.5 36.1 %all-to-all-start = ((f32[32,8,8,128]{3,2,1,0:T(8,128)}), f32[32,8,8,128]{3,2,1,0:T(8,128)S(1)}, u32[]{:S(2)}, u32[]{:S(2)}) async-start(f32[32,8,8,128]{3,2,1,0:T(8,128)} %bitcast.19), calls=%async_computation | async-start | bytes 2097152 | tf_op jit(solution)/shard_map/all_to_all | solution.py:567
  42.5 1.1 copy-start.1
  42.5 7.0 %copy-start.3 = (f32[4097]{0:T(1024)S(1)}, f32[4097]{0:T(1024)}, u32[]{:S(2)}) copy-start(f32[4097]{0:T(1024)} %param.19) | copy-start | bytes 49168
  42.6 7.5 %copy-start.4 = (s32[32,8,8]{0,2,1:T(8,128)S(1)}, s32[32,8,8]{0,2,1:T(8,128)}, u32[]{:S(2)}) copy-start(s32[32,8,8]{0,2,1:T(8,128)} %param.18) | copy-start | bytes 24580
  43.6 169.1 %all-to-all-start.1 = ((f32[32,56,8,128]{3,2,1,0:T(8,128)}), f32[32,56,8,128]{3,2,1,0:T(8,128)}, u32[]{:S(2)}, u32[]{:S(2)}) async-start(f32[32,56,8,128]{3,2,1,0:T(8,128)} %bitcast.18), calls=%async_computation.1 | async-start | bytes 14680064 | tf_op jit(solution)/shard_map/all_to_all | solution.py:567
  226.7 29.3 %all-to-all-start.2 = ((f32[8,32,8,128]{3,2,1,0:T(8,128)}), f32[8,32,8,128]{3,2,1,0:T(8,128)S(1)}, u32[]{:S(2)}, u32[]{:S(2)}) async-start(f32[8,32,8,128]{3,2,1,0:T(8,128)} %get-tuple-element.26.refs_0_), calls=%async_computation.2 | async-start | bytes 2097152 | tf_op jit(solution)/shard_map/all_to_all | solution.py:567
  256.0 1.0 copy-start
  257.0 164.7 %all-to-all-start.3 = ((f32[8,224,8,128]{3,2,1,0:T(8,128)}), f32[8,224,8,128]{3,2,1,0:T(8,128)}, u32[]{:S(2)}, u32[]{:S(2)}) async-start(f32[8,224,8,128]{3,2,1,0:T(8,128)} %filter_cycles.1.refs_1_), calls=%async_computation.3 | async-start | bytes 14680064 | tf_op jit(solution)/shard_map/all_to_all | solution.py:567
  280.2 3.6 collective-permute-start.3
  280.2 14.9 %collective-permute-start.4 = (f32[4,32,8,128]{3,2,1,0:T(8,128)}, f32[4,32,8,128]{3,2,1,0:T(8,128)S(1)}, u32[]{:S(2)}, u32[]{:S(2)}) collective-permute-start(f32[4,32,8,128]{3,2,1,0:T(8,128)} %get-tuple-element.29), channel_id=1, source_target_pairs={{0,2},{1,3},{2,0},{3,1},{4,6},{5,7},{6,4},{7,5},{8,10},{9,11},{10,... | collective-permute-start | bytes 1572872 | tf_op jit(solution)/shard_map/ppermute | solution.py:580
  280.4 25.2 %collective-permute-start.5 = (f32[4,32,8,128]{3,2,1,0:T(8,128)}, f32[4,32,8,128]{3,2,1,0:T(8,128)S(1)}, u32[]{:S(2)}, u32[]{:S(2)}) collective-permute-start(f32[4,32,8,128]{3,2,1,0:T(8,128)} %get-tuple-element.30), channel_id=1, source_target_pairs={{0,3},{1,2},{2,1},{3,0},{4,7},{5,6},{6,5},{7,4},{8,11},{9,10},{10,... | collective-permute-start | bytes 1572872 | tf_op jit(solution)/shard_map/ppermute | solution.py:580
  306.3 26.9 %collective-permute-start.6 = (f32[4,32,8,128]{3,2,1,0:T(8,128)S(1)}, f32[4,32,8,128]{3,2,1,0:T(8,128)S(1)}, u32[]{:S(2)}, u32[]{:S(2)}) collective-permute-start(f32[4,32,8,128]{3,2,1,0:T(8,128)S(1)} %pad_maximum_fusion.1), channel_id=1, source_target_pairs={{0,4},{4,0},{8,12},{12,8},{1,5},{5,1},{9,13},{13,9},{2,6},{6,2},{1... | collective-permute-start | bytes 1572872 | tf_op jit(solution)/shard_map/ppermute | solution.py:580
  308.1 85.0 %collective-permute-start.7 = (f32[4,32,8,128]{3,2,1,0:T(8,128)S(1)}, f32[4,32,8,128]{3,2,1,0:T(8,128)S(1)}, u32[]{:S(2)}, u32[]{:S(2)}) collective-permute-start(f32[4,32,8,128]{3,2,1,0:T(8,128)S(1)} %pad_maximum_fusion.2), channel_id=1, source_target_pairs={{0,8},{4,12},{8,0},{12,4},{1,9},{5,13},{9,1},{13,5},{2,10},{6,14},... | collective-permute-start | bytes 1572872 | tf_op jit(solution)/shard_map/ppermute | solution.py:580
  309.7 92.7 %collective-permute-start.8 = (f32[4,32,8,128]{3,2,1,0:T(8,128)S(1)}, f32[4,32,8,128]{3,2,1,0:T(8,128)S(1)}, u32[]{:S(2)}, u32[]{:S(2)}) collective-permute-start(f32[4,32,8,128]{3,2,1,0:T(8,128)S(1)} %pad_maximum_fusion.3), channel_id=1, source_target_pairs={{0,12},{4,8},{8,4},{12,0},{1,13},{5,9},{9,5},{13,1},{2,14},{6,10},... | collective-permute-start | bytes 1572872 | tf_op jit(solution)/shard_map/ppermute | solution.py:580
  421.7 104.8 %all-to-all-start.4 = ((f32[32,32,8,128]{3,2,1,0:T(8,128)}), f32[32,32,8,128]{3,2,1,0:T(8,128)}, u32[]{:S(2)}, u32[]{:S(2)}) async-start(f32[32,32,8,128]{3,2,1,0:T(8,128)} %pick_far.1), calls=%async_computation.4 | async-start | bytes 8388608 | tf_op jit(solution)/shard_map/all_to_all | solution.py:567
  443.5 26.9 %collective-permute-start = (f32[4,8,4,8,128]{4,3,2,1,0:T(8,128)}, f32[4,8,4,8,128]{4,3,2,1,0:T(8,128)S(1)}, u32[]{:S(2)}, u32[]{:S(2)}) collective-permute-start(f32[4,8,4,8,128]{4,3,2,1,0:T(8,128)} %get-tuple-element.23), channel_id=1, source_target_pairs={{0,1},{1,0},{2,3},{3,2},{4,5},{5,4},{6,7},{7,6},{8,9},{9,8},{10,11... | collective-permute-start | bytes 1572872 | tf_op jit(solution)/shard_map/ppermute | solution.py:580
  443.7 39.4 %collective-permute-start.1 = (f32[4,8,4,8,128]{4,3,2,1,0:T(8,128)}, f32[4,8,4,8,128]{4,3,2,1,0:T(8,128)S(1)}, u32[]{:S(2)}, u32[]{:S(2)}) collective-permute-start(f32[4,8,4,8,128]{4,3,2,1,0:T(8,128)} %get-tuple-element.24), channel_id=1, source_target_pairs={{0,2},{1,3},{2,0},{3,1},{4,6},{5,7},{6,4},{7,5},{8,10},{9,11},{10,... | collective-permute-start | bytes 1572872 | tf_op jit(solution)/shard_map/ppermute | solution.py:580
  457.4 2.9 copy-start.6
  457.4 2.9 copy-start.2
  460.2 35.9 %collective-permute-start.2 = (f32[4,8,4,8,128]{4,3,2,1,0:T(8,128)S(1)}, f32[4,8,4,8,128]{4,3,2,1,0:T(8,128)S(1)}, u32[]{:S(2)}, u32[]{:S(2)}) collective-permute-start(f32[4,8,4,8,128]{4,3,2,1,0:T(8,128)S(1)} %copy-done.6), channel_id=1, source_target_pairs={{0,3},{1,2},{2,1},{3,0},{4,7},{5,6},{6,5},{7,4},{8,11},{9,10},{10,... | collective-permute-start | bytes 1572872 | tf_op jit(solution)/shard_map/ppermute | solution.py:580
  496.2 42.9 %collective-permute-start.9 = (f32[4,8,4,8,128]{4,3,2,1,0:T(8,128)S(1)}, f32[4,8,4,8,128]{4,3,2,1,0:T(8,128)S(1)}, u32[]{:S(2)}, u32[]{:S(2)}) collective-permute-start(f32[4,8,4,8,128]{4,3,2,1,0:T(8,128)S(1)} %pad_maximum_fusion.4), channel_id=1, source_target_pairs={{0,4},{4,0},{8,12},{12,8},{1,5},{5,1},{9,13},{13,9},{2,6},{6,2},{1... | collective-permute-start | bytes 1572872 | tf_op jit(solution)/shard_map/ppermute | solution.py:580
  496.8 42.4 %collective-permute-start.10 = (f32[4,8,4,8,128]{4,3,2,1,0:T(8,128)S(1)}, f32[4,8,4,8,128]{4,3,2,1,0:T(8,128)S(1)}, u32[]{:S(2)}, u32[]{:S(2)}) collective-permute-start(f32[4,8,4,8,128]{4,3,2,1,0:T(8,128)S(1)} %pad_maximum_fusion.5), channel_id=1, source_target_pairs={{0,8},{4,12},{8,0},{12,4},{1,9},{5,13},{9,1},{13,5},{2,10},{6,14},... | collective-permute-start | bytes 1572872 | tf_op jit(solution)/shard_map/ppermute | solution.py:580
  499.7 39.5 %collective-permute-start.11 = (f32[4,8,4,8,128]{4,3,2,1,0:T(8,128)S(1)}, f32[4,8,4,8,128]{4,3,2,1,0:T(8,128)S(1)}, u32[]{:S(2)}, u32[]{:S(2)}) collective-permute-start(f32[4,8,4,8,128]{4,3,2,1,0:T(8,128)S(1)} %pad_maximum_fusion.6), channel_id=1, source_target_pairs={{0,12},{4,8},{8,4},{12,0},{1,13},{5,9},{9,5},{13,1},{2,14},{6,10},... | collective-permute-start | bytes 1572872 | tf_op jit(solution)/shard_map/ppermute | solution.py:580
  539.2 1.0 copy-start.7
  (2 other events, 1.6 us)

commit v6 on v5

--- a/solution.py
+++ b/solution.py
@@ -97,6 +97,10 @@
     return parts
 
 
+def rows_dot(lhs, rhs):
+    return lax.dot_general(lhs, rhs, (((1,), (1,)), ((), ())), preferred_element_type=f32)
+
+
 def spread_kernel(values, cycle_taps, phi_taps, cycle_start, phi_start, out, turn):
     n = values.shape[1]
     shares, parts, rows = out.shape[:3]
@@ -107,9 +111,8 @@
         left_high, left_low = cycle_factor(loaded, cycle_at, phi_at)
         empty = jnp.zeros((256 - 144, n), bf16)
         right_high, right_low = [jnp.concatenate([x, empty], axis=0) for x in phi_factor(phi_taps[k], phi_at)]
-        left = jnp.concatenate([left_high, left_high, left_low], axis=1)
-        right = jnp.concatenate([right_high, right_low, right_high], axis=1)
-        product = lax.dot_general(left, right, (((1,), (1,)), ((), ())), preferred_element_type=f32)
+        product = rows_dot(jnp.concatenate([left_high, left_low], axis=0), right_high)
+        product = product[: TR * GROUPS] + product[TR * GROUPS :] + rows_dot(left_high, right_low)
         for g in range(GROUPS):
             tile = product[g * TR : (g + 1) * TR, :LANES]
             if g:
@@ -162,9 +165,7 @@
         tile = jnp.concatenate(pieces, axis=0).T
         following = pltpu.roll(tile[:16], cycles * (GROUPS - 1), 1)
         left_high, left_low = split(jnp.concatenate([tile, following], axis=0))
-        left = jnp.concatenate([left_high, left_low, left_high], axis=1)
-        right = jnp.concatenate([right_high, right_high, right_low], axis=0)
-        picked = dot(left, right)
+        picked = dot(left_high, right_high) + dot(left_low, right_high) + dot(left_high, right_low)
         lane = phi_at & 127
         first, second = shifted_window(phi_taps[k], lane & 7)
         block = lane >> 3
@@ -285,9 +286,9 @@
     shares, outs = refs[:2], refs[2:]
     per_column = tile_list.shape[2]
     first = shares[0].shape[1]
-    rows = outs[0].shape[2]
-
-    for d, (out, share) in enumerate(outs_by_device(outs)):
+    rows = outs[0].shape[1]
+
+    for d, out in enumerate(outs):
         block = place[0] + (place[2] ^ d)
 
         def one(k, carry):
@@ -295,22 +296,22 @@
             inside, beyond = jnp.minimum(j, first - 1), jnp.maximum(j - first, 0)
             for row in range(rows):
                 at = place[3] + row
-                out[share, k, row] = jnp.where(j < first, shares[0][at, inside], shares[1][at, beyond])
+                out[k, row] = jnp.where(j < first, shares[0][at, inside], shares[1][at, beyond])
             return carry
 
         lax.fori_loop(0, per_column, one, 0)
 
 
-def pick_near(shares, place, tile_list, part_count):
+def pick_near(shares, place, tile_list):
     blocks, columns, per_column = tile_list.shape
-    shape = (blocks // 2 // part_count, per_column, shares[0].shape[0] // 2, 8, LANES)
+    shape = (per_column, shares[0].shape[0] // 2, 8, LANES)
     return pl.pallas_call(
         pick_near_kernel,
         grid=(1,),
         in_specs=[pl.BlockSpec(memory_space=pltpu.SMEM)] * 2
         + [pl.BlockSpec(part.shape, lambda i: (0, 0, 0, 0)) for part in shares],
-        out_specs=[pl.BlockSpec(shape, lambda i: (0, 0, 0, 0, 0))] * part_count,
-        out_shape=[jax.ShapeDtypeStruct(shape, f32)] * part_count,
+        out_specs=[pl.BlockSpec(shape, lambda i: (0, 0, 0, 0))] * (blocks // 2),
+        out_shape=[jax.ShapeDtypeStruct(shape, f32)] * (blocks // 2),
         compiler_params=pltpu.CompilerParams(vmem_limit_bytes=VMEM_LIMIT),
         cost_estimate=pl.CostEstimate(flops=0, bytes_accessed=12 * 2**20, transcendentals=0),
         name="pick_near",
@@ -462,75 +463,76 @@
 COLLECT_BATCH = 32
 
 
-def collect_kernel(chunks, tile_list, *refs):
-    arrived, rest = refs[: len(chunks)], refs[len(chunks) :]
-    tables, (out, others, total, sem) = rest[:7], rest[7:]
-    step = pl.program_id(0)
-    per_column = tile_list.shape[2]
+def collect_kernel(begins, tile_list, *refs):
+    count = len(begins)
+    arrived, tables, (out, others) = refs[:count], refs[count : count + 7], refs[count + 7 : count + 9]
+    total, given_sem, sem = refs[count + 9 : count + 12]
+    given = refs[count + 12 :]
+    blocks, _, per_column = tile_list.shape
     cycle_blocks = total.shape[0]
-    collecting = tile_list.shape[0] // COLLECT_STEP
     first = cycle_blocks - others.shape[0]
-
-    @pl.when(step == 0)
-    def _():
-        def clear(j, carry):
-            total[j] = jnp.zeros(total.shape[1:], f32)
-            return carry
-
-        lax.fori_loop(0, cycle_blocks, clear, 0, unroll=8)
-
-    @pl.when(step < collecting)
-    def _():
-        for d in range(COLLECT_STEP):
-            for ref, begin in zip(arrived, chunks):
-                for c in range(0, ref.shape[1], COLLECT_BATCH):
+    stretches = [pl.ds(at, COLLECT_STEP) for at in range(0, blocks, COLLECT_STEP)]
+    fetches = [
+        [pltpu.make_async_copy(x.at[part], g.at[part], given_sem.at[i, c]) for i, (x, g) in enumerate(zip(arrived, given))]
+        for c, part in enumerate(stretches)
+    ]
+    for fetch in fetches:
+        for copy in fetch:
+            copy.start()
+
+    def clear(j, carry):
+        total[j] = jnp.zeros(total.shape[1:], f32)
+        return carry
+
+    lax.fori_loop(0, cycle_blocks, clear, 0, unroll=8)
+    for c, fetch in enumerate(fetches):
+        for copy in fetch:
+            copy.wait()
+
+        def one(d, carry):
+            for ref, begin in zip(given, begins):
+                extent = ref.shape[1]
+                for at in range(0, extent, COLLECT_BATCH):
                     where = []
-                    for slot in range(begin + c, min(begin + c + COLLECT_BATCH, begin + ref.shape[1])):
+                    for slot in range(begin + at, begin + min(at + COLLECT_BATCH, extent)):
                         q, k = slot // per_column, slot % per_column
-                        where.append((tile_list[step * COLLECT_STEP + d, q, k], q))
-                    sums = [total[j, q] + ref[d, c + at] for at, (j, q) in enumerate(where)]
+                        where.append((tile_list[d, q, k], q))
+                    sums = [total[j, q] + ref[d, at + i] for i, (j, q) in enumerate(where)]
                     for (j, q), x in zip(where, sums):
                         total[j, q] = x
-
+            return carry
+
+        lax.fori_loop(c * COLLECT_STEP, (c + 1) * COLLECT_STEP, one, 0)
     hand_over = pltpu.make_async_copy(total.at[pl.ds(first, others.shape[0])], others, sem)
-
-    @pl.when(step >= collecting)
-    def _():
-        @pl.when(step == collecting)
-        def _():
-            hand_over.start()
-
-        filter_into(tables, total, (step - collecting) * FILTER_STEP, out)
-
-        @pl.when(step == pl.num_programs(0) - 1)
-        def _():
-            hand_over.wait()
-
-
-def collect_and_filter(arrived, chunks, tile_list, tables, cycle_blocks, part):
+    hand_over.start()
+    filter_into(tables, total, 0, out)
+    hand_over.wait()
+
+
+def collect_and_filter(arrived, begins, tile_list, tables, cycle_blocks):
     blocks, columns, per_column = tile_list.shape
-    collecting = blocks // COLLECT_STEP
-    steps = part // FILTER_STEP
     return pl.pallas_call(
-        functools.partial(collect_kernel, chunks),
-        grid=(collecting + steps,),
+        functools.partial(collect_kernel, begins),
+        grid=(1,),
         in_specs=[pl.BlockSpec(memory_space=pltpu.SMEM)]
-        + [
-            pl.BlockSpec((COLLECT_STEP,) + x.shape[1:], lambda i: (jnp.minimum(i, collecting - 1), 0, 0, 0))
-            for x in arrived
-        ]
+        + [pl.BlockSpec(memory_space=pl.ANY)] * len(arrived)
         + whole_specs(tables),
         out_specs=[
-            pl.BlockSpec((columns, FILTER_STEP, 8, LANES), lambda i: (0, jnp.maximum(i - collecting, 0), 0, 0)),
+            pl.BlockSpec((columns, FILTER_STEP, 8, LANES), lambda i: (0, 0, 0, 0)),
             pl.BlockSpec(memory_space=pl.ANY),
         ],
         out_shape=[
-            jax.ShapeDtypeStruct((columns, part, 8, LANES), f32),
-            jax.ShapeDtypeStruct((cycle_blocks - part, columns, 8, LANES), f32),
+            jax.ShapeDtypeStruct((columns, FILTER_STEP, 8, LANES), f32),
+            jax.ShapeDtypeStruct((cycle_blocks - FILTER_STEP, columns, 8, LANES), f32),
         ],
-        scratch_shapes=[pltpu.VMEM((cycle_blocks, columns, 8, LANES), f32), pltpu.SemaphoreType.DMA],
+        scratch_shapes=[
+            pltpu.VMEM((cycle_blocks, columns, 8, LANES), f32),
+            pltpu.SemaphoreType.DMA((len(arrived), blocks // COLLECT_STEP)),
+            pltpu.SemaphoreType.DMA,
+        ]
+        + [pltpu.VMEM(x.shape, f32) for x in arrived],
         compiler_params=pltpu.CompilerParams(vmem_limit_bytes=VMEM_LIMIT),
-        cost_estimate=filter_cost(part + 64),
+        cost_estimate=filter_cost(FILTER_STEP + 64),
         name="collect_filter",
     )(tile_list, *arrived, *tables)
 
@@ -542,7 +544,6 @@
 
 
 SLOT_CHUNKS = (8, 56)
-FILTER_FIRST = 32
 AXES = ("half", "share", "tile")
 
 
@@ -572,7 +573,7 @@
         arrived.append(exchange(tiles.reshape(blocks, extent, 8, LANES), AXES))
         begins.append(at)
         at += extent
-    early, others = collect_and_filter(arrived, begins, tile_list, tables, cycle_blocks, FILTER_FIRST)
+    early, others = collect_and_filter(arrived, begins, tile_list, tables, cycle_blocks)
     late = filter_cycles(others, tables)
 
     def pass_on(parts):
@@ -588,14 +589,6 @@
     far = pick_far([early, late], tile_list)
     late_share = exchange(after(late, early_share), AXES[:2])
     own = pass_on(pick_own([after(early, far), late], place, tile_list, part_count))
-    far_tiles = exchange(after(far, late_share, *own[1:]), AXES)
-    near = pass_on(pick_near([early_share, late_share], place, tile_list, part_count))
-
-    far_tiles = far_tiles.reshape(columns, part_count, near_slots, 8, LANES)
-    far_spec = pl.BlockSpec((columns, part_count, STEP_SLOTS, 8, LANES), lambda i, at: (0, 0, i, 0, 0))
-
-    def far_rows(begin, tiles, k):
-        return [(r, tiles[0][r % columns, r // columns, k]) for r in range(TR)]
 
     def own_rows(begin, tiles, k):
         step = pl.program_id(0)
@@ -604,16 +597,6 @@
                 source = begin[1] ^ (p * part_count + t)
                 yield t * shares + p, tiles[0][source, step * STEP_SLOTS + k]
 
-    def near_rows(begin, tiles, k):
-        apart = begin[1] // part_count ^ pl.program_id(0)
-        for t in range(part_count):
-            source = begin[1] % part_count ^ t
-            for p in range(shares):
-                row = tiles[0][source, k, p]
-                for d in range(1, shares):
-                    row = jnp.where(apart == d, tiles[d][source, k, p], row)
-                yield t * shares + p, row
-
     def whole_specs_at(arrays):
         return [pl.BlockSpec(x.shape, functools.partial(lambda nd, i, at: (0,) * nd, x.ndim)) for x in arrays]
 
@@ -622,13 +605,31 @@
 
     own = [jnp.concatenate(own)]
     gradient = read_points(points, begin_at(half, half), near_slots, own, whole_specs_at(own), TR // 2, own_rows, None)
-    gradient = read_points(points, begin_at(1 - half, half), near_slots, [far_tiles], [far_spec], TR, far_rows, gradient)
-    near = [after(x, gradient) for x in near]
+    whole = merge_rows(early_share, 0, cycle_blocks, None)
+    far_tiles = exchange(after(far, late_share, gradient, whole), AXES)
+    near = list(pick_near([early_share, late_share], place, tile_list))
+    for d in range(1, blocks // 2):
+        near[d] = lax.ppermute(near[d], AXES[1:], [(i, i ^ d) for i in range(blocks // 2)])
+
+    far_tiles = far_tiles.reshape(columns, part_count, near_slots, 8, LANES)
+    far_spec = pl.BlockSpec((columns, part_count, STEP_SLOTS, 8, LANES), lambda i, at: (0, 0, i, 0, 0))
+
+    def far_rows(begin, tiles, k):
+        return [(r, tiles[0][r % columns, r // columns, k]) for r in range(TR)]
+
+    def near_rows(begin, tiles, k):
+        for t in range(part_count):
+            source = begin[1] ^ (pl.program_id(0) * part_count + t)
+            for p in range(shares):
+                yield t * shares + p, tiles[0][source, k, p]
+
+    moved = near[5]
+    near = [jnp.stack(near)]
     gradient = read_points(
         points, begin_at(half, 1 - half), near_slots, near, whole_specs_at(near), TR // 2, near_rows, gradient
     )
-    whole = merge_rows(early_share, 0, cycle_blocks, None)
-    whole = merge_rows(late_share, FILTER_FIRST, cycle_blocks, whole)
+    gradient = read_points(points, begin_at(1 - half, half), near_slots, [far_tiles], [far_spec], TR, far_rows, gradient)
+    whole = merge_rows(after(late_share, moved), FILTER_STEP, cycle_blocks, whole)
     return whole, gradient[None]
 
 

time: 554 us -> 553 us (level)
  starting transfers between devices: 43.5 us -> 67.1 us
  waiting for transfers between devices: 352 us -> 332 us
    ppermute x0 -> x15, waiting for transfers between devices: none -> 45.4 us  [row_owner_plan(): lax.ppermute(near[d], AXES[1:], [(i, i ^ d) for i in range(blocks // 2)])]
    all_to_all x5, waiting for transfers between devices: 213 us -> 172 us  [exchange(): return lax.all_to_all(x, axes, 0, 0, tiled=True)]
    ppermute x0 -> x15, starting transfers between devices: none -> 29.2 us  [row_owner_plan(): lax.ppermute(near[d], AXES[1:], [(i, i ^ d) for i in range(blocks // 2)])]
    ppermute x12 -> x6, waiting for transfers between devices: 138 us -> 115 us  [step(): return lax.ppermute(x, axis, [(i, i ^ d) for i in range(size)]) if d else x]
    ppermute x12 -> x6, starting transfers between devices: 11.2 us -> 5.54 us  [step(): return lax.ppermute(x, axis, [(i, i ^ d) for i in range(size)]) if d else x]
  transfers between devices with their start and end apart: 17 -> 26, of which waited for: 11 -> 17; matrix products, arithmetic and copies ran while one was open for 2% -> 1% of each run, Pallas kernels for 20% -> 20%
where the time goes in v6:
time: 553 us; the launch traced here: 549 us
  waiting for transfers between devices  332 us (60%)
  Pallas kernels  138 us (25%)
  starting transfers between devices  67.1 us (12%)
  local copies, waits for them, and re-layouts  8.87 us (2%)
    all_to_all x5, waiting for transfers between devices, exchange(): return lax.all_to_all(x, axes, 0, 0, tiled=True)  172 us
    ppermute x6, waiting for transfers between devices, step(): return lax.ppermute(x, axis, [(i, i ^ d) for i in range(size)]) if d else x  115 us
    ppermute x15, waiting for transfers between devices, row_owner_plan(): lax.ppermute(near[d], AXES[1:], [(i, i ^ d) for i in range(blocks // 2)])  45.4 us
    pallas_call x3, Pallas kernels, read_points(): pl.pallas_call(functools.partial(read_kernel, len(tile_specs), cycles, pl...  36.9 us
    pallas_call x2, Pallas kernels, spread_tiles(): pl.pallas_call(spread_kernel, grid=(slots // STEP_SLOTS,), in_specs=point...  33.3 us
    all_to_all x5, starting transfers between devices, exchange(): return lax.all_to_all(x, axes, 0, 0, tiled=True)  32.3 us
    ppermute x15, starting transfers between devices, row_owner_plan(): lax.ppermute(near[d], AXES[1:], [(i, i ^ d) for i in range(blocks // 2)])  29.2 us
    pallas_call x1, Pallas kernels, filter_cycles(): pl.pallas_call(filter_kernel, grid=(blocks // FILTER_STEP,), in_specs=who...  18.1 us
  transfers between devices with their start and end apart: 26, of which 17 were waited for; matrix products, arithmetic and copies ran while one was open for 1% of the time, Pallas kernels for 20%

profile of v6, /device:TPU:0, one launch (start us, length us, event | category | flops | bytes accessed | tf_op | source)
XLA Modules:
  0.0 549.1 jit_solution(4278702361977259035)
XLA Ops:
  0.6 5.7 %spread.2 = f32[8,4,1,8,8,128]{5,4,3,2,1,0:T(8,128)} custom-call(f32[64,1024]{1,0:T(8,128)} %bitcast.64, f32[64,8,1024]{2,1,0:T(8,128)} %bitcast.54, f32[64,8,1024]{2,1,0:T(8,128)} %bitcast.59, s32[64,1024]{1,0:T(8,128)} %bitcast.66, s32[64,1024]{1,0:T(8,128)} %bitcast.71), custom_call_target="tpu_custom_call" | custom-call | flops 3221225472 | bytes 1671168 | tf_op jit(solution)/shard_map/spread/pallas_call | solution.py:137
  6.3 7.3 %all-to-all-start = ((f32[32,8,8,128]{3,2,1,0:T(8,128)}), f32[32,8,8,128]{3,2,1,0:T(8,128)S(1)}, u32[]{:S(2)}, u32[]{:S(2)}) async-start(f32[32,8,8,128]{3,2,1,0:T(8,128)} %bitcast.51), calls=%async_computation | async-start | bytes 2097152 | tf_op jit(solution)/shard_map/all_to_all | solution.py:568
  13.6 27.7 %spread.3 = f32[8,4,1,56,8,128]{5,4,3,2,1,0:T(8,128)} custom-call(f32[64,1024]{1,0:T(8,128)} %bitcast.65, f32[64,8,1024]{2,1,0:T(8,128)} %bitcast.55, f32[64,8,1024]{2,1,0:T(8,128)} %bitcast.60, s32[64,1024]{1,0:T(8,128)} %bitcast.67, s32[64,1024]{1,0:T(8,128)} %bitcast.72), custom_call_target="tpu_custom_call" | custom-call | flops 22548578304 | bytes 11698176 | tf_op jit(solution)/shard_map/spread/pallas_call | solution.py:137
  42.3 5.9 %all-to-all-start.1 = ((f32[32,56,8,128]{3,2,1,0:T(8,128)}), f32[32,56,8,128]{3,2,1,0:T(8,128)}, u32[]{:S(2)}, u32[]{:S(2)}) async-start(f32[32,56,8,128]{3,2,1,0:T(8,128)} %bitcast.50), calls=%async_computation.1 | async-start | bytes 14680064 | tf_op jit(solution)/shard_map/all_to_all | solution.py:568
  50.2 161.2 %all-to-all-done.1.refs_1_ = f32[32,56,8,128]{3,2,1,0:T(8,128)} async-done(((f32[32,56,8,128]{3,2,1,0:T(8,128)}), f32[32,56,8,128]{3,2,1,0:T(8,128)}, u32[]{:S(2)}, u32[]{:S(2)}) %all-to-all-start.1) | async-done | bytes 7340064 | tf_op jit(solution)/shard_map/all_to_all | solution.py:568
  211.4 12.1 %collect_filter.1 = (f32[8,32,8,128]{3,2,1,0:T(8,128)}, f32[224,8,8,128]{3,2,1,0:T(8,128)}) custom-call(s32[32,8,8]{2,1,0:T(8,128)} %copy.23.tile_list, f32[32,8,8,128]{3,2,1,0:T(8,128)} %copy-done.1, f32[32,56,8,128]{3,2,1,0:T(8,128)} %all-to-all-done.1.refs_1_, bf16[128,384]{1,0:T(8,128)(2,1)} %constant.33.clone.refs_2_.refs_0_, ...), custom_call_target="tpu_custom_call" | custom-call | flops 3623878656 | bytes 6291456 | tf_op jit(solution)/shard_map/collect_filter/pallas_call | solution.py:514
  227.1 18.1 %filter_cycles.1.refs_1_ = f32[8,224,8,128]{3,2,1,0:T(8,128)} custom-call(bf16[128,384]{1,0:T(8,128)(2,1)} %constant.33.clone.refs_2_.refs_0_, bf16[128,384]{1,0:T(8,128)(2,1)} %constant.34.clone.refs_3_.refs_1_, bf16[768,256]{1,0:T(8,128)(2,1)} %constant.35.clone.refs_4_.refs_2_, bf16[768,256]{1,0:T(8,128)(2,1)} %constant.36.clone.refs_5_.refs_3_, ...), custom_call_target="tpu_custom_call" | custom-call | flops 8455716864 | bytes 14680064 | tf_op jit(solution)/shard_map/filter_cycles/pallas_call | solution.py:450
  245.2 7.6 %all-to-all-done.2.refs_0_.arrived = f32[8,32,8,128]{3,2,1,0:T(8,128)S(1)} async-done(((f32[8,32,8,128]{3,2,1,0:T(8,128)}), f32[8,32,8,128]{3,2,1,0:T(8,128)S(1)}, u32[]{:S(2)}, u32[]{:S(2)}) %all-to-all-start.2) | async-done | bytes 1048608 | tf_op jit(solution)/shard_map/all_to_all | solution.py:568
  259.5 9.9 %pick_far.1 = f32[32,32,8,128]{3,2,1,0:T(8,128)} custom-call(s32[32,8,8]{2,1,0:T(8,128)} %copy.23.tile_list, f32[8,32,8,128]{3,2,1,0:T(8,128)} %get-tuple-element.33.refs_0_, f32[8,224,8,128]{3,2,1,0:T(8,128)} %filter_cycles.1.refs_1_), custom_call_target="tpu_custom_call" | custom-call | bytes 12582912 | tf_op jit(solution)/shard_map/pick_far/pallas_call | solution.py:232
  269.3 7.7 %pick_own.1 = (f32[4,32,8,128]{3,2,1,0:T(8,128)}, f32[4,32,8,128]{3,2,1,0:T(8,128)}, f32[4,32,8,128]{3,2,1,0:T(8,128)}, f32[4,32,8,128]{3,2,1,0:T(8,128)}) custom-call(s32[5]{0:T(128)} %stack.105.place, s32[32,8,8]{2,1,0:T(8,128)} %copy.23.tile_list, f32[8,32,8,128]{3,2,1,0:T(8,128)} %get-tuple-element.33.refs_0_, f32[8,224,8,128]{3,2,1,0:T(8,128)} %filter_cycles.1.refs_1_), custom_call_target="tpu_custom_call" | custom-call | bytes 10485760 | tf_op jit(solution)/shard_map/pick_own/pallas_call | solution.py:272
  280.0 11.9 %collective-permute-done.2 = f32[4,32,8,128]{3,2,1,0:T(8,128)S(1)} collective-permute-done((f32[4,32,8,128]{3,2,1,0:T(8,128)}, f32[4,32,8,128]{3,2,1,0:T(8,128)S(1)}, u32[]{:S(2)}, u32[]{:S(2)}) %collective-permute-start.2) | collective-permute-done | bytes 524320 | tf_op jit(solution)/shard_map/ppermute | solution.py:581
  291.9 10.4 %collective-permute-done.3 = f32[4,32,8,128]{3,2,1,0:T(8,128)S(1)} collective-permute-done((f32[4,32,8,128]{3,2,1,0:T(8,128)}, f32[4,32,8,128]{3,2,1,0:T(8,128)S(1)}, u32[]{:S(2)}, u32[]{:S(2)}) %collective-permute-start.3) | collective-permute-done | bytes 524320 | tf_op jit(solution)/shard_map/ppermute | solution.py:581
  306.8 23.3 %collective-permute-done.4 = f32[4,32,8,128]{3,2,1,0:T(8,128)S(1)} collective-permute-done((f32[4,32,8,128]{3,2,1,0:T(8,128)S(1)}, f32[4,32,8,128]{3,2,1,0:T(8,128)S(1)}, u32[]{:S(2)}, u32[]{:S(2)}) %collective-permute-start.4) | collective-permute-done | bytes 524320 | tf_op jit(solution)/shard_map/ppermute | solution.py:581
  330.1 59.9 %collective-permute-done.5 = f32[4,32,8,128]{3,2,1,0:T(8,128)S(1)} collective-permute-done((f32[4,32,8,128]{3,2,1,0:T(8,128)S(1)}, f32[4,32,8,128]{3,2,1,0:T(8,128)S(1)}, u32[]{:S(2)}, u32[]{:S(2)}) %collective-permute-start.5) | collective-permute-done | bytes 524320 | tf_op jit(solution)/shard_map/ppermute | solution.py:581
  390.0 9.3 %collective-permute-done.6 = f32[4,32,8,128]{3,2,1,0:T(8,128)S(1)} collective-permute-done((f32[4,32,8,128]{3,2,1,0:T(8,128)S(1)}, f32[4,32,8,128]{3,2,1,0:T(8,128)S(1)}, u32[]{:S(2)}, u32[]{:S(2)}) %collective-permute-start.6) | collective-permute-done | bytes 524320 | tf_op jit(solution)/shard_map/ppermute | solution.py:581
  400.6 12.4 %read_back.3.rest_1_ = f32[64,1024]{1,0:T(8,128)} custom-call(s32[3]{0:T(128)} %pad_add_fusion.2.begin, f32[64,8,1024]{2,1,0:T(8,128)} %bitcast.56, f32[64,8,1024]{2,1,0:T(8,128)} %bitcast.61, s32[64,1024]{1,0:T(8,128)} %bitcast.68, s32[64,1024]{1,0:T(8,128)} %bitcast.73, f32[16,32,8,128]{3,2,1,0:T(8,128)} %copy-done.5), custom_call_target="tpu_custom_call" | custom-call | flops 6442450944 | bytes 4587520 | tf_op jit(solution)/shard_map/read_back/pallas_call | solution.py:189
  418.5 10.5 %all-to-all-start.4 = ((f32[32,32,8,128]{3,2,1,0:T(8,128)}), f32[32,32,8,128]{3,2,1,0:T(8,128)}, u32[]{:S(2)}, u32[]{:S(2)}) async-start(f32[32,32,8,128]{3,2,1,0:T(8,128)} %pick_far.1), calls=%async_computation.4 | async-start | bytes 8388608 | tf_op jit(solution)/shard_map/all_to_all | solution.py:568
  430.2 7.0 %pick_near.1 = (f32[8,4,8,128]{3,2,1,0:T(8,128)}, f32[8,4,8,128]{3,2,1,0:T(8,128)}, f32[8,4,8,128]{3,2,1,0:T(8,128)}, f32[8,4,8,128]{3,2,1,0:T(8,128)}, f32[8,4,...) custom-call(s32[5]{0:T(128)} %stack.105.place, ...), custom_call_target="tpu_custom_call" | custom-call | bytes 12582912 | tf_op jit(solution)/shard_map/pick_near/pallas_call | solution.py:308
  442.3 16.4 %collective-permute-done = f32[8,4,8,128]{3,2,1,0:T(8,128)S(1)} collective-permute-done((f32[8,4,8,128]{3,2,1,0:T(8,128)}, f32[8,4,8,128]{3,2,1,0:T(8,128)S(1)}, u32[]{:S(2)}, u32[]{:S(2)}) %collective-permute-start) | collective-permute-done | bytes 131104 | tf_op jit(solution)/shard_map/ppermute | solution.py:612
  462.8 10.1 %merge_rows.3 = f32[256,8,1024]{2,1,0:T(8,128)} custom-call(f32[8,224,8,128]{3,2,1,0:T(8,128)} %all-to-all-done.3.refs_1_.arrived, f32[256,8,1024]{2,1,0:T(8,128)} %merge_rows.2.rest_0_), custom_call_target="tpu_custom_call", output_to_operand_aliasing={{}: (1, {})} | custom-call | bytes 14680064 | tf_op jit(solution)/shard_map/merge_rows/pallas_call | solution.py:334
  482.1 9.2 %collective-permute-start.17 = (f32[8,4,8,128]{3,2,1,0:T(8,128)S(1)}, f32[8,4,8,128]{3,2,1,0:T(8,128)S(1)}, u32[]{:S(2)}, u32[]{:S(2)}) collective-permute-start(f32[8,4,8,128]{3,2,1,0:T(8,128)S(1)} %copy-done.9), channel_id=1, source_target_pairs={{0,12},{1,13},{2,14},{3,15},{4,8},{5,9},{6,10},{7,11},{8,4},{9,5},... | collective-permute-start | bytes 393224 | tf_op jit(solution)/shard_map/ppermute | solution.py:612
  491.3 10.4 %collective-permute-done.13 = f32[8,4,8,128]{3,2,1,0:T(8,128)S(1)} collective-permute-done((f32[8,4,8,128]{3,2,1,0:T(8,128)S(1)}, f32[8,4,8,128]{3,2,1,0:T(8,128)S(1)}, u32[]{:S(2)}, u32[]{:S(2)}) %collective-permute-start.13) | collective-permute-done | bytes 131104 | tf_op jit(solution)/shard_map/ppermute | solution.py:612
  524.6 12.4 %read_back.4.rest_1_ = f32[64,1024]{1,0:T(8,128)} custom-call(s32[3]{0:T(128)} %pad_add_fusion.1.begin, f32[64,8,1024]{2,1,0:T(8,128)} %bitcast.57, f32[64,8,1024]{2,1,0:T(8,128)} %bitcast.62, s32[64,1024]{1,0:T(8,128)} %bitcast.69, s32[64,1024]{1,0:T(8,128)} %bitcast.74, f32[16,8,4,8,128]{4,3,2,1,0:T(8,128)} %copy-done.4, ...), custom_call_target="tpu_custom_call", output_to_operand_aliasing={{}: (6, {})} | custom-call | flops 6442450944 | bytes 4587520 | tf_op jit(solution)/shard_map/read_back/pallas_call | solution.py:189
  537.0 12.1 %read_back.5 = f32[64,1024]{1,0:T(8,128)} custom-call(s32[3]{0:T(128)} %add_add_fusion.begin, f32[64,8,1024]{2,1,0:T(8,128)} %bitcast.58, f32[64,8,1024]{2,1,0:T(8,128)} %bitcast.63, s32[64,1024]{1,0:T(8,128)} %bitcast.70, s32[64,1024]{1,0:T(8,128)} %bitcast.75, f32[8,4,32,8,128]{4,3,2,1,0:T(8,128)} %bitcast.14.rest_0_, ...), custom_call_target="tpu_custom_call", output_to_operand_aliasing={{}: (6, {})} | custom-call | flops 12884901888 | bytes 6684672 | tf_op jit(solution)/shard_map/read_back/pallas_call | solution.py:189
  (108 shorter events, 69.7 us)
Async XLA Ops:
  6.3 35.0 %all-to-all-start = ((f32[32,8,8,128]{3,2,1,0:T(8,128)}), f32[32,8,8,128]{3,2,1,0:T(8,128)S(1)}, u32[]{:S(2)}, u32[]{:S(2)}) async-start(f32[32,8,8,128]{3,2,1,0:T(8,128)} %bitcast.51), calls=%async_computation | async-start | bytes 2097152 | tf_op jit(solution)/shard_map/all_to_all | solution.py:568
  42.3 169.1 %all-to-all-start.1 = ((f32[32,56,8,128]{3,2,1,0:T(8,128)}), f32[32,56,8,128]{3,2,1,0:T(8,128)}, u32[]{:S(2)}, u32[]{:S(2)}) async-start(f32[32,56,8,128]{3,2,1,0:T(8,128)} %bitcast.50), calls=%async_computation.1 | async-start | bytes 14680064 | tf_op jit(solution)/shard_map/all_to_all | solution.py:568
  223.5 29.3 %all-to-all-start.2 = ((f32[8,32,8,128]{3,2,1,0:T(8,128)}), f32[8,32,8,128]{3,2,1,0:T(8,128)S(1)}, u32[]{:S(2)}, u32[]{:S(2)}) async-start(f32[8,32,8,128]{3,2,1,0:T(8,128)} %get-tuple-element.33.refs_0_), calls=%async_computation.2 | async-start | bytes 2097152 | tf_op jit(solution)/shard_map/all_to_all | solution.py:568
  253.8 164.7 %all-to-all-start.3 = ((f32[8,224,8,128]{3,2,1,0:T(8,128)}), f32[8,224,8,128]{3,2,1,0:T(8,128)}, u32[]{:S(2)}, u32[]{:S(2)}) async-start(f32[8,224,8,128]{3,2,1,0:T(8,128)} %filter_cycles.1.refs_1_), calls=%async_computation.3 | async-start | bytes 14680064 | tf_op jit(solution)/shard_map/all_to_all | solution.py:568
  277.0 14.9 %collective-permute-start.2 = (f32[4,32,8,128]{3,2,1,0:T(8,128)}, f32[4,32,8,128]{3,2,1,0:T(8,128)S(1)}, u32[]{:S(2)}, u32[]{:S(2)}) collective-permute-start(f32[4,32,8,128]{3,2,1,0:T(8,128)} %get-tuple-element.36), channel_id=1, source_target_pairs={{0,2},{1,3},{2,0},{3,1},{4,6},{5,7},{6,4},{7,5},{8,10},{9,11},{10,... | collective-permute-start | bytes 1572872 | tf_op jit(solution)/shard_map/ppermute | solution.py:581
  277.1 25.2 %collective-permute-start.3 = (f32[4,32,8,128]{3,2,1,0:T(8,128)}, f32[4,32,8,128]{3,2,1,0:T(8,128)S(1)}, u32[]{:S(2)}, u32[]{:S(2)}) collective-permute-start(f32[4,32,8,128]{3,2,1,0:T(8,128)} %get-tuple-element.37), channel_id=1, source_target_pairs={{0,3},{1,2},{2,1},{3,0},{4,7},{5,6},{6,5},{7,4},{8,11},{9,10},{10,... | collective-permute-start | bytes 1572872 | tf_op jit(solution)/shard_map/ppermute | solution.py:581
  302.5 27.6 %collective-permute-start.4 = (f32[4,32,8,128]{3,2,1,0:T(8,128)S(1)}, f32[4,32,8,128]{3,2,1,0:T(8,128)S(1)}, u32[]{:S(2)}, u32[]{:S(2)}) collective-permute-start(f32[4,32,8,128]{3,2,1,0:T(8,128)S(1)} %pad_maximum_fusion), channel_id=1, source_target_pairs={{0,4},{4,0},{8,12},{12,8},{1,5},{5,1},{9,13},{13,9},{2,6},{6,2},{1... | collective-permute-start | bytes 1572872 | tf_op jit(solution)/shard_map/ppermute | solution.py:581
  304.3 85.7 %collective-permute-start.5 = (f32[4,32,8,128]{3,2,1,0:T(8,128)S(1)}, f32[4,32,8,128]{3,2,1,0:T(8,128)S(1)}, u32[]{:S(2)}, u32[]{:S(2)}) collective-permute-start(f32[4,32,8,128]{3,2,1,0:T(8,128)S(1)} %pad_maximum_fusion.1), channel_id=1, source_target_pairs={{0,8},{4,12},{8,0},{12,4},{1,9},{5,13},{9,1},{13,5},{2,10},{6,14},... | collective-permute-start | bytes 1572872 | tf_op jit(solution)/shard_map/ppermute | solution.py:581
  305.8 93.4 %collective-permute-start.6 = (f32[4,32,8,128]{3,2,1,0:T(8,128)S(1)}, f32[4,32,8,128]{3,2,1,0:T(8,128)S(1)}, u32[]{:S(2)}, u32[]{:S(2)}) collective-permute-start(f32[4,32,8,128]{3,2,1,0:T(8,128)S(1)} %pad_maximum_fusion.2), channel_id=1, source_target_pairs={{0,12},{4,8},{8,4},{12,0},{1,13},{5,9},{9,5},{13,1},{2,14},{6,10},... | collective-permute-start | bytes 1572872 | tf_op jit(solution)/shard_map/ppermute | solution.py:581
  418.5 118.6 %all-to-all-start.4 = ((f32[32,32,8,128]{3,2,1,0:T(8,128)}), f32[32,32,8,128]{3,2,1,0:T(8,128)}, u32[]{:S(2)}, u32[]{:S(2)}) async-start(f32[32,32,8,128]{3,2,1,0:T(8,128)} %pick_far.1), calls=%async_computation.4 | async-start | bytes 8388608 | tf_op jit(solution)/shard_map/all_to_all | solution.py:568
  437.2 21.6 %collective-permute-start = (f32[8,4,8,128]{3,2,1,0:T(8,128)}, f32[8,4,8,128]{3,2,1,0:T(8,128)S(1)}, u32[]{:S(2)}, u32[]{:S(2)}) collective-permute-start(f32[8,4,8,128]{3,2,1,0:T(8,128)} %get-tuple-element.31), channel_id=1, source_target_pairs={{0,5},{1,4},{2,7},{3,6},{4,1},{5,0},{6,3},{7,2},{8,13},{9,12},{10,... | collective-permute-start | bytes 393224 | tf_op jit(solution)/shard_map/ppermute | solution.py:612
  438.6 34.3 %collective-permute-start.7 = (f32[8,4,8,128]{3,2,1,0:T(8,128)}, f32[8,4,8,128]{3,2,1,0:T(8,128)S(1)}, u32[]{:S(2)}, u32[]{:S(2)}) collective-permute-start(f32[8,4,8,128]{3,2,1,0:T(8,128)} %get-tuple-element.40), channel_id=1, source_target_pairs={{0,1},{1,0},{2,3},{3,2},{4,5},{5,4},{6,7},{7,6},{8,9},{9,8},{10,11... | collective-permute-start | bytes 393224 | tf_op jit(solution)/shard_map/ppermute | solution.py:612
  439.5 33.6 %collective-permute-start.8 = (f32[8,4,8,128]{3,2,1,0:T(8,128)}, f32[8,4,8,128]{3,2,1,0:T(8,128)S(1)}, u32[]{:S(2)}, u32[]{:S(2)}) collective-permute-start(f32[8,4,8,128]{3,2,1,0:T(8,128)} %get-tuple-element.41), channel_id=1, source_target_pairs={{0,2},{1,3},{2,0},{3,1},{4,6},{5,7},{6,4},{7,5},{8,10},{9,11},{10,... | collective-permute-start | bytes 393224 | tf_op jit(solution)/shard_map/ppermute | solution.py:612
  440.5 32.7 %collective-permute-start.9 = (f32[8,4,8,128]{3,2,1,0:T(8,128)}, f32[8,4,8,128]{3,2,1,0:T(8,128)S(1)}, u32[]{:S(2)}, u32[]{:S(2)}) collective-permute-start(f32[8,4,8,128]{3,2,1,0:T(8,128)} %get-tuple-element.42), channel_id=1, source_target_pairs={{0,3},{1,2},{2,1},{3,0},{4,7},{5,6},{6,5},{7,4},{8,11},{9,10},{10,... | collective-permute-start | bytes 393224 | tf_op jit(solution)/shard_map/ppermute | solution.py:612
  440.9 34.0 %collective-permute-start.10 = (f32[8,4,8,128]{3,2,1,0:T(8,128)}, f32[8,4,8,128]{3,2,1,0:T(8,128)S(1)}, u32[]{:S(2)}, u32[]{:S(2)}) collective-permute-start(f32[8,4,8,128]{3,2,1,0:T(8,128)} %get-tuple-element.43), channel_id=1, source_target_pairs={{0,4},{1,5},{2,6},{3,7},{4,0},{5,1},{6,2},{7,3},{8,12},{9,13},{10,... | collective-permute-start | bytes 393224 | tf_op jit(solution)/shard_map/ppermute | solution.py:612
  458.8 19.7 %collective-permute-start.11 = (f32[8,4,8,128]{3,2,1,0:T(8,128)}, f32[8,4,8,128]{3,2,1,0:T(8,128)S(1)}, u32[]{:S(2)}, u32[]{:S(2)}) collective-permute-start(f32[8,4,8,128]{3,2,1,0:T(8,128)} %get-tuple-element.44), channel_id=1, source_target_pairs={{0,6},{1,7},{2,4},{3,5},{4,2},{5,3},{6,0},{7,1},{8,14},{9,15},{10,... | collective-permute-start | bytes 393224 | tf_op jit(solution)/shard_map/ppermute | solution.py:612
  473.1 28.6 %collective-permute-start.13 = (f32[8,4,8,128]{3,2,1,0:T(8,128)S(1)}, f32[8,4,8,128]{3,2,1,0:T(8,128)S(1)}, u32[]{:S(2)}, u32[]{:S(2)}) collective-permute-start(f32[8,4,8,128]{3,2,1,0:T(8,128)S(1)} %copy-done.13), channel_id=1, source_target_pairs={{0,8},{1,9},{2,10},{3,11},{4,12},{5,13},{6,14},{7,15},{8,0},{9,1},... | collective-permute-start | bytes 393224 | tf_op jit(solution)/shard_map/ppermute | solution.py:612
  473.2 31.3 %collective-permute-start.14 = (f32[8,4,8,128]{3,2,1,0:T(8,128)S(1)}, f32[8,4,8,128]{3,2,1,0:T(8,128)S(1)}, u32[]{:S(2)}, u32[]{:S(2)}) collective-permute-start(f32[8,4,8,128]{3,2,1,0:T(8,128)S(1)} %copy-done.12), channel_id=1, source_target_pairs={{0,9},{1,8},{2,11},{3,10},{4,13},{5,12},{6,15},{7,14},{8,1},{9,0},... | collective-permute-start | bytes 393224 | tf_op jit(solution)/shard_map/ppermute | solution.py:612
  474.9 33.0 %collective-permute-start.15 = (f32[8,4,8,128]{3,2,1,0:T(8,128)S(1)}, f32[8,4,8,128]{3,2,1,0:T(8,128)S(1)}, u32[]{:S(2)}, u32[]{:S(2)}) collective-permute-start(f32[8,4,8,128]{3,2,1,0:T(8,128)S(1)} %copy-done.11), channel_id=1, source_target_pairs={{0,10},{1,11},{2,8},{3,9},{4,14},{5,15},{6,12},{7,13},{8,2},{9,3},... | collective-permute-start | bytes 393224 | tf_op jit(solution)/shard_map/ppermute | solution.py:612
  478.4 31.7 %collective-permute-start.16 = (f32[8,4,8,128]{3,2,1,0:T(8,128)S(1)}, f32[8,4,8,128]{3,2,1,0:T(8,128)S(1)}, u32[]{:S(2)}, u32[]{:S(2)}) collective-permute-start(f32[8,4,8,128]{3,2,1,0:T(8,128)S(1)} %copy-done.10), channel_id=1, source_target_pairs={{0,11},{1,10},{2,9},{3,8},{4,15},{5,14},{6,13},{7,12},{8,3},{9,2},... | collective-permute-start | bytes 393224 | tf_op jit(solution)/shard_map/ppermute | solution.py:612
  482.1 30.8 %collective-permute-start.17 = (f32[8,4,8,128]{3,2,1,0:T(8,128)S(1)}, f32[8,4,8,128]{3,2,1,0:T(8,128)S(1)}, u32[]{:S(2)}, u32[]{:S(2)}) collective-permute-start(f32[8,4,8,128]{3,2,1,0:T(8,128)S(1)} %copy-done.9), channel_id=1, source_target_pairs={{0,12},{1,13},{2,14},{3,15},{4,8},{5,9},{6,10},{7,11},{8,4},{9,5},... | collective-permute-start | bytes 393224 | tf_op jit(solution)/shard_map/ppermute | solution.py:612
  501.7 15.3 %collective-permute-start.18 = (f32[8,4,8,128]{3,2,1,0:T(8,128)S(1)}, f32[8,4,8,128]{3,2,1,0:T(8,128)S(1)}, u32[]{:S(2)}, u32[]{:S(2)}) collective-permute-start(f32[8,4,8,128]{3,2,1,0:T(8,128)S(1)} %copy-done.8), channel_id=1, source_target_pairs={{0,13},{1,12},{2,15},{3,14},{4,9},{5,8},{6,11},{7,10},{8,5},{9,4},... | collective-permute-start | bytes 393224 | tf_op jit(solution)/shard_map/ppermute | solution.py:612
  504.5 16.6 %collective-permute-start.19 = (f32[8,4,8,128]{3,2,1,0:T(8,128)S(1)}, f32[8,4,8,128]{3,2,1,0:T(8,128)S(1)}, u32[]{:S(2)}, u32[]{:S(2)}) collective-permute-start(f32[8,4,8,128]{3,2,1,0:T(8,128)S(1)} %copy-done.7), channel_id=1, source_target_pairs={{0,14},{1,15},{2,12},{3,13},{4,10},{5,11},{6,8},{7,9},{8,6},{9,7},... | collective-permute-start | bytes 393224 | tf_op jit(solution)/shard_map/ppermute | solution.py:612
  507.9 15.3 %collective-permute-start.20 = (f32[8,4,8,128]{3,2,1,0:T(8,128)S(1)}, f32[8,4,8,128]{3,2,1,0:T(8,128)S(1)}, u32[]{:S(2)}, u32[]{:S(2)}) collective-permute-start(f32[8,4,8,128]{3,2,1,0:T(8,128)S(1)} %copy-done.6), channel_id=1, source_target_pairs={{0,15},{1,14},{2,13},{3,12},{4,11},{5,10},{6,9},{7,8},{8,7},{9,6},... | collective-permute-start | bytes 393224 | tf_op jit(solution)/shard_map/ppermute | solution.py:612
  (17 other events, 243.2 us)

commit v7 on v6

--- a/solution.py
+++ b/solution.py
@@ -619,14 +619,18 @@
 
     def near_rows(begin, tiles, k):
         for t in range(part_count):
-            source = begin[1] ^ (pl.program_id(0) * part_count + t)
             for p in range(shares):
-                yield t * shares + p, tiles[0][source, k, p]
+                yield t * shares + p, tiles[t][k, p]
 
     moved = near[5]
-    near = [jnp.stack(near)]
+    near = jnp.stack(near)
+
+    def near_spec(t):
+        return pl.BlockSpec((None,) + near.shape[1:], lambda i, at: (at[1] ^ (i * part_count + t), 0, 0, 0, 0))
+
+    near_specs = [near_spec(t) for t in range(part_count)]
     gradient = read_points(
-        points, begin_at(half, 1 - half), near_slots, near, whole_specs_at(near), TR // 2, near_rows, gradient
+        points, begin_at(half, 1 - half), near_slots, [near] * part_count, near_specs, TR // 2, near_rows, gradient
     )
     gradient = read_points(points, begin_at(1 - half, half), near_slots, [far_tiles], [far_spec], TR, far_rows, gradient)
     whole = merge_rows(after(late_share, moved), FILTER_STEP, cycle_blocks, whole)

time: 553 us -> 553 us (level)
  no operation moved by 1% of the time
where the time goes in v7:
time: 553 us; the launch traced here: 549 us
  waiting for transfers between devices  332 us (60%)
  Pallas kernels  137 us (25%)
  starting transfers between devices  67.1 us (12%)
  local copies, waits for them, and re-layouts  8.87 us (2%)
    all_to_all x5, waiting for transfers between devices, exchange(): return lax.all_to_all(x, axes, 0, 0, tiled=True)  172 us
    ppermute x6, waiting for transfers between devices, step(): return lax.ppermute(x, axis, [(i, i ^ d) for i in range(size)]) if d else x  115 us
    ppermute x15, waiting for transfers between devices, row_owner_plan(): lax.ppermute(near[d], AXES[1:], [(i, i ^ d) for i in range(blocks // 2)])  45.4 us
    pallas_call x3, Pallas kernels, read_points(): pl.pallas_call(functools.partial(read_kernel, len(tile_specs), cycles, pl...  36.5 us
    pallas_call x2, Pallas kernels, spread_tiles(): pl.pallas_call(spread_kernel, grid=(slots // STEP_SLOTS,), in_specs=point...  33.3 us
    all_to_all x5, starting transfers between devices, exchange(): return lax.all_to_all(x, axes, 0, 0, tiled=True)  32.3 us
    ppermute x15, starting transfers between devices, row_owner_plan(): lax.ppermute(near[d], AXES[1:], [(i, i ^ d) for i in range(blocks // 2)])  29.2 us
    pallas_call x1, Pallas kernels, filter_cycles(): pl.pallas_call(filter_kernel, grid=(blocks // FILTER_STEP,), in_specs=who...  18.1 us
  transfers between devices with their start and end apart: 26, of which 17 were waited for; matrix products, arithmetic and copies ran while one was open for 1% of the time, Pallas kernels for 20%

profile of v7, /device:TPU:0, one launch (start us, length us, event | category | flops | bytes accessed | tf_op | source)
XLA Modules:
  0.0 548.7 jit_solution(8657913065631423797)
XLA Ops:
  0.6 5.7 %spread.2 = f32[8,4,1,8,8,128]{5,4,3,2,1,0:T(8,128)} custom-call(f32[64,1024]{1,0:T(8,128)} %bitcast.64, f32[64,8,1024]{2,1,0:T(8,128)} %bitcast.54, f32[64,8,1024]{2,1,0:T(8,128)} %bitcast.59, s32[64,1024]{1,0:T(8,128)} %bitcast.66, s32[64,1024]{1,0:T(8,128)} %bitcast.71), custom_call_target="tpu_custom_call" | custom-call | flops 3221225472 | bytes 1671168 | tf_op jit(solution)/shard_map/spread/pallas_call | solution.py:137
  6.3 7.3 %all-to-all-start = ((f32[32,8,8,128]{3,2,1,0:T(8,128)}), f32[32,8,8,128]{3,2,1,0:T(8,128)S(1)}, u32[]{:S(2)}, u32[]{:S(2)}) async-start(f32[32,8,8,128]{3,2,1,0:T(8,128)} %bitcast.51), calls=%async_computation | async-start | bytes 2097152 | tf_op jit(solution)/shard_map/all_to_all | solution.py:568
  13.6 27.7 %spread.3 = f32[8,4,1,56,8,128]{5,4,3,2,1,0:T(8,128)} custom-call(f32[64,1024]{1,0:T(8,128)} %bitcast.65, f32[64,8,1024]{2,1,0:T(8,128)} %bitcast.55, f32[64,8,1024]{2,1,0:T(8,128)} %bitcast.60, s32[64,1024]{1,0:T(8,128)} %bitcast.67, s32[64,1024]{1,0:T(8,128)} %bitcast.72), custom_call_target="tpu_custom_call" | custom-call | flops 22548578304 | bytes 11698176 | tf_op jit(solution)/shard_map/spread/pallas_call | solution.py:137
  42.3 5.9 %all-to-all-start.1 = ((f32[32,56,8,128]{3,2,1,0:T(8,128)}), f32[32,56,8,128]{3,2,1,0:T(8,128)}, u32[]{:S(2)}, u32[]{:S(2)}) async-start(f32[32,56,8,128]{3,2,1,0:T(8,128)} %bitcast.50), calls=%async_computation.1 | async-start | bytes 14680064 | tf_op jit(solution)/shard_map/all_to_all | solution.py:568
  50.2 161.2 %all-to-all-done.1.refs_1_ = f32[32,56,8,128]{3,2,1,0:T(8,128)} async-done(((f32[32,56,8,128]{3,2,1,0:T(8,128)}), f32[32,56,8,128]{3,2,1,0:T(8,128)}, u32[]{:S(2)}, u32[]{:S(2)}) %all-to-all-start.1) | async-done | bytes 7340064 | tf_op jit(solution)/shard_map/all_to_all | solution.py:568
  211.4 12.1 %collect_filter.1 = (f32[8,32,8,128]{3,2,1,0:T(8,128)}, f32[224,8,8,128]{3,2,1,0:T(8,128)}) custom-call(s32[32,8,8]{2,1,0:T(8,128)} %copy.23.tile_list, f32[32,8,8,128]{3,2,1,0:T(8,128)} %copy-done.1, f32[32,56,8,128]{3,2,1,0:T(8,128)} %all-to-all-done.1.refs_1_, bf16[128,384]{1,0:T(8,128)(2,1)} %constant.33.clone.refs_2_.refs_0_, ...), custom_call_target="tpu_custom_call" | custom-call | flops 3623878656 | bytes 6291456 | tf_op jit(solution)/shard_map/collect_filter/pallas_call | solution.py:514
  227.1 18.1 %filter_cycles.1.refs_1_ = f32[8,224,8,128]{3,2,1,0:T(8,128)} custom-call(bf16[128,384]{1,0:T(8,128)(2,1)} %constant.33.clone.refs_2_.refs_0_, bf16[128,384]{1,0:T(8,128)(2,1)} %constant.34.clone.refs_3_.refs_1_, bf16[768,256]{1,0:T(8,128)(2,1)} %constant.35.clone.refs_4_.refs_2_, bf16[768,256]{1,0:T(8,128)(2,1)} %constant.36.clone.refs_5_.refs_3_, ...), custom_call_target="tpu_custom_call" | custom-call | flops 8455716864 | bytes 14680064 | tf_op jit(solution)/shard_map/filter_cycles/pallas_call | solution.py:450
  245.2 7.6 %all-to-all-done.2.refs_0_.arrived = f32[8,32,8,128]{3,2,1,0:T(8,128)S(1)} async-done(((f32[8,32,8,128]{3,2,1,0:T(8,128)}), f32[8,32,8,128]{3,2,1,0:T(8,128)S(1)}, u32[]{:S(2)}, u32[]{:S(2)}) %all-to-all-start.2) | async-done | bytes 1048608 | tf_op jit(solution)/shard_map/all_to_all | solution.py:568
  259.5 9.9 %pick_far.1 = f32[32,32,8,128]{3,2,1,0:T(8,128)} custom-call(s32[32,8,8]{2,1,0:T(8,128)} %copy.23.tile_list, f32[8,32,8,128]{3,2,1,0:T(8,128)} %get-tuple-element.33.refs_0_, f32[8,224,8,128]{3,2,1,0:T(8,128)} %filter_cycles.1.refs_1_), custom_call_target="tpu_custom_call" | custom-call | bytes 12582912 | tf_op jit(solution)/shard_map/pick_far/pallas_call | solution.py:232
  269.3 7.7 %pick_own.1 = (f32[4,32,8,128]{3,2,1,0:T(8,128)}, f32[4,32,8,128]{3,2,1,0:T(8,128)}, f32[4,32,8,128]{3,2,1,0:T(8,128)}, f32[4,32,8,128]{3,2,1,0:T(8,128)}) custom-call(s32[5]{0:T(128)} %stack.105.place, s32[32,8,8]{2,1,0:T(8,128)} %copy.23.tile_list, f32[8,32,8,128]{3,2,1,0:T(8,128)} %get-tuple-element.33.refs_0_, f32[8,224,8,128]{3,2,1,0:T(8,128)} %filter_cycles.1.refs_1_), custom_call_target="tpu_custom_call" | custom-call | bytes 10485760 | tf_op jit(solution)/shard_map/pick_own/pallas_call | solution.py:272
  280.0 11.9 %collective-permute-done.2 = f32[4,32,8,128]{3,2,1,0:T(8,128)S(1)} collective-permute-done((f32[4,32,8,128]{3,2,1,0:T(8,128)}, f32[4,32,8,128]{3,2,1,0:T(8,128)S(1)}, u32[]{:S(2)}, u32[]{:S(2)}) %collective-permute-start.2) | collective-permute-done | bytes 524320 | tf_op jit(solution)/shard_map/ppermute | solution.py:581
  291.9 10.4 %collective-permute-done.3 = f32[4,32,8,128]{3,2,1,0:T(8,128)S(1)} collective-permute-done((f32[4,32,8,128]{3,2,1,0:T(8,128)}, f32[4,32,8,128]{3,2,1,0:T(8,128)S(1)}, u32[]{:S(2)}, u32[]{:S(2)}) %collective-permute-start.3) | collective-permute-done | bytes 524320 | tf_op jit(solution)/shard_map/ppermute | solution.py:581
  306.8 23.3 %collective-permute-done.4 = f32[4,32,8,128]{3,2,1,0:T(8,128)S(1)} collective-permute-done((f32[4,32,8,128]{3,2,1,0:T(8,128)S(1)}, f32[4,32,8,128]{3,2,1,0:T(8,128)S(1)}, u32[]{:S(2)}, u32[]{:S(2)}) %collective-permute-start.4) | collective-permute-done | bytes 524320 | tf_op jit(solution)/shard_map/ppermute | solution.py:581
  330.1 59.9 %collective-permute-done.5 = f32[4,32,8,128]{3,2,1,0:T(8,128)S(1)} collective-permute-done((f32[4,32,8,128]{3,2,1,0:T(8,128)S(1)}, f32[4,32,8,128]{3,2,1,0:T(8,128)S(1)}, u32[]{:S(2)}, u32[]{:S(2)}) %collective-permute-start.5) | collective-permute-done | bytes 524320 | tf_op jit(solution)/shard_map/ppermute | solution.py:581
  390.0 9.3 %collective-permute-done.6 = f32[4,32,8,128]{3,2,1,0:T(8,128)S(1)} collective-permute-done((f32[4,32,8,128]{3,2,1,0:T(8,128)S(1)}, f32[4,32,8,128]{3,2,1,0:T(8,128)S(1)}, u32[]{:S(2)}, u32[]{:S(2)}) %collective-permute-start.6) | collective-permute-done | bytes 524320 | tf_op jit(solution)/shard_map/ppermute | solution.py:581
  400.6 12.4 %read_back.3.rest_4_ = f32[64,1024]{1,0:T(8,128)} custom-call(s32[3]{0:T(128)} %pad_add_fusion.2.begin, f32[64,8,1024]{2,1,0:T(8,128)} %bitcast.56, f32[64,8,1024]{2,1,0:T(8,128)} %bitcast.61, s32[64,1024]{1,0:T(8,128)} %bitcast.68, s32[64,1024]{1,0:T(8,128)} %bitcast.73, f32[16,32,8,128]{3,2,1,0:T(8,128)} %copy-done.5), custom_call_target="tpu_custom_call" | custom-call | flops 6442450944 | bytes 4587520 | tf_op jit(solution)/shard_map/read_back/pallas_call | solution.py:189
  418.5 10.5 %all-to-all-start.4 = ((f32[32,32,8,128]{3,2,1,0:T(8,128)}), f32[32,32,8,128]{3,2,1,0:T(8,128)}, u32[]{:S(2)}, u32[]{:S(2)}) async-start(f32[32,32,8,128]{3,2,1,0:T(8,128)} %pick_far.1), calls=%async_computation.4 | async-start | bytes 8388608 | tf_op jit(solution)/shard_map/all_to_all | solution.py:568
  430.2 7.0 %pick_near.1 = (f32[8,4,8,128]{3,2,1,0:T(8,128)}, f32[8,4,8,128]{3,2,1,0:T(8,128)}, f32[8,4,8,128]{3,2,1,0:T(8,128)}, f32[8,4,8,128]{3,2,1,0:T(8,128)}, f32[8,4,...) custom-call(s32[5]{0:T(128)} %stack.105.place, ...), custom_call_target="tpu_custom_call" | custom-call | bytes 12582912 | tf_op jit(solution)/shard_map/pick_near/pallas_call | solution.py:308
  442.3 16.4 %collective-permute-done = f32[8,4,8,128]{3,2,1,0:T(8,128)S(1)} collective-permute-done((f32[8,4,8,128]{3,2,1,0:T(8,128)}, f32[8,4,8,128]{3,2,1,0:T(8,128)S(1)}, u32[]{:S(2)}, u32[]{:S(2)}) %collective-permute-start) | collective-permute-done | bytes 131104 | tf_op jit(solution)/shard_map/ppermute | solution.py:612
  462.8 10.1 %merge_rows.3 = f32[256,8,1024]{2,1,0:T(8,128)} custom-call(f32[8,224,8,128]{3,2,1,0:T(8,128)} %all-to-all-done.3.refs_1_.arrived, f32[256,8,1024]{2,1,0:T(8,128)} %merge_rows.2.rest_0_), custom_call_target="tpu_custom_call", output_to_operand_aliasing={{}: (1, {})} | custom-call | bytes 14680064 | tf_op jit(solution)/shard_map/merge_rows/pallas_call | solution.py:334
  482.1 9.2 %collective-permute-start.17 = (f32[8,4,8,128]{3,2,1,0:T(8,128)S(1)}, f32[8,4,8,128]{3,2,1,0:T(8,128)S(1)}, u32[]{:S(2)}, u32[]{:S(2)}) collective-permute-start(f32[8,4,8,128]{3,2,1,0:T(8,128)S(1)} %copy-done.9), channel_id=1, source_target_pairs={{0,12},{1,13},{2,14},{3,15},{4,8},{5,9},{6,10},{7,11},{8,4},{9,5},... | collective-permute-start | bytes 393224 | tf_op jit(solution)/shard_map/ppermute | solution.py:612
  491.3 10.4 %collective-permute-done.13 = f32[8,4,8,128]{3,2,1,0:T(8,128)S(1)} collective-permute-done((f32[8,4,8,128]{3,2,1,0:T(8,128)S(1)}, f32[8,4,8,128]{3,2,1,0:T(8,128)S(1)}, u32[]{:S(2)}, u32[]{:S(2)}) %collective-permute-start.13) | collective-permute-done | bytes 131104 | tf_op jit(solution)/shard_map/ppermute | solution.py:612
  524.6 12.0 %read_back.4.rest_1_ = f32[64,1024]{1,0:T(8,128)} custom-call(s32[3]{0:T(128)} %pad_add_fusion.1.begin, f32[64,8,1024]{2,1,0:T(8,128)} %bitcast.57, f32[64,8,1024]{2,1,0:T(8,128)} %bitcast.62, s32[64,1024]{1,0:T(8,128)} %bitcast.69, s32[64,1024]{1,0:T(8,128)} %bitcast.74, f32[16,8,4,8,128]{4,3,2,1,0:T(8,128)} %copy-done.4, ...), custom_call_target="tpu_custom_call", output_to_operand_aliasing={{}: (9, {})} | custom-call | flops 6442450944 | bytes 4587520 | tf_op jit(solution)/shard_map/read_back/pallas_call | solution.py:189
  536.6 12.1 %read_back.5 = f32[64,1024]{1,0:T(8,128)} custom-call(s32[3]{0:T(128)} %add_add_fusion.begin, f32[64,8,1024]{2,1,0:T(8,128)} %bitcast.58, f32[64,8,1024]{2,1,0:T(8,128)} %bitcast.63, s32[64,1024]{1,0:T(8,128)} %bitcast.70, s32[64,1024]{1,0:T(8,128)} %bitcast.75, f32[8,4,32,8,128]{4,3,2,1,0:T(8,128)} %bitcast.14.rest_0_, ...), custom_call_target="tpu_custom_call", output_to_operand_aliasing={{}: (6, {})} | custom-call | flops 12884901888 | bytes 6684672 | tf_op jit(solution)/shard_map/read_back/pallas_call | solution.py:189
  (108 shorter events, 69.7 us)
Async XLA Ops:
  6.3 35.0 %all-to-all-start = ((f32[32,8,8,128]{3,2,1,0:T(8,128)}), f32[32,8,8,128]{3,2,1,0:T(8,128)S(1)}, u32[]{:S(2)}, u32[]{:S(2)}) async-start(f32[32,8,8,128]{3,2,1,0:T(8,128)} %bitcast.51), calls=%async_computation | async-start | bytes 2097152 | tf_op jit(solution)/shard_map/all_to_all | solution.py:568
  42.3 169.1 %all-to-all-start.1 = ((f32[32,56,8,128]{3,2,1,0:T(8,128)}), f32[32,56,8,128]{3,2,1,0:T(8,128)}, u32[]{:S(2)}, u32[]{:S(2)}) async-start(f32[32,56,8,128]{3,2,1,0:T(8,128)} %bitcast.50), calls=%async_computation.1 | async-start | bytes 14680064 | tf_op jit(solution)/shard_map/all_to_all | solution.py:568
  223.5 29.3 %all-to-all-start.2 = ((f32[8,32,8,128]{3,2,1,0:T(8,128)}), f32[8,32,8,128]{3,2,1,0:T(8,128)S(1)}, u32[]{:S(2)}, u32[]{:S(2)}) async-start(f32[8,32,8,128]{3,2,1,0:T(8,128)} %get-tuple-element.33.refs_0_), calls=%async_computation.2 | async-start | bytes 2097152 | tf_op jit(solution)/shard_map/all_to_all | solution.py:568
  253.8 164.7 %all-to-all-start.3 = ((f32[8,224,8,128]{3,2,1,0:T(8,128)}), f32[8,224,8,128]{3,2,1,0:T(8,128)}, u32[]{:S(2)}, u32[]{:S(2)}) async-start(f32[8,224,8,128]{3,2,1,0:T(8,128)} %filter_cycles.1.refs_1_), calls=%async_computation.3 | async-start | bytes 14680064 | tf_op jit(solution)/shard_map/all_to_all | solution.py:568
  277.0 14.9 %collective-permute-start.2 = (f32[4,32,8,128]{3,2,1,0:T(8,128)}, f32[4,32,8,128]{3,2,1,0:T(8,128)S(1)}, u32[]{:S(2)}, u32[]{:S(2)}) collective-permute-start(f32[4,32,8,128]{3,2,1,0:T(8,128)} %get-tuple-element.36), channel_id=1, source_target_pairs={{0,2},{1,3},{2,0},{3,1},{4,6},{5,7},{6,4},{7,5},{8,10},{9,11},{10,... | collective-permute-start | bytes 1572872 | tf_op jit(solution)/shard_map/ppermute | solution.py:581
  277.1 25.2 %collective-permute-start.3 = (f32[4,32,8,128]{3,2,1,0:T(8,128)}, f32[4,32,8,128]{3,2,1,0:T(8,128)S(1)}, u32[]{:S(2)}, u32[]{:S(2)}) collective-permute-start(f32[4,32,8,128]{3,2,1,0:T(8,128)} %get-tuple-element.37), channel_id=1, source_target_pairs={{0,3},{1,2},{2,1},{3,0},{4,7},{5,6},{6,5},{7,4},{8,11},{9,10},{10,... | collective-permute-start | bytes 1572872 | tf_op jit(solution)/shard_map/ppermute | solution.py:581
  302.5 27.6 %collective-permute-start.4 = (f32[4,32,8,128]{3,2,1,0:T(8,128)S(1)}, f32[4,32,8,128]{3,2,1,0:T(8,128)S(1)}, u32[]{:S(2)}, u32[]{:S(2)}) collective-permute-start(f32[4,32,8,128]{3,2,1,0:T(8,128)S(1)} %pad_maximum_fusion), channel_id=1, source_target_pairs={{0,4},{4,0},{8,12},{12,8},{1,5},{5,1},{9,13},{13,9},{2,6},{6,2},{1... | collective-permute-start | bytes 1572872 | tf_op jit(solution)/shard_map/ppermute | solution.py:581
  304.3 85.7 %collective-permute-start.5 = (f32[4,32,8,128]{3,2,1,0:T(8,128)S(1)}, f32[4,32,8,128]{3,2,1,0:T(8,128)S(1)}, u32[]{:S(2)}, u32[]{:S(2)}) collective-permute-start(f32[4,32,8,128]{3,2,1,0:T(8,128)S(1)} %pad_maximum_fusion.1), channel_id=1, source_target_pairs={{0,8},{4,12},{8,0},{12,4},{1,9},{5,13},{9,1},{13,5},{2,10},{6,14},... | collective-permute-start | bytes 1572872 | tf_op jit(solution)/shard_map/ppermute | solution.py:581
  305.8 93.4 %collective-permute-start.6 = (f32[4,32,8,128]{3,2,1,0:T(8,128)S(1)}, f32[4,32,8,128]{3,2,1,0:T(8,128)S(1)}, u32[]{:S(2)}, u32[]{:S(2)}) collective-permute-start(f32[4,32,8,128]{3,2,1,0:T(8,128)S(1)} %pad_maximum_fusion.2), channel_id=1, source_target_pairs={{0,12},{4,8},{8,4},{12,0},{1,13},{5,9},{9,5},{13,1},{2,14},{6,10},... | collective-permute-start | bytes 1572872 | tf_op jit(solution)/shard_map/ppermute | solution.py:581
  418.5 118.1 %all-to-all-start.4 = ((f32[32,32,8,128]{3,2,1,0:T(8,128)}), f32[32,32,8,128]{3,2,1,0:T(8,128)}, u32[]{:S(2)}, u32[]{:S(2)}) async-start(f32[32,32,8,128]{3,2,1,0:T(8,128)} %pick_far.1), calls=%async_computation.4 | async-start | bytes 8388608 | tf_op jit(solution)/shard_map/all_to_all | solution.py:568
  437.2 21.6 %collective-permute-start = (f32[8,4,8,128]{3,2,1,0:T(8,128)}, f32[8,4,8,128]{3,2,1,0:T(8,128)S(1)}, u32[]{:S(2)}, u32[]{:S(2)}) collective-permute-start(f32[8,4,8,128]{3,2,1,0:T(8,128)} %get-tuple-element.31), channel_id=1, source_target_pairs={{0,5},{1,4},{2,7},{3,6},{4,1},{5,0},{6,3},{7,2},{8,13},{9,12},{10,... | collective-permute-start | bytes 393224 | tf_op jit(solution)/shard_map/ppermute | solution.py:612
  438.6 34.3 %collective-permute-start.7 = (f32[8,4,8,128]{3,2,1,0:T(8,128)}, f32[8,4,8,128]{3,2,1,0:T(8,128)S(1)}, u32[]{:S(2)}, u32[]{:S(2)}) collective-permute-start(f32[8,4,8,128]{3,2,1,0:T(8,128)} %get-tuple-element.40), channel_id=1, source_target_pairs={{0,1},{1,0},{2,3},{3,2},{4,5},{5,4},{6,7},{7,6},{8,9},{9,8},{10,11... | collective-permute-start | bytes 393224 | tf_op jit(solution)/shard_map/ppermute | solution.py:612
  439.5 33.6 %collective-permute-start.8 = (f32[8,4,8,128]{3,2,1,0:T(8,128)}, f32[8,4,8,128]{3,2,1,0:T(8,128)S(1)}, u32[]{:S(2)}, u32[]{:S(2)}) collective-permute-start(f32[8,4,8,128]{3,2,1,0:T(8,128)} %get-tuple-element.41), channel_id=1, source_target_pairs={{0,2},{1,3},{2,0},{3,1},{4,6},{5,7},{6,4},{7,5},{8,10},{9,11},{10,... | collective-permute-start | bytes 393224 | tf_op jit(solution)/shard_map/ppermute | solution.py:612
  440.5 32.7 %collective-permute-start.9 = (f32[8,4,8,128]{3,2,1,0:T(8,128)}, f32[8,4,8,128]{3,2,1,0:T(8,128)S(1)}, u32[]{:S(2)}, u32[]{:S(2)}) collective-permute-start(f32[8,4,8,128]{3,2,1,0:T(8,128)} %get-tuple-element.42), channel_id=1, source_target_pairs={{0,3},{1,2},{2,1},{3,0},{4,7},{5,6},{6,5},{7,4},{8,11},{9,10},{10,... | collective-permute-start | bytes 393224 | tf_op jit(solution)/shard_map/ppermute | solution.py:612
  440.9 34.0 %collective-permute-start.10 = (f32[8,4,8,128]{3,2,1,0:T(8,128)}, f32[8,4,8,128]{3,2,1,0:T(8,128)S(1)}, u32[]{:S(2)}, u32[]{:S(2)}) collective-permute-start(f32[8,4,8,128]{3,2,1,0:T(8,128)} %get-tuple-element.43), channel_id=1, source_target_pairs={{0,4},{1,5},{2,6},{3,7},{4,0},{5,1},{6,2},{7,3},{8,12},{9,13},{10,... | collective-permute-start | bytes 393224 | tf_op jit(solution)/shard_map/ppermute | solution.py:612
  458.8 19.7 %collective-permute-start.11 = (f32[8,4,8,128]{3,2,1,0:T(8,128)}, f32[8,4,8,128]{3,2,1,0:T(8,128)S(1)}, u32[]{:S(2)}, u32[]{:S(2)}) collective-permute-start(f32[8,4,8,128]{3,2,1,0:T(8,128)} %get-tuple-element.44), channel_id=1, source_target_pairs={{0,6},{1,7},{2,4},{3,5},{4,2},{5,3},{6,0},{7,1},{8,14},{9,15},{10,... | collective-permute-start | bytes 393224 | tf_op jit(solution)/shard_map/ppermute | solution.py:612
  473.1 28.6 %collective-permute-start.13 = (f32[8,4,8,128]{3,2,1,0:T(8,128)S(1)}, f32[8,4,8,128]{3,2,1,0:T(8,128)S(1)}, u32[]{:S(2)}, u32[]{:S(2)}) collective-permute-start(f32[8,4,8,128]{3,2,1,0:T(8,128)S(1)} %copy-done.13), channel_id=1, source_target_pairs={{0,8},{1,9},{2,10},{3,11},{4,12},{5,13},{6,14},{7,15},{8,0},{9,1},... | collective-permute-start | bytes 393224 | tf_op jit(solution)/shard_map/ppermute | solution.py:612
  473.2 31.3 %collective-permute-start.14 = (f32[8,4,8,128]{3,2,1,0:T(8,128)S(1)}, f32[8,4,8,128]{3,2,1,0:T(8,128)S(1)}, u32[]{:S(2)}, u32[]{:S(2)}) collective-permute-start(f32[8,4,8,128]{3,2,1,0:T(8,128)S(1)} %copy-done.12), channel_id=1, source_target_pairs={{0,9},{1,8},{2,11},{3,10},{4,13},{5,12},{6,15},{7,14},{8,1},{9,0},... | collective-permute-start | bytes 393224 | tf_op jit(solution)/shard_map/ppermute | solution.py:612
  474.9 33.0 %collective-permute-start.15 = (f32[8,4,8,128]{3,2,1,0:T(8,128)S(1)}, f32[8,4,8,128]{3,2,1,0:T(8,128)S(1)}, u32[]{:S(2)}, u32[]{:S(2)}) collective-permute-start(f32[8,4,8,128]{3,2,1,0:T(8,128)S(1)} %copy-done.11), channel_id=1, source_target_pairs={{0,10},{1,11},{2,8},{3,9},{4,14},{5,15},{6,12},{7,13},{8,2},{9,3},... | collective-permute-start | bytes 393224 | tf_op jit(solution)/shard_map/ppermute | solution.py:612
  478.4 31.7 %collective-permute-start.16 = (f32[8,4,8,128]{3,2,1,0:T(8,128)S(1)}, f32[8,4,8,128]{3,2,1,0:T(8,128)S(1)}, u32[]{:S(2)}, u32[]{:S(2)}) collective-permute-start(f32[8,4,8,128]{3,2,1,0:T(8,128)S(1)} %copy-done.10), channel_id=1, source_target_pairs={{0,11},{1,10},{2,9},{3,8},{4,15},{5,14},{6,13},{7,12},{8,3},{9,2},... | collective-permute-start | bytes 393224 | tf_op jit(solution)/shard_map/ppermute | solution.py:612
  482.1 30.8 %collective-permute-start.17 = (f32[8,4,8,128]{3,2,1,0:T(8,128)S(1)}, f32[8,4,8,128]{3,2,1,0:T(8,128)S(1)}, u32[]{:S(2)}, u32[]{:S(2)}) collective-permute-start(f32[8,4,8,128]{3,2,1,0:T(8,128)S(1)} %copy-done.9), channel_id=1, source_target_pairs={{0,12},{1,13},{2,14},{3,15},{4,8},{5,9},{6,10},{7,11},{8,4},{9,5},... | collective-permute-start | bytes 393224 | tf_op jit(solution)/shard_map/ppermute | solution.py:612
  501.7 15.3 %collective-permute-start.18 = (f32[8,4,8,128]{3,2,1,0:T(8,128)S(1)}, f32[8,4,8,128]{3,2,1,0:T(8,128)S(1)}, u32[]{:S(2)}, u32[]{:S(2)}) collective-permute-start(f32[8,4,8,128]{3,2,1,0:T(8,128)S(1)} %copy-done.8), channel_id=1, source_target_pairs={{0,13},{1,12},{2,15},{3,14},{4,9},{5,8},{6,11},{7,10},{8,5},{9,4},... | collective-permute-start | bytes 393224 | tf_op jit(solution)/shard_map/ppermute | solution.py:612
  504.5 16.6 %collective-permute-start.19 = (f32[8,4,8,128]{3,2,1,0:T(8,128)S(1)}, f32[8,4,8,128]{3,2,1,0:T(8,128)S(1)}, u32[]{:S(2)}, u32[]{:S(2)}) collective-permute-start(f32[8,4,8,128]{3,2,1,0:T(8,128)S(1)} %copy-done.7), channel_id=1, source_target_pairs={{0,14},{1,15},{2,12},{3,13},{4,10},{5,11},{6,8},{7,9},{8,6},{9,7},... | collective-permute-start | bytes 393224 | tf_op jit(solution)/shard_map/ppermute | solution.py:612
  507.9 15.3 %collective-permute-start.20 = (f32[8,4,8,128]{3,2,1,0:T(8,128)S(1)}, f32[8,4,8,128]{3,2,1,0:T(8,128)S(1)}, u32[]{:S(2)}, u32[]{:S(2)}) collective-permute-start(f32[8,4,8,128]{3,2,1,0:T(8,128)S(1)} %copy-done.6), channel_id=1, source_target_pairs={{0,15},{1,14},{2,13},{3,12},{4,11},{5,10},{6,9},{7,8},{8,7},{9,6},... | collective-permute-start | bytes 393224 | tf_op jit(solution)/shard_map/ppermute | solution.py:612
  (17 other events, 243.2 us)

commit v8 on v7

--- a/solution.py
+++ b/solution.py
@@ -606,7 +606,7 @@
     own = [jnp.concatenate(own)]
     gradient = read_points(points, begin_at(half, half), near_slots, own, whole_specs_at(own), TR // 2, own_rows, None)
     whole = merge_rows(early_share, 0, cycle_blocks, None)
-    far_tiles = exchange(after(far, late_share, gradient, whole), AXES)
+    far_tiles = exchange(after(far, late_share, gradient), AXES)
     near = list(pick_near([early_share, late_share], place, tile_list))
     for d in range(1, blocks // 2):
         near[d] = lax.ppermute(near[d], AXES[1:], [(i, i ^ d) for i in range(blocks // 2)])

time: 553 us -> 553 us (level)
  no operation moved by 1% of the time
where the time goes in v8:
time: 553 us; the launch traced here: 549 us
  waiting for transfers between devices  332 us (60%)
  Pallas kernels  137 us (25%)
  starting transfers between devices  66.7 us (12%)
  local copies, waits for them, and re-layouts  8.87 us (2%)
    all_to_all x5, waiting for transfers between devices, exchange(): return lax.all_to_all(x, axes, 0, 0, tiled=True)  174 us
    ppermute x6, waiting for transfers between devices, step(): return lax.ppermute(x, axis, [(i, i ^ d) for i in range(size)]) if d else x  115 us
    ppermute x15, waiting for transfers between devices, row_owner_plan(): lax.ppermute(near[d], AXES[1:], [(i, i ^ d) for i in range(blocks // 2)])  43.1 us
    pallas_call x3, Pallas kernels, read_points(): pl.pallas_call(functools.partial(read_kernel, len(tile_specs), cycles, pl...  36.5 us
    pallas_call x2, Pallas kernels, spread_tiles(): pl.pallas_call(spread_kernel, grid=(slots // STEP_SLOTS,), in_specs=point...  33.3 us
    all_to_all x5, starting transfers between devices, exchange(): return lax.all_to_all(x, axes, 0, 0, tiled=True)  32.3 us
    ppermute x15, starting transfers between devices, row_owner_plan(): lax.ppermute(near[d], AXES[1:], [(i, i ^ d) for i in range(blocks // 2)])  28.8 us
    pallas_call x1, Pallas kernels, filter_cycles(): pl.pallas_call(filter_kernel, grid=(blocks // FILTER_STEP,), in_specs=who...  18.1 us
  transfers between devices with their start and end apart: 26, of which 17 were waited for; matrix products, arithmetic and copies ran while one was open for 1% of the time, Pallas kernels for 20%

profile of v8, /device:TPU:0, one launch (start us, length us, event | category | flops | bytes accessed | tf_op | source)
XLA Modules:
  0.0 548.7 jit_solution(4706046319245755242)
XLA Ops:
  0.6 5.7 %spread.2 = f32[8,4,1,8,8,128]{5,4,3,2,1,0:T(8,128)} custom-call(f32[64,1024]{1,0:T(8,128)} %bitcast.64, f32[64,8,1024]{2,1,0:T(8,128)} %bitcast.54, f32[64,8,1024]{2,1,0:T(8,128)} %bitcast.59, s32[64,1024]{1,0:T(8,128)} %bitcast.66, s32[64,1024]{1,0:T(8,128)} %bitcast.71), custom_call_target="tpu_custom_call" | custom-call | flops 3221225472 | bytes 1671168 | tf_op jit(solution)/shard_map/spread/pallas_call | solution.py:137
  6.3 7.3 %all-to-all-start = ((f32[32,8,8,128]{3,2,1,0:T(8,128)}), f32[32,8,8,128]{3,2,1,0:T(8,128)S(1)}, u32[]{:S(2)}, u32[]{:S(2)}) async-start(f32[32,8,8,128]{3,2,1,0:T(8,128)} %bitcast.51), calls=%async_computation | async-start | bytes 2097152 | tf_op jit(solution)/shard_map/all_to_all | solution.py:568
  13.6 27.7 %spread.3 = f32[8,4,1,56,8,128]{5,4,3,2,1,0:T(8,128)} custom-call(f32[64,1024]{1,0:T(8,128)} %bitcast.65, f32[64,8,1024]{2,1,0:T(8,128)} %bitcast.55, f32[64,8,1024]{2,1,0:T(8,128)} %bitcast.60, s32[64,1024]{1,0:T(8,128)} %bitcast.67, s32[64,1024]{1,0:T(8,128)} %bitcast.72), custom_call_target="tpu_custom_call" | custom-call | flops 22548578304 | bytes 11698176 | tf_op jit(solution)/shard_map/spread/pallas_call | solution.py:137
  42.3 5.9 %all-to-all-start.1 = ((f32[32,56,8,128]{3,2,1,0:T(8,128)}), f32[32,56,8,128]{3,2,1,0:T(8,128)}, u32[]{:S(2)}, u32[]{:S(2)}) async-start(f32[32,56,8,128]{3,2,1,0:T(8,128)} %bitcast.50), calls=%async_computation.1 | async-start | bytes 14680064 | tf_op jit(solution)/shard_map/all_to_all | solution.py:568
  50.2 161.2 %all-to-all-done.1.refs_1_ = f32[32,56,8,128]{3,2,1,0:T(8,128)} async-done(((f32[32,56,8,128]{3,2,1,0:T(8,128)}), f32[32,56,8,128]{3,2,1,0:T(8,128)}, u32[]{:S(2)}, u32[]{:S(2)}) %all-to-all-start.1) | async-done | bytes 7340064 | tf_op jit(solution)/shard_map/all_to_all | solution.py:568
  211.4 12.1 %collect_filter.1 = (f32[8,32,8,128]{3,2,1,0:T(8,128)}, f32[224,8,8,128]{3,2,1,0:T(8,128)}) custom-call(s32[32,8,8]{2,1,0:T(8,128)} %copy.23.tile_list, f32[32,8,8,128]{3,2,1,0:T(8,128)} %copy-done.1, f32[32,56,8,128]{3,2,1,0:T(8,128)} %all-to-all-done.1.refs_1_, bf16[128,384]{1,0:T(8,128)(2,1)} %constant.33.clone.refs_2_.refs_0_, ...), custom_call_target="tpu_custom_call" | custom-call | flops 3623878656 | bytes 6291456 | tf_op jit(solution)/shard_map/collect_filter/pallas_call | solution.py:514
  227.1 18.1 %filter_cycles.1.refs_1_ = f32[8,224,8,128]{3,2,1,0:T(8,128)} custom-call(bf16[128,384]{1,0:T(8,128)(2,1)} %constant.33.clone.refs_2_.refs_0_, bf16[128,384]{1,0:T(8,128)(2,1)} %constant.34.clone.refs_3_.refs_1_, bf16[768,256]{1,0:T(8,128)(2,1)} %constant.35.clone.refs_4_.refs_2_, bf16[768,256]{1,0:T(8,128)(2,1)} %constant.36.clone.refs_5_.refs_3_, ...), custom_call_target="tpu_custom_call" | custom-call | flops 8455716864 | bytes 14680064 | tf_op jit(solution)/shard_map/filter_cycles/pallas_call | solution.py:450
  245.2 7.6 %all-to-all-done.2.refs_0_.arrived = f32[8,32,8,128]{3,2,1,0:T(8,128)S(1)} async-done(((f32[8,32,8,128]{3,2,1,0:T(8,128)}), f32[8,32,8,128]{3,2,1,0:T(8,128)S(1)}, u32[]{:S(2)}, u32[]{:S(2)}) %all-to-all-start.2) | async-done | bytes 1048608 | tf_op jit(solution)/shard_map/all_to_all | solution.py:568
  259.5 9.9 %pick_far.1 = f32[32,32,8,128]{3,2,1,0:T(8,128)} custom-call(s32[32,8,8]{2,1,0:T(8,128)} %copy.23.tile_list, f32[8,32,8,128]{3,2,1,0:T(8,128)} %get-tuple-element.33.refs_0_, f32[8,224,8,128]{3,2,1,0:T(8,128)} %filter_cycles.1.refs_1_), custom_call_target="tpu_custom_call" | custom-call | bytes 12582912 | tf_op jit(solution)/shard_map/pick_far/pallas_call | solution.py:232
  269.3 7.7 %pick_own.1 = (f32[4,32,8,128]{3,2,1,0:T(8,128)}, f32[4,32,8,128]{3,2,1,0:T(8,128)}, f32[4,32,8,128]{3,2,1,0:T(8,128)}, f32[4,32,8,128]{3,2,1,0:T(8,128)}) custom-call(s32[5]{0:T(128)} %stack.105.place, s32[32,8,8]{2,1,0:T(8,128)} %copy.23.tile_list, f32[8,32,8,128]{3,2,1,0:T(8,128)} %get-tuple-element.33.refs_0_, f32[8,224,8,128]{3,2,1,0:T(8,128)} %filter_cycles.1.refs_1_), custom_call_target="tpu_custom_call" | custom-call | bytes 10485760 | tf_op jit(solution)/shard_map/pick_own/pallas_call | solution.py:272
  280.0 11.9 %collective-permute-done.2 = f32[4,32,8,128]{3,2,1,0:T(8,128)S(1)} collective-permute-done((f32[4,32,8,128]{3,2,1,0:T(8,128)}, f32[4,32,8,128]{3,2,1,0:T(8,128)S(1)}, u32[]{:S(2)}, u32[]{:S(2)}) %collective-permute-start.2) | collective-permute-done | bytes 524320 | tf_op jit(solution)/shard_map/ppermute | solution.py:581
  291.9 10.4 %collective-permute-done.3 = f32[4,32,8,128]{3,2,1,0:T(8,128)S(1)} collective-permute-done((f32[4,32,8,128]{3,2,1,0:T(8,128)}, f32[4,32,8,128]{3,2,1,0:T(8,128)S(1)}, u32[]{:S(2)}, u32[]{:S(2)}) %collective-permute-start.3) | collective-permute-done | bytes 524320 | tf_op jit(solution)/shard_map/ppermute | solution.py:581
  306.8 23.3 %collective-permute-done.4 = f32[4,32,8,128]{3,2,1,0:T(8,128)S(1)} collective-permute-done((f32[4,32,8,128]{3,2,1,0:T(8,128)S(1)}, f32[4,32,8,128]{3,2,1,0:T(8,128)S(1)}, u32[]{:S(2)}, u32[]{:S(2)}) %collective-permute-start.4) | collective-permute-done | bytes 524320 | tf_op jit(solution)/shard_map/ppermute | solution.py:581
  330.1 59.9 %collective-permute-done.5 = f32[4,32,8,128]{3,2,1,0:T(8,128)S(1)} collective-permute-done((f32[4,32,8,128]{3,2,1,0:T(8,128)S(1)}, f32[4,32,8,128]{3,2,1,0:T(8,128)S(1)}, u32[]{:S(2)}, u32[]{:S(2)}) %collective-permute-start.5) | collective-permute-done | bytes 524320 | tf_op jit(solution)/shard_map/ppermute | solution.py:581
  390.0 9.3 %collective-permute-done.6 = f32[4,32,8,128]{3,2,1,0:T(8,128)S(1)} collective-permute-done((f32[4,32,8,128]{3,2,1,0:T(8,128)S(1)}, f32[4,32,8,128]{3,2,1,0:T(8,128)S(1)}, u32[]{:S(2)}, u32[]{:S(2)}) %collective-permute-start.6) | collective-permute-done | bytes 524320 | tf_op jit(solution)/shard_map/ppermute | solution.py:581
  400.6 12.4 %read_back.3.rest_4_ = f32[64,1024]{1,0:T(8,128)} custom-call(s32[3]{0:T(128)} %pad_add_fusion.2.begin, f32[64,8,1024]{2,1,0:T(8,128)} %bitcast.56, f32[64,8,1024]{2,1,0:T(8,128)} %bitcast.61, s32[64,1024]{1,0:T(8,128)} %bitcast.68, s32[64,1024]{1,0:T(8,128)} %bitcast.73, f32[16,32,8,128]{3,2,1,0:T(8,128)} %copy-done.5), custom_call_target="tpu_custom_call" | custom-call | flops 6442450944 | bytes 4587520 | tf_op jit(solution)/shard_map/read_back/pallas_call | solution.py:189
  418.5 10.5 %all-to-all-start.4 = ((f32[32,32,8,128]{3,2,1,0:T(8,128)}), f32[32,32,8,128]{3,2,1,0:T(8,128)}, u32[]{:S(2)}, u32[]{:S(2)}) async-start(f32[32,32,8,128]{3,2,1,0:T(8,128)} %pick_far.1), calls=%async_computation.4 | async-start | bytes 8388608 | tf_op jit(solution)/shard_map/all_to_all | solution.py:568
  432.9 7.0 %pick_near.1 = (f32[8,4,8,128]{3,2,1,0:T(8,128)}, f32[8,4,8,128]{3,2,1,0:T(8,128)}, f32[8,4,8,128]{3,2,1,0:T(8,128)}, f32[8,4,8,128]{3,2,1,0:T(8,128)}, f32[8,4,...) custom-call(s32[5]{0:T(128)} %stack.105.place, ...), custom_call_target="tpu_custom_call" | custom-call | bytes 12582912 | tf_op jit(solution)/shard_map/pick_near/pallas_call | solution.py:308
  445.0 14.1 %collective-permute-done = f32[8,4,8,128]{3,2,1,0:T(8,128)S(1)} collective-permute-done((f32[8,4,8,128]{3,2,1,0:T(8,128)}, f32[8,4,8,128]{3,2,1,0:T(8,128)S(1)}, u32[]{:S(2)}, u32[]{:S(2)}) %collective-permute-start) | collective-permute-done | bytes 131104 | tf_op jit(solution)/shard_map/ppermute | solution.py:612
  462.8 10.1 %merge_rows.3 = f32[256,8,1024]{2,1,0:T(8,128)} custom-call(f32[8,224,8,128]{3,2,1,0:T(8,128)} %all-to-all-done.3.refs_1_.arrived, f32[256,8,1024]{2,1,0:T(8,128)} %merge_rows.2.rest_0_), custom_call_target="tpu_custom_call", output_to_operand_aliasing={{}: (1, {})} | custom-call | bytes 14680064 | tf_op jit(solution)/shard_map/merge_rows/pallas_call | solution.py:334
  482.1 9.2 %collective-permute-start.17 = (f32[8,4,8,128]{3,2,1,0:T(8,128)S(1)}, f32[8,4,8,128]{3,2,1,0:T(8,128)S(1)}, u32[]{:S(2)}, u32[]{:S(2)}) collective-permute-start(f32[8,4,8,128]{3,2,1,0:T(8,128)S(1)} %copy-done.9), channel_id=1, source_target_pairs={{0,12},{1,13},{2,14},{3,15},{4,8},{5,9},{6,10},{7,11},{8,4},{9,5},... | collective-permute-start | bytes 393224 | tf_op jit(solution)/shard_map/ppermute | solution.py:612
  491.3 10.4 %collective-permute-done.13 = f32[8,4,8,128]{3,2,1,0:T(8,128)S(1)} collective-permute-done((f32[8,4,8,128]{3,2,1,0:T(8,128)S(1)}, f32[8,4,8,128]{3,2,1,0:T(8,128)S(1)}, u32[]{:S(2)}, u32[]{:S(2)}) %collective-permute-start.13) | collective-permute-done | bytes 131104 | tf_op jit(solution)/shard_map/ppermute | solution.py:612
  524.6 12.0 %read_back.4.rest_1_ = f32[64,1024]{1,0:T(8,128)} custom-call(s32[3]{0:T(128)} %pad_add_fusion.1.begin, f32[64,8,1024]{2,1,0:T(8,128)} %bitcast.57, f32[64,8,1024]{2,1,0:T(8,128)} %bitcast.62, s32[64,1024]{1,0:T(8,128)} %bitcast.69, s32[64,1024]{1,0:T(8,128)} %bitcast.74, f32[16,8,4,8,128]{4,3,2,1,0:T(8,128)} %copy-done.4, ...), custom_call_target="tpu_custom_call", output_to_operand_aliasing={{}: (9, {})} | custom-call | flops 6442450944 | bytes 4587520 | tf_op jit(solution)/shard_map/read_back/pallas_call | solution.py:189
  536.6 12.1 %read_back.5 = f32[64,1024]{1,0:T(8,128)} custom-call(s32[3]{0:T(128)} %add_add_fusion.begin, f32[64,8,1024]{2,1,0:T(8,128)} %bitcast.58, f32[64,8,1024]{2,1,0:T(8,128)} %bitcast.63, s32[64,1024]{1,0:T(8,128)} %bitcast.70, s32[64,1024]{1,0:T(8,128)} %bitcast.75, f32[8,4,32,8,128]{4,3,2,1,0:T(8,128)} %bitcast.14.rest_0_, ...), custom_call_target="tpu_custom_call", output_to_operand_aliasing={{}: (6, {})} | custom-call | flops 12884901888 | bytes 6684672 | tf_op jit(solution)/shard_map/read_back/pallas_call | solution.py:189
  (108 shorter events, 72.1 us)
Async XLA Ops:
  6.3 35.0 %all-to-all-start = ((f32[32,8,8,128]{3,2,1,0:T(8,128)}), f32[32,8,8,128]{3,2,1,0:T(8,128)S(1)}, u32[]{:S(2)}, u32[]{:S(2)}) async-start(f32[32,8,8,128]{3,2,1,0:T(8,128)} %bitcast.51), calls=%async_computation | async-start | bytes 2097152 | tf_op jit(solution)/shard_map/all_to_all | solution.py:568
  42.3 169.1 %all-to-all-start.1 = ((f32[32,56,8,128]{3,2,1,0:T(8,128)}), f32[32,56,8,128]{3,2,1,0:T(8,128)}, u32[]{:S(2)}, u32[]{:S(2)}) async-start(f32[32,56,8,128]{3,2,1,0:T(8,128)} %bitcast.50), calls=%async_computation.1 | async-start | bytes 14680064 | tf_op jit(solution)/shard_map/all_to_all | solution.py:568
  223.5 29.3 %all-to-all-start.2 = ((f32[8,32,8,128]{3,2,1,0:T(8,128)}), f32[8,32,8,128]{3,2,1,0:T(8,128)S(1)}, u32[]{:S(2)}, u32[]{:S(2)}) async-start(f32[8,32,8,128]{3,2,1,0:T(8,128)} %get-tuple-element.33.refs_0_), calls=%async_computation.2 | async-start | bytes 2097152 | tf_op jit(solution)/shard_map/all_to_all | solution.py:568
  253.8 164.7 %all-to-all-start.3 = ((f32[8,224,8,128]{3,2,1,0:T(8,128)}), f32[8,224,8,128]{3,2,1,0:T(8,128)}, u32[]{:S(2)}, u32[]{:S(2)}) async-start(f32[8,224,8,128]{3,2,1,0:T(8,128)} %filter_cycles.1.refs_1_), calls=%async_computation.3 | async-start | bytes 14680064 | tf_op jit(solution)/shard_map/all_to_all | solution.py:568
  277.0 14.9 %collective-permute-start.2 = (f32[4,32,8,128]{3,2,1,0:T(8,128)}, f32[4,32,8,128]{3,2,1,0:T(8,128)S(1)}, u32[]{:S(2)}, u32[]{:S(2)}) collective-permute-start(f32[4,32,8,128]{3,2,1,0:T(8,128)} %get-tuple-element.36), channel_id=1, source_target_pairs={{0,2},{1,3},{2,0},{3,1},{4,6},{5,7},{6,4},{7,5},{8,10},{9,11},{10,... | collective-permute-start | bytes 1572872 | tf_op jit(solution)/shard_map/ppermute | solution.py:581
  277.1 25.2 %collective-permute-start.3 = (f32[4,32,8,128]{3,2,1,0:T(8,128)}, f32[4,32,8,128]{3,2,1,0:T(8,128)S(1)}, u32[]{:S(2)}, u32[]{:S(2)}) collective-permute-start(f32[4,32,8,128]{3,2,1,0:T(8,128)} %get-tuple-element.37), channel_id=1, source_target_pairs={{0,3},{1,2},{2,1},{3,0},{4,7},{5,6},{6,5},{7,4},{8,11},{9,10},{10,... | collective-permute-start | bytes 1572872 | tf_op jit(solution)/shard_map/ppermute | solution.py:581
  302.5 27.6 %collective-permute-start.4 = (f32[4,32,8,128]{3,2,1,0:T(8,128)S(1)}, f32[4,32,8,128]{3,2,1,0:T(8,128)S(1)}, u32[]{:S(2)}, u32[]{:S(2)}) collective-permute-start(f32[4,32,8,128]{3,2,1,0:T(8,128)S(1)} %pad_maximum_fusion), channel_id=1, source_target_pairs={{0,4},{4,0},{8,12},{12,8},{1,5},{5,1},{9,13},{13,9},{2,6},{6,2},{1... | collective-permute-start | bytes 1572872 | tf_op jit(solution)/shard_map/ppermute | solution.py:581
  304.3 85.7 %collective-permute-start.5 = (f32[4,32,8,128]{3,2,1,0:T(8,128)S(1)}, f32[4,32,8,128]{3,2,1,0:T(8,128)S(1)}, u32[]{:S(2)}, u32[]{:S(2)}) collective-permute-start(f32[4,32,8,128]{3,2,1,0:T(8,128)S(1)} %pad_maximum_fusion.1), channel_id=1, source_target_pairs={{0,8},{4,12},{8,0},{12,4},{1,9},{5,13},{9,1},{13,5},{2,10},{6,14},... | collective-permute-start | bytes 1572872 | tf_op jit(solution)/shard_map/ppermute | solution.py:581
  305.8 93.4 %collective-permute-start.6 = (f32[4,32,8,128]{3,2,1,0:T(8,128)S(1)}, f32[4,32,8,128]{3,2,1,0:T(8,128)S(1)}, u32[]{:S(2)}, u32[]{:S(2)}) collective-permute-start(f32[4,32,8,128]{3,2,1,0:T(8,128)S(1)} %pad_maximum_fusion.2), channel_id=1, source_target_pairs={{0,12},{4,8},{8,4},{12,0},{1,13},{5,9},{9,5},{13,1},{2,14},{6,10},... | collective-permute-start | bytes 1572872 | tf_op jit(solution)/shard_map/ppermute | solution.py:581
  418.5 118.1 %all-to-all-start.4 = ((f32[32,32,8,128]{3,2,1,0:T(8,128)}), f32[32,32,8,128]{3,2,1,0:T(8,128)}, u32[]{:S(2)}, u32[]{:S(2)}) async-start(f32[32,32,8,128]{3,2,1,0:T(8,128)} %pick_far.1), calls=%async_computation.4 | async-start | bytes 8388608 | tf_op jit(solution)/shard_map/all_to_all | solution.py:568
  439.9 19.2 %collective-permute-start = (f32[8,4,8,128]{3,2,1,0:T(8,128)}, f32[8,4,8,128]{3,2,1,0:T(8,128)S(1)}, u32[]{:S(2)}, u32[]{:S(2)}) collective-permute-start(f32[8,4,8,128]{3,2,1,0:T(8,128)} %get-tuple-element.31), channel_id=1, source_target_pairs={{0,5},{1,4},{2,7},{3,6},{4,1},{5,0},{6,3},{7,2},{8,13},{9,12},{10,... | collective-permute-start | bytes 393224 | tf_op jit(solution)/shard_map/ppermute | solution.py:612
  441.4 31.5 %collective-permute-start.7 = (f32[8,4,8,128]{3,2,1,0:T(8,128)}, f32[8,4,8,128]{3,2,1,0:T(8,128)S(1)}, u32[]{:S(2)}, u32[]{:S(2)}) collective-permute-start(f32[8,4,8,128]{3,2,1,0:T(8,128)} %get-tuple-element.40), channel_id=1, source_target_pairs={{0,1},{1,0},{2,3},{3,2},{4,5},{5,4},{6,7},{7,6},{8,9},{9,8},{10,11... | collective-permute-start | bytes 393224 | tf_op jit(solution)/shard_map/ppermute | solution.py:612
  442.3 30.8 %collective-permute-start.8 = (f32[8,4,8,128]{3,2,1,0:T(8,128)}, f32[8,4,8,128]{3,2,1,0:T(8,128)S(1)}, u32[]{:S(2)}, u32[]{:S(2)}) collective-permute-start(f32[8,4,8,128]{3,2,1,0:T(8,128)} %get-tuple-element.41), channel_id=1, source_target_pairs={{0,2},{1,3},{2,0},{3,1},{4,6},{5,7},{6,4},{7,5},{8,10},{9,11},{10,... | collective-permute-start | bytes 393224 | tf_op jit(solution)/shard_map/ppermute | solution.py:612
  443.2 30.0 %collective-permute-start.9 = (f32[8,4,8,128]{3,2,1,0:T(8,128)}, f32[8,4,8,128]{3,2,1,0:T(8,128)S(1)}, u32[]{:S(2)}, u32[]{:S(2)}) collective-permute-start(f32[8,4,8,128]{3,2,1,0:T(8,128)} %get-tuple-element.42), channel_id=1, source_target_pairs={{0,3},{1,2},{2,1},{3,0},{4,7},{5,6},{6,5},{7,4},{8,11},{9,10},{10,... | collective-permute-start | bytes 393224 | tf_op jit(solution)/shard_map/ppermute | solution.py:612
  443.6 31.3 %collective-permute-start.10 = (f32[8,4,8,128]{3,2,1,0:T(8,128)}, f32[8,4,8,128]{3,2,1,0:T(8,128)S(1)}, u32[]{:S(2)}, u32[]{:S(2)}) collective-permute-start(f32[8,4,8,128]{3,2,1,0:T(8,128)} %get-tuple-element.43), channel_id=1, source_target_pairs={{0,4},{1,5},{2,6},{3,7},{4,0},{5,1},{6,2},{7,3},{8,12},{9,13},{10,... | collective-permute-start | bytes 393224 | tf_op jit(solution)/shard_map/ppermute | solution.py:612
  459.2 19.3 %collective-permute-start.11 = (f32[8,4,8,128]{3,2,1,0:T(8,128)}, f32[8,4,8,128]{3,2,1,0:T(8,128)S(1)}, u32[]{:S(2)}, u32[]{:S(2)}) collective-permute-start(f32[8,4,8,128]{3,2,1,0:T(8,128)} %get-tuple-element.44), channel_id=1, source_target_pairs={{0,6},{1,7},{2,4},{3,5},{4,2},{5,3},{6,0},{7,1},{8,14},{9,15},{10,... | collective-permute-start | bytes 393224 | tf_op jit(solution)/shard_map/ppermute | solution.py:612
  473.1 28.7 %collective-permute-start.13 = (f32[8,4,8,128]{3,2,1,0:T(8,128)S(1)}, f32[8,4,8,128]{3,2,1,0:T(8,128)S(1)}, u32[]{:S(2)}, u32[]{:S(2)}) collective-permute-start(f32[8,4,8,128]{3,2,1,0:T(8,128)S(1)} %copy-done.13), channel_id=1, source_target_pairs={{0,8},{1,9},{2,10},{3,11},{4,12},{5,13},{6,14},{7,15},{8,0},{9,1},... | collective-permute-start | bytes 393224 | tf_op jit(solution)/shard_map/ppermute | solution.py:612
  473.2 31.3 %collective-permute-start.14 = (f32[8,4,8,128]{3,2,1,0:T(8,128)S(1)}, f32[8,4,8,128]{3,2,1,0:T(8,128)S(1)}, u32[]{:S(2)}, u32[]{:S(2)}) collective-permute-start(f32[8,4,8,128]{3,2,1,0:T(8,128)S(1)} %copy-done.12), channel_id=1, source_target_pairs={{0,9},{1,8},{2,11},{3,10},{4,13},{5,12},{6,15},{7,14},{8,1},{9,0},... | collective-permute-start | bytes 393224 | tf_op jit(solution)/shard_map/ppermute | solution.py:612
  474.9 33.0 %collective-permute-start.15 = (f32[8,4,8,128]{3,2,1,0:T(8,128)S(1)}, f32[8,4,8,128]{3,2,1,0:T(8,128)S(1)}, u32[]{:S(2)}, u32[]{:S(2)}) collective-permute-start(f32[8,4,8,128]{3,2,1,0:T(8,128)S(1)} %copy-done.11), channel_id=1, source_target_pairs={{0,10},{1,11},{2,8},{3,9},{4,14},{5,15},{6,12},{7,13},{8,2},{9,3},... | collective-permute-start | bytes 393224 | tf_op jit(solution)/shard_map/ppermute | solution.py:612
  478.4 31.7 %collective-permute-start.16 = (f32[8,4,8,128]{3,2,1,0:T(8,128)S(1)}, f32[8,4,8,128]{3,2,1,0:T(8,128)S(1)}, u32[]{:S(2)}, u32[]{:S(2)}) collective-permute-start(f32[8,4,8,128]{3,2,1,0:T(8,128)S(1)} %copy-done.10), channel_id=1, source_target_pairs={{0,11},{1,10},{2,9},{3,8},{4,15},{5,14},{6,13},{7,12},{8,3},{9,2},... | collective-permute-start | bytes 393224 | tf_op jit(solution)/shard_map/ppermute | solution.py:612
  482.1 30.8 %collective-permute-start.17 = (f32[8,4,8,128]{3,2,1,0:T(8,128)S(1)}, f32[8,4,8,128]{3,2,1,0:T(8,128)S(1)}, u32[]{:S(2)}, u32[]{:S(2)}) collective-permute-start(f32[8,4,8,128]{3,2,1,0:T(8,128)S(1)} %copy-done.9), channel_id=1, source_target_pairs={{0,12},{1,13},{2,14},{3,15},{4,8},{5,9},{6,10},{7,11},{8,4},{9,5},... | collective-permute-start | bytes 393224 | tf_op jit(solution)/shard_map/ppermute | solution.py:612
  501.7 15.2 %collective-permute-start.18 = (f32[8,4,8,128]{3,2,1,0:T(8,128)S(1)}, f32[8,4,8,128]{3,2,1,0:T(8,128)S(1)}, u32[]{:S(2)}, u32[]{:S(2)}) collective-permute-start(f32[8,4,8,128]{3,2,1,0:T(8,128)S(1)} %copy-done.8), channel_id=1, source_target_pairs={{0,13},{1,12},{2,15},{3,14},{4,9},{5,8},{6,11},{7,10},{8,5},{9,4},... | collective-permute-start | bytes 393224 | tf_op jit(solution)/shard_map/ppermute | solution.py:612
  504.5 16.6 %collective-permute-start.19 = (f32[8,4,8,128]{3,2,1,0:T(8,128)S(1)}, f32[8,4,8,128]{3,2,1,0:T(8,128)S(1)}, u32[]{:S(2)}, u32[]{:S(2)}) collective-permute-start(f32[8,4,8,128]{3,2,1,0:T(8,128)S(1)} %copy-done.7), channel_id=1, source_target_pairs={{0,14},{1,15},{2,12},{3,13},{4,10},{5,11},{6,8},{7,9},{8,6},{9,7},... | collective-permute-start | bytes 393224 | tf_op jit(solution)/shard_map/ppermute | solution.py:612
  507.9 15.3 %collective-permute-start.20 = (f32[8,4,8,128]{3,2,1,0:T(8,128)S(1)}, f32[8,4,8,128]{3,2,1,0:T(8,128)S(1)}, u32[]{:S(2)}, u32[]{:S(2)}) collective-permute-start(f32[8,4,8,128]{3,2,1,0:T(8,128)S(1)} %copy-done.6), channel_id=1, source_target_pairs={{0,15},{1,14},{2,13},{3,12},{4,11},{5,10},{6,9},{7,8},{8,7},{9,6},... | collective-permute-start | bytes 393224 | tf_op jit(solution)/shard_map/ppermute | solution.py:612
  (17 other events, 240.4 us)
